TPU v7x, 256 devices: a whole 4x4x8 slice. The times are simulated.
256 devices in a mesh: teacher: 8 (over x, z_hi), tensor: 16 (over y, z_lo), student: 2 (over core).
Axes of the slice: x: 4, y: 4, z: 8 (z_hi: 2, z_lo: 4; z = z_hi * 4 + z_lo), core: 2. Of those that a mesh axis runs over, the one named last changes fastest.
Arguments:
- teacher_hidden: bfloat16 [4096, 16384], P(('teacher', 'student'), 'tensor'), may hold values from -1800 to 1800
- norm_gain: bfloat16 [16384], P('tensor'), may hold values from 0.5 to 1.5
- projector: bfloat16 [16384, 4096], P('tensor'), may hold values from -0.0625 to 0.0625
- doc_lengths: int32 [16, 16], replicated, may hold values from 1 to 40, 256 in all within a row
- doc_student: int32 [16, 16], replicated, may hold values from 0 to 15, each once within a row
- student_resid: bfloat16 [10240, 4096], P(('teacher', 'student'), 'tensor'), may hold values from -6 to 6
- student_attn: bfloat16 [10240, 4096], P(('teacher', 'student'), 'tensor'), may hold values from -6 to 6
- out_weight: bfloat16 [4096, 4096], P(None, 'tensor'), may hold values from -0.125 to 0.125
Outputs:
- act_grad: bfloat16 [10240, 4096], P(('teacher', 'student'), 'tensor')
- weight_grad: bfloat16 [4096, 4096], P(None, 'tensor')
Inputs may be any that keep to these rules, and one draw needn't show every extreme that they name: `doc_lengths`: row g lists the lengths of the 16 documents of teacher sequence g in order; each row sums to 256. doc_student[g, c] is the student replica that trains on document c of sequence g; each row names every replica once.
All inputs are finite; a program needn't handle non-finite values.
Results may differ from a plain program's by a relative error of at most 0.005.
Values may be sent and summed in bfloat16 or wider, within the bound.
No kernel may reach another device: no remote copies, remote signals or barrier semaphores. Data moves between devices by JAX's collectives and lax.ppermute only.
A program may use at most 128 MiB of HBM per device.

v0:
```python
import jax
import jax.numpy as jnp
from jax import lax
from jax.sharding import PartitionSpec as P

DT = 16384


def body(
    teacher_hidden,
    norm_gain,
    projector,
    doc_lengths,
    doc_student,
    student_resid,
    student_attn,
    out_weight,
):
    groups = lax.axis_size(("teacher", "student"))
    slot_rows = student_attn.shape[0] // groups
    seq_rows = teacher_hidden.shape[0]
    own_index = lax.axis_index(("teacher", "student"))
    offsets = jnp.cumsum(doc_lengths, axis=1) - doc_lengths
    replicas = jnp.arange(groups, dtype=jnp.int32)
    position = jnp.arange(slot_rows, dtype=jnp.int32)
    matches = (doc_student[own_index][:, None] == replicas[None, :]).astype(jnp.int32)
    outgoing_length = jnp.sum(matches * doc_lengths[own_index][:, None], axis=0)
    outgoing_offset = jnp.sum(matches * offsets[own_index][:, None], axis=0)
    outgoing_live = (position[None, :] < outgoing_length[:, None]).reshape(-1, 1)
    outgoing_index = jnp.where(
        outgoing_live[:, 0].reshape(groups, slot_rows),
        outgoing_offset[:, None] + position[None, :],
        0,
    ).reshape(-1)
    arrivals = (doc_student == own_index).astype(jnp.int32)
    incoming_length = jnp.sum(arrivals * doc_lengths, axis=1)
    incoming_live = (position[None, :] < incoming_length[:, None]).reshape(-1, 1)
    picked = jnp.where(
        outgoing_live, teacher_hidden[outgoing_index], jnp.zeros((), teacher_hidden.dtype)
    )
    arrived = lax.all_to_all(
        picked.reshape(groups, slot_rows, teacher_hidden.shape[1]),
        ("teacher", "student"),
        split_axis=0,
        concat_axis=0,
        tiled=True,
    )
    wide = arrived.reshape(groups * slot_rows, arrived.shape[2]).astype(jnp.float32)
    power = lax.psum(jnp.sum(wide * wide, axis=1), "tensor")
    normed = (wide * lax.rsqrt(power[:, None] / DT + 1e-05) * norm_gain.astype(jnp.float32)).astype(
        jnp.bfloat16
    )
    partial_value = jnp.dot(normed, projector, preferred_element_type=jnp.float32)
    target = lax.psum_scatter(partial_value, "tensor", scatter_dimension=1, tiled=True)
    gathered = lax.all_gather(student_attn, "tensor", axis=1, tiled=True)
    student_out = student_resid.astype(jnp.float32) + jnp.dot(
        gathered, out_weight, preferred_element_type=jnp.float32
    )
    residual = jnp.where(incoming_live, student_out - target, 0.0).astype(jnp.bfloat16)
    partial_grad = lax.dot_general(
        residual, out_weight, (((1,), (1,)), ((), ())), preferred_element_type=jnp.float32
    )
    act_grad = lax.psum_scatter(partial_grad, "tensor", scatter_dimension=1, tiled=True).astype(
        jnp.bfloat16
    )
    local_weight = lax.dot_general(
        gathered, residual, (((0,), (0,)), ((), ())), preferred_element_type=jnp.float32
    )
    summed = lax.psum(local_weight, ("teacher", "student"))
    weight_grad = (summed / (groups * seq_rows)).astype(jnp.bfloat16)
    return (act_grad, weight_grad)


def solution(mesh):
    return jax.shard_map(
        body,
        mesh=mesh,
        in_specs=(
            P(("teacher", "student"), "tensor"),
            P("tensor"),
            P("tensor", None),
            P(),
            P(),
            P(("teacher", "student"), "tensor"),
            P(("teacher", "student"), "tensor"),
            P(None, "tensor"),
        ),
        out_specs=(P(("teacher", "student"), "tensor"), P(None, "tensor")),
        check_vma=False,
    )
```

profile of v0, /device:TPU:57, one launch (start us, length us, event | category | flops | bytes accessed | tf_op | source)
XLA Modules:
  0.0 877.0 jit_solution(16797783794070415856)
XLA Ops:
  7.2 0.0 copy-start
  7.2 0.0 all-gather.2.cloned.1.call-start
  7.2 0.7 all-gather.2.cloned.1.call-update
  7.9 0.9 reduce_window_sum.11
  8.8 0.7 fusion.8
  9.5 0.1 select_reduce_fusion.1
  9.6 0.1 add_select_fusion
  9.7 0.1 select_n.41
  9.8 5.0 gather_fusion
  14.8 0.1 iota_compare_fusion.1
  14.9 0.0 copy-start.4
  14.9 1.2 broadcast_select_fusion
  16.1 10.7 %all-to-all-start = ((bf16[16,40,1024]{2,1,0:T(8,128)(2,1)}), bf16[16,40,1024]{2,1,0:T(8,128)(2,1)S(1)}, u32[]{:S(2)}, u32[]{:S(2)}) async-start(bf16[16,40,1024]{2,1,0:T(8,128)(2,1)} %broadcast_select_fusion), calls=%async_computation | async-start | bytes 2621440 | tf_op jit(solution)/shard_map/all_to_all | solution.py:41
  26.8 0.0 reduce-scatter.3.cloned.1.call-start
  26.9 0.0 copy-done.4
  26.9 58.1 %all-to-all-done = bf16[16,40,1024]{2,1,0:T(8,128)(2,1)S(1)} async-done(((bf16[16,40,1024]{2,1,0:T(8,128)(2,1)}), bf16[16,40,1024]{2,1,0:T(8,128)(2,1)S(1)}, u32[]{:S(2)}, u32[]{:S(2)}) %all-to-all-start) | async-done | bytes 1310752 | tf_op jit(solution)/shard_map/all_to_all | solution.py:41
  85.0 0.3 multiply_reduce_fusion
  85.3 0.1 reduce_sum.42
  85.4 33.4 %psum.14 = f32[640]{0:T(1024)S(1)} all-reduce(f32[640]{0:T(1024)S(1)} %reduce_sum.42), channel_id=1, replica_groups=mesh['teacher'=8,'tensor'=16,'student'=2] {'tensor'}, use_global_device_ids=true, to_apply=%region_5.6 | all-reduce | flops 640 | bytes 5120 | tf_op jit(solution)/shard_map/psum | solution.py:49
  118.8 0.4 fusion.1
  119.2 11.5 %fusion.10 = f32[640,4096]{1,0:T(8,128)} fusion(bf16[640,1024]{1,0:T(8,128)(2,1)S(1)} %fusion.1, bf16[1024,4096]{1,0:T(8,128)(2,1)} %param.10), kind=kOutput, calls=%fused_computation.30 | convolution fusion | flops 5368709120 | bytes 20185088 | tf_op jit(solution)/shard_map/dot_general | solution.py:53
  130.7 0.0 copy-start.2
  130.7 0.0 copy-start.3
  130.7 0.0 copy-start.5
  130.7 0.0 reduce-scatter.3.cloned.1.call-update
  130.8 0.0 all-reduce.2.cloned.1.call-start
  130.8 0.6 copy-done.2
  131.4 0.0 copy-done.3
  131.4 0.1 select_reduce_fusion.2
  131.6 0.1 iota_compare_fusion.2
  131.6 0.1 lt.66
  131.7 35.1 %all-gather.2.cloned.1.call-done = bf16[640,4096]{1,0:T(8,128)(2,1)} async-done(((bf16[640,256]{1,0:T(8,128)(2,1)}), bf16[640,4096]{1,0:T(8,128)(2,1)}) %all-gather.2.cloned.1.call-update) | async-done | bytes 5242896 | tf_op jit(solution)/shard_map/all_gather | solution.py:55
  166.8 232.2 %reduce-scatter.3.cloned.1.call-done = f32[640,256]{1,0:T(8,128)} async-done(((f32[640,4096]{1,0:T(8,128)}), f32[640,256]{1,0:T(8,128)}) %reduce-scatter.3.cloned.1.call-update) | async-done | bytes 655376 | tf_op jit(solution)/shard_map/reduce_scatter | solution.py:54
  399.0 0.0 copy-done
  399.0 0.0 copy-done.5
  399.0 0.0 copy-start.1
  399.0 4.3 fusion.4
  403.3 0.0 copy-done.1
  403.3 3.9 convolution_bitcast_fusion
  407.2 0.0 all-reduce.2.cloned.1.call-update
  407.2 0.0 reduce-scatter.5.cloned.1.call-start
  407.3 5.5 fusion.11
  412.8 0.0 reduce-scatter.5.cloned.1.call-update
  412.8 226.2 %all-reduce.2.cloned.1.call-done = f32[4096,256]{0,1:T(8,128)} async-done(((f32[4096,256]{0,1:T(8,128)}), f32[4096,256]{0,1:T(8,128)}) %all-reduce.2.cloned.1.call-update) | async-done | bytes 4194320 | tf_op jit(solution)/shard_map/psum | solution.py:69
  639.0 3.9 multiply_convert_fusion
  642.9 4.1 copy.10
  646.9 221.7 %reduce-scatter.5.cloned.1.call-done = f32[640,256]{1,0:T(8,128)} async-done(((f32[640,4096]{1,0:T(8,128)}), f32[640,256]{1,0:T(8,128)}) %reduce-scatter.5.cloned.1.call-update) | async-done | bytes 655376 | tf_op jit(solution)/shard_map/reduce_scatter | solution.py:63
  868.6 1.8 convert_element_type.36
  (4 shorter events, 0.0 us)
Async XLA Ops:
  7.2 391.8 %copy-start = (bf16[4096,256]{1,0:T(8,128)(2,1)S(1)}, bf16[4096,256]{1,0:T(8,128)(2,1)}, u32[]{:S(2)}) copy-start(bf16[4096,256]{1,0:T(8,128)(2,1)} %param.15) | copy-start | bytes 6291460
  7.2 159.6 %all-gather.2.cloned.1.call-start = ((), (), s32[]{:S(2)}) async-start(), calls=%async_computation.3 | async-start | bytes 5570560 | tf_op jit(solution)/shard_map/all_gather | solution.py:55
  14.9 12.0 %copy-start.4 = (bf16[1024]{0:T(1024)(128)(2,1)S(1)}, bf16[1024]{0:T(1024)(128)(2,1)}, u32[]{:S(2)}) copy-start(bf16[1024]{0:T(1024)(128)(2,1)} %param.9) | copy-start | bytes 6148
  16.1 68.9 %all-to-all-start = ((bf16[16,40,1024]{2,1,0:T(8,128)(2,1)}), bf16[16,40,1024]{2,1,0:T(8,128)(2,1)S(1)}, u32[]{:S(2)}, u32[]{:S(2)}) async-start(bf16[16,40,1024]{2,1,0:T(8,128)(2,1)} %broadcast_select_fusion), calls=%async_computation | async-start | bytes 2621440 | tf_op jit(solution)/shard_map/all_to_all | solution.py:41
  26.8 372.2 %reduce-scatter.3.cloned.1.call-start = ((), (), s32[]{:S(2)}) async-start(), calls=%async_computation.4 | async-start | bytes 11141120 | tf_op jit(solution)/shard_map/reduce_scatter | solution.py:54
  130.7 0.7 copy-start.2
  130.7 0.7 copy-start.3
  130.7 268.3 %copy-start.5 = (bf16[640,256]{1,0:T(8,128)(2,1)S(1)}, bf16[640,256]{1,0:T(8,128)(2,1)}, u32[]{:S(2)}) copy-start(bf16[640,256]{1,0:T(8,128)(2,1)} %param.13) | copy-start | bytes 983044
  130.8 508.3 %all-reduce.2.cloned.1.call-start = ((), (), s32[]{:S(2)}) async-start(), calls=%async_computation.6 | async-start | bytes 8388608 | tf_op jit(solution)/shard_map/psum | solution.py:69
  399.0 4.3 copy-start.1
  407.2 461.4 %reduce-scatter.5.cloned.1.call-start = ((), (), s32[]{:S(2)}) async-start(), calls=%async_computation.5 | async-start | bytes 11141120 | tf_op jit(solution)/shard_map/reduce_scatter | solution.py:63
Sparse Core Ops, SparseCore 0:
  9.7 157.0 all-gather.1
  169.4 229.5 reduce-scatter.2
  407.3 231.6 all-reduce.1
  641.4 227.1 reduce-scatter.4
where the time goes:
time: 884 us; the launch traced here: 877 us
  waiting for transfers between devices  774 us (88%)
  blocking collectives  33.4 us (4%)
  matrix products  25.2 us (3%)
  between operations  13.9 us (2%)
  starting transfers between devices  10.9 us (1%)
  local copies, waits for them, and re-layouts  9.99 us (1%)
  other arithmetic  9.66 us (1%)
    reduce_scatter x1, waiting for transfers between devices, body(): lax.psum_scatter(partial_value, 'tensor', scatter_dimension=1, tiled=True)  232 us
    psum x1, waiting for transfers between devices, body(): summed = lax.psum(local_weight, ('teacher', 'student'))  226 us
    reduce_scatter x1, waiting for transfers between devices, body(): lax.psum_scatter(partial_grad, 'tensor', scatter_dimension=1, tiled=True)  222 us
    all_to_all x1, waiting for transfers between devices, body(): lax.all_to_all(picked.reshape(groups, slot_rows, teacher_hidden.shape[1])...  58.1 us
    all_gather x1, waiting for transfers between devices, body(): gathered = lax.all_gather(student_attn, 'tensor', axis=1, tiled=True)  35.1 us
    psum x1, blocking collectives, body(): power = lax.psum(jnp.sum(wide * wide, axis=1), 'tensor')  33.4 us
  transfers between devices with their start and end apart: 5, of which 5 were waited for; matrix products, arithmetic and copies ran while one was open for 4% of the time, Pallas kernels for 0%

commit v1 on v0

v1 whole, which is shorter than its diff:
```python
import jax
import jax.numpy as jnp
from jax import lax
from jax.experimental import pallas as pl
from jax.experimental.pallas import tpu as pltpu
from jax.sharding import Mesh
from jax.sharding import PartitionSpec as P

DT = 16384
EPS = 1e-05
GROUP = ("x", "zh", "core")
TENSOR = ("y", "zl")
BF = jnp.bfloat16
F32 = jnp.float32
VMEM_LIMIT = 40 * 1024 * 1024


def ring(n, k):
    return [(i, (i + k) % n) for i in range(n)]


SWAP = [(0, 1), (1, 0)]


def eye_mask(n):
    return lax.broadcasted_iota(jnp.int32, (n, n), 0) == lax.broadcasted_iota(jnp.int32, (n, n), 1)


def split_rows(row):
    high = row.astype(BF).astype(F32)
    rest = row - high
    middle = rest.astype(BF).astype(F32)
    low = rest - middle
    at = lax.broadcasted_iota(jnp.int32, (16, row.shape[1]), 0)
    return jnp.where(at == 0, high, jnp.where(at == 1, middle, jnp.where(at == 2, low, 0.0))).astype(BF)


def project_kernel(place, hidden, gain, projector, *rest):
    outs, scaled = rest[:4], rest[4]
    step = pl.program_id(0)
    rows = hidden.shape[0]

    @pl.when(step == 0)
    def _():
        wide = hidden[...].astype(F32)
        scaled[...] = (wide * gain[...].astype(F32)).astype(BF)
        power = jnp.sum(wide * wide, axis=1, keepdims=True)
        parts = split_rows(jnp.sum(jnp.where(eye_mask(rows), power, 0.0), axis=0, keepdims=True))
        for out in outs:
            out[rows:, :rows] = parts
            out[rows:, rows:] = jnp.zeros((16, out.shape[1] - rows), BF)

    for i, out in enumerate(outs):

        @pl.when(step == i)
        def _(out=out):
            out[:rows, :] = jnp.dot(scaled[...], projector[...], preferred_element_type=F32).astype(BF)


def project(y, hidden, gain, projector):
    rows, depth = hidden.shape
    width = projector.shape[1] // 4
    return pl.pallas_call(
        project_kernel,
        grid_spec=pltpu.PrefetchScalarGridSpec(
            num_scalar_prefetch=1,
            grid=(4,),
            in_specs=[
                pl.BlockSpec((rows, depth), lambda i, s: (0, 0)),
                pl.BlockSpec((1, depth), lambda i, s: (0, 0)),
                pl.BlockSpec((depth, width), lambda i, s: (0, (s[0] + i) % 4)),
            ],
            out_specs=[pl.BlockSpec((rows + 16, width), lambda i, s: (0, 0))] * 4,
            scratch_shapes=[pltpu.VMEM((rows, depth), BF)],
        ),
        out_shape=[jax.ShapeDtypeStruct((rows + 16, width), BF)] * 4,
        compiler_params=pltpu.CompilerParams(vmem_limit_bytes=VMEM_LIMIT),
        cost_estimate=pl.CostEstimate(
            flops=2 * rows * depth * 4 * width, bytes_accessed=2 * depth * 4 * width, transcendentals=0
        ),
        name="project",
    )(y.reshape(1), hidden, gain.reshape(1, depth), projector)


def fold_kernel(place, a, b, c, d, *outs):
    rows = a.shape[0] - 16
    width = outs[0].shape[1]
    total = sum(r[rows:, :rows].astype(F32) for r in (a, b, c, d))
    parts = split_rows(jnp.sum(total, axis=0, keepdims=True))
    for k, out in enumerate(outs):
        at = pl.ds(pl.multiple_of(((place[0] + k) % 4) * width, width), width)
        out[:rows, :] = sum(r[:rows, at].astype(F32) for r in (a, b, c, d)).astype(BF)
        out[rows:, :] = parts


def fold(zl, parts):
    rows, width = parts[0].shape[0], parts[0].shape[1] // 4
    vmem = pl.BlockSpec(memory_space=pltpu.VMEM)
    return pl.pallas_call(
        fold_kernel,
        in_specs=[pl.BlockSpec(memory_space=pltpu.SMEM)] + [vmem] * 4,
        out_specs=[vmem] * 4,
        out_shape=[jax.ShapeDtypeStruct((rows, width), BF)] * 4,
        compiler_params=pltpu.CompilerParams(vmem_limit_bytes=VMEM_LIMIT),
        name="fold",
    )(zl.reshape(1), *parts)


def middle_kernel(place, attn, weight, resid, a, b, c, d, g0, g1, g2, g3, keep, send):
    rows = resid.shape[0]
    y, core = place[0], place[1]
    total = sum(r[:rows, :].astype(F32) for r in (a, b, c, d))
    power = jnp.sum(sum(r[rows:, :].astype(F32) for r in (a, b, c, d)), axis=0, keepdims=True)
    power = jnp.sum(jnp.where(eye_mask(rows), power, 0.0), axis=1, keepdims=True)
    value = resid[...].astype(F32) - total * lax.rsqrt(power / DT + EPS)
    for t in range(16):
        value += jnp.dot(attn[t], weight[t], preferred_element_type=F32)
    residual = value.astype(BF)
    for k, out in enumerate((g0, g1, g2, g3)):
        for z in range(4):
            w = weight[((y + k) % 4) * 4 + z]
            out[z] = lax.dot_general(
                residual, w, (((1,), (1,)), ((), ())), preferred_element_type=F32
            ).astype(BF)
    for out, half in ((keep, core), (send, 1 - core)):
        for i in range(8):
            out[i] = lax.dot_general(
                attn[half * 8 + i], residual, (((0,), (0,)), ((), ())), preferred_element_type=F32
            ).astype(out.dtype)


def middle(place, attn, weight, resid, parts):
    rows = resid.shape[0]
    vmem = pl.BlockSpec(memory_space=pltpu.VMEM)
    return pl.pallas_call(
        middle_kernel,
        in_specs=[pl.BlockSpec(memory_space=pltpu.SMEM)] + [vmem] * 7,
        out_specs=[vmem] * 6,
        out_shape=[jax.ShapeDtypeStruct((4, rows, 256), BF)] * 4
        + [jax.ShapeDtypeStruct((8, 256, 256), F32)] * 2,
        compiler_params=pltpu.CompilerParams(vmem_limit_bytes=VMEM_LIMIT),
        name="middle",
    )(place, attn, weight, resid, *parts)


def exchange(pieces, axis):
    return [pieces[0]] + [lax.ppermute(pieces[k], axis, ring(4, k)) for k in (1, 2, 3)]


def add_up(pieces):
    return sum(p.astype(F32) for p in pieces)


def body(hidden, gain, projector, doc_lengths, doc_student, resid, attn, weight):
    groups, slot = 16, resid.shape[0] // 16
    rows = hidden.shape[0]
    me = lax.axis_index(GROUP)
    x, y, zl, core = (lax.axis_index(a) for a in ("x", "y", "zl", "core"))

    offsets = jnp.cumsum(doc_lengths, axis=1) - doc_lengths
    matches = (doc_student[me][:, None] == jnp.arange(groups, dtype=jnp.int32)[None, :]).astype(jnp.int32)
    length = jnp.sum(matches * doc_lengths[me][:, None], axis=0)
    offset = jnp.sum(matches * offsets[me][:, None], axis=0)
    position = jnp.arange(slot, dtype=jnp.int32)
    where = jnp.where(position[None, :] < length[:, None], offset[:, None] + position[None, :], -1).reshape(-1)
    select = (jnp.arange(rows, dtype=jnp.int32)[:, None] == where[None, :]).astype(BF)

    def to_sequence(slots):
        got = lax.all_to_all(slots.reshape(groups, slot, -1), GROUP, 0, 0, tiled=True)
        return jnp.dot(select, got.reshape(groups * slot, -1), preferred_element_type=F32).astype(BF)

    attn_rows = to_sequence(attn)
    resid_rows = to_sequence(resid)

    parts = exchange(project(y, hidden, gain, projector), "y")
    parts = exchange(fold(zl, parts), "zl")

    gathered = lax.all_gather(attn_rows, "zl", axis=0, tiled=True)
    gathered = lax.all_gather(gathered, "y", axis=0, tiled=True)

    g0, g1, g2, g3, keep, send = middle(
        jnp.stack([y, core]),
        gathered.reshape(16, rows, 256),
        weight.reshape(16, 256, 256),
        resid_rows,
        parts,
    )

    grads = exchange([g0, g1, g2, g3], "y")
    grads = [
        add_up([lax.dynamic_index_in_dim(g, (zl + k) % 4, 0, keepdims=False) for g in grads]).astype(BF)
        for k in range(4)
    ]
    grad = add_up(exchange(grads, "zl")).astype(BF)
    slots = lax.dot_general(select, grad, (((0,), (0,)), ((), ())), preferred_element_type=F32).astype(BF)
    act_grad = lax.all_to_all(slots.reshape(groups, slot, -1), GROUP, 0, 0, tiled=True).reshape(resid.shape)

    other = lax.ppermute(send, "core", SWAP)
    pieces = [
        (
            lax.dynamic_slice_in_dim(keep, ((x + k) % 4) * 2, 2, 0)
            + lax.dynamic_slice_in_dim(other, ((x + k) % 4) * 2, 2, 0)
        ).astype(BF)
        for k in range(4)
    ]
    own = lax.reduce_precision(add_up(exchange(pieces, "x")), 8, 7)
    far = lax.ppermute(own.astype(BF), "zh", SWAP)
    done = ((own + far.astype(F32)) / (groups * rows)).astype(BF)
    half = lax.all_gather(done.reshape(512, 256), "x", axis=0, tiled=True)
    twin = lax.ppermute(half, "core", SWAP)
    first = jnp.where(core == 0, half, twin)
    second = jnp.where(core == 0, twin, half)
    weight_grad = jnp.concatenate([first, second], axis=0)
    return act_grad, weight_grad


def solution(mesh):
    fine = Mesh(mesh.devices.reshape(4, 2, 4, 4, 2), ("x", "zh", "y", "zl", "core"))
    return jax.shard_map(
        body,
        mesh=fine,
        in_specs=(
            P(GROUP, TENSOR),
            P(TENSOR),
            P(TENSOR, None),
            P(),
            P(),
            P(GROUP, TENSOR),
            P(GROUP, TENSOR),
            P(None, TENSOR),
        ),
        out_specs=(P(GROUP, TENSOR), P(None, TENSOR)),
        check_vma=False,
    )
```

time: 884 us -> 252 us (0.29)
  waiting for transfers between devices: 774 us -> 137 us
  starting transfers between devices: 10.9 us -> 52.8 us
  blocking collectives: 33.4 us -> 11.4 us
  matrix products: 25.2 us -> 3.64 us
  Pallas kernels: 0 us -> 11.7 us
    reduce_scatter x2 -> x0, waiting for transfers between devices: 454 us -> none  [the longest x1 232 us: body(): lax.psum_scatter(partial_value, 'tensor', scatter_dimension=1, tiled=True)]
    psum x1 -> x0, waiting for transfers between devices: 226 us -> none  [body(): summed = lax.psum(local_weight, ('teacher', 'student'))]
    ppermute x0 -> x18, waiting for transfers between devices: none -> 84.2 us  [the longest x15 68.4 us: exchange(): lax.ppermute(pieces[k], axis, ring(4, k))]
    psum x1 -> x0, blocking collectives: 33.4 us -> none  [body(): power = lax.psum(jnp.sum(wide * wide, axis=1), 'tensor')]
    all_to_all x1 -> x3, waiting for transfers between devices: 58.1 us -> 28.2 us  [the longest x1 15 us: body(): lax.all_to_all(slots.reshape(groups, slot, -1), GROUP, 0, 0, tiled=True)]
    ppermute x0 -> x18, starting transfers between devices: none -> 25.1 us  [the longest x15 18 us: exchange(): lax.ppermute(pieces[k], axis, ring(4, k))]
    dot_general x4 -> x3, matrix products: 25.2 us -> 3.64 us  [the longest x1 2.12 us: body(): lax.dot_general(select, grad, (((0,), (0,)), ((), ())), preferred_element...]
    all_to_all x1 -> x3, starting transfers between devices: 10.7 us -> 27.6 us  [the longest x2 18.8 us: to_sequence(): lax.all_to_all(slots.reshape(groups, slot, -1), GROUP, 0, 0, tiled=True)]
  transfers between devices with their start and end apart: 5 -> 23, of which waited for: 5 -> 14; matrix products, arithmetic and copies ran while one was open for 4% -> 3% of each run, Pallas kernels for 0% -> 3%
where the time goes in v1:
time: 252 us; the launch traced here: 251 us
  waiting for transfers between devices  137 us (54%)
  starting transfers between devices  52.8 us (21%)
  between operations  14.2 us (6%)
  Pallas kernels  11.7 us (5%)
  blocking collectives  11.4 us (5%)
  other arithmetic  10.3 us (4%)
  local copies, waits for them, and re-layouts  9.58 us (4%)
  matrix products  3.64 us (1%)
    ppermute x15, waiting for transfers between devices, exchange(): lax.ppermute(pieces[k], axis, ring(4, k))  68.4 us
    all_gather x1, waiting for transfers between devices, body(): half = lax.all_gather(done.reshape(512, 256), 'x', axis=0, tiled=True)  24.9 us
    all_to_all x2, starting transfers between devices, to_sequence(): lax.all_to_all(slots.reshape(groups, slot, -1), GROUP, 0, 0, tiled=True)  18.8 us
    ppermute x15, starting transfers between devices, exchange(): lax.ppermute(pieces[k], axis, ring(4, k))  18 us
    all_to_all x1, waiting for transfers between devices, body(): lax.all_to_all(slots.reshape(groups, slot, -1), GROUP, 0, 0, tiled=True)  15 us
    all_to_all x2, waiting for transfers between devices, to_sequence(): lax.all_to_all(slots.reshape(groups, slot, -1), GROUP, 0, 0, tiled=True)  13.2 us
    ppermute x1, waiting for transfers between devices, body(): far = lax.ppermute(own.astype(BF), 'zh', SWAP)  11.6 us
    all_gather x1, blocking collectives, body(): gathered = lax.all_gather(attn_rows, 'zl', axis=0, tiled=True)  11.4 us
  transfers between devices with their start and end apart: 23, of which 14 were waited for; matrix products, arithmetic and copies ran while one was open for 3% of the time, Pallas kernels for 3%

profile of v1, /device:TPU:57, one launch (start us, length us, event | category | flops | bytes accessed | tf_op | source)
XLA Modules:
  0.0 251.0 jit_solution(15178272047975602403)
XLA Ops:
  7.2 10.9 %all-to-all-start = ((bf16[16,40,256]{2,1,0:T(8,128)(2,1)}), bf16[16,40,256]{2,1,0:T(8,128)(2,1)S(1)}, u32[]{:S(2)}, u32[]{:S(2)}) async-start(bf16[16,40,256]{2,1,0:T(8,128)(2,1)} %bitcast.36), calls=%async_computation | async-start | bytes 655360 | tf_op jit(solution)/shard_map/all_to_all | solution.py:169
  18.1 0.9 reduce_window_sum.11
  19.9 13.2 %all-to-all-done = bf16[16,40,256]{2,1,0:T(8,128)(2,1)S(1)} async-done(((bf16[16,40,256]{2,1,0:T(8,128)(2,1)}), bf16[16,40,256]{2,1,0:T(8,128)(2,1)S(1)}, u32[]{:S(2)}, u32[]{:S(2)}) %all-to-all-start) | async-done | bytes 327712 | tf_op jit(solution)/shard_map/all_to_all | solution.py:169
  33.4 11.4 %all_gather.9 = bf16[1024,256]{1,0:T(8,128)(2,1)} all-gather(bf16[256,256]{1,0:T(8,128)(2,1)S(1)} %convolution_convert_fusion.2), channel_id=1, replica_groups=mesh['x'=4,'zh'=2,'y'=4,'zl'=4,'core'=2] {'zl'}, dimensions={0}, use_global_device_ids=true | all-gather | bytes 655360 | tf_op jit(solution)/shard_map/all_gather | solution.py:178
  44.8 8.0 %all-to-all-start.1 = ((bf16[16,40,256]{2,1,0:T(8,128)(2,1)}), bf16[16,40,256]{2,1,0:T(8,128)(2,1)}, u32[]{:S(2)}, u32[]{:S(2)}) async-start(bf16[16,40,256]{2,1,0:T(8,128)(2,1)} %bitcast.9), calls=%async_computation.1 | async-start | bytes 655360 | tf_op jit(solution)/shard_map/all_to_all | solution.py:169
  52.9 3.4 %copy-done = bf16[1024,4096]{1,0:T(8,128)(2,1)S(1)} copy-done((bf16[1024,4096]{1,0:T(8,128)(2,1)S(1)}, bf16[1024,4096]{1,0:T(8,128)(2,1)}, u32[]{:S(2)}) %copy-start) | copy-done | bytes 8388632
  56.3 4.7 %project.1 = (bf16[272,1024]{1,0:T(8,128)(2,1)S(1)}, bf16[272,1024]{1,0:T(8,128)(2,1)}, bf16[272,1024]{1,0:T(8,128)(2,1)}, bf16[272,1024]{1,0:T(8,128)(2,1)}) custom-call(s32[1]{0:T(128)} %bitcast.3.place, bf16[256,1024]{1,0:T(8,128)(2,1)S(1)} %copy-done.4, bf16[1,1024]{1,0:T(2,128)(2,1)S(1)} %reshape.113.gain, bf16[1024,4096]{1,0:T(8,128)(2,1)S(1)} %copy-done), custom_call_target="tpu_custom_call" | custom-call | flops 2147483648 | bytes 8388608 | tf_op jit(solution)/shard_map/project/pallas_call | solution.py:63
  61.0 2.2 collective-permute-start.1
  63.3 24.3 %collective-permute-done.b = bf16[272,1024]{1,0:T(8,128)(2,1)S(1)} collective-permute-done((bf16[272,1024]{1,0:T(8,128)(2,1)}, bf16[272,1024]{1,0:T(8,128)(2,1)S(1)}, u32[]{:S(2)}, u32[]{:S(2)}) %collective-permute-start) | collective-permute-done | bytes 557088 | tf_op jit(solution)/shard_map/ppermute | solution.py:147
  87.6 12.9 %collective-permute-done.2.d = bf16[272,1024]{1,0:T(8,128)(2,1)} collective-permute-done((bf16[272,1024]{1,0:T(8,128)(2,1)}, bf16[272,1024]{1,0:T(8,128)(2,1)}, u32[]{:S(2)}, u32[]{:S(2)}) %collective-permute-start.2) | collective-permute-done | bytes 557088 | tf_op jit(solution)/shard_map/ppermute | solution.py:147
  100.5 2.1 fold.1
  102.7 1.3 collective-permute-start.3
  104.0 1.0 collective-permute-start.4
  105.0 1.5 collective-permute-start.5
  106.4 1.3 convolution_convert_fusion.1.resid
  107.7 8.0 %collective-permute-done.4.c = bf16[272,256]{1,0:T(8,128)(2,1)S(1)} collective-permute-done((bf16[272,256]{1,0:T(8,128)(2,1)}, bf16[272,256]{1,0:T(8,128)(2,1)S(1)}, u32[]{:S(2)}, u32[]{:S(2)}) %collective-permute-start.4) | collective-permute-done | bytes 139296 | tf_op jit(solution)/shard_map/ppermute | solution.py:147
  115.6 2.6 %collective-permute-done.5.d = bf16[272,256]{1,0:T(8,128)(2,1)S(1)} collective-permute-done((bf16[272,256]{1,0:T(8,128)(2,1)S(1)}, bf16[272,256]{1,0:T(8,128)(2,1)S(1)}, u32[]{:S(2)}, u32[]{:S(2)}) %collective-permute-start.5) | collective-permute-done | bytes 139296 | tf_op jit(solution)/shard_map/ppermute | solution.py:147
  118.2 1.6 copy-done.2
  119.8 4.8 %middle.1 = (bf16[4,256,256]{2,1,0:T(8,128)(2,1)S(1)}, bf16[4,256,256]{2,1,0:T(8,128)(2,1)S(1)}, bf16[4,256,256]{2,1,0:T(8,128)(2,1)S(1)}, bf16[4,256,256]{2,1,0...) custom-call(s32[2]{0:T(128)S(1)} %pad_add_fusion.place, bf16[16,256,256]{2,1,0:T(8,128)(2,1)S(1)} %bitcast.33, ...), custom_call_target="tpu_custom_call" | custom-call | tf_op jit(solution)/shard_map/middle/pallas_call | solution.py:135
  124.6 1.4 copy-done.3
  126.0 0.8 copy-done.5
  126.8 0.8 copy-done.7
  127.6 0.8 copy-done.9
  128.9 4.1 %collective-permute-done.12 = f32[8,256,256]{2,1,0:T(8,128)} collective-permute-done((f32[8,256,256]{2,1,0:T(8,128)}, f32[8,256,256]{2,1,0:T(8,128)}, u32[]{:S(2)}, u32[]{:S(2)}) %collective-permute-start.12) | collective-permute-done | bytes 2097184 | tf_op jit(solution)/shard_map/ppermute | solution.py:198
  133.0 2.0 add_convert_fusion.2
  135.0 1.4 collective-permute-start.13
  136.5 2.4 collective-permute-start.14
  138.9 1.2 collective-permute-start.15
  140.1 4.0 %collective-permute-done.13 = bf16[2,256,256]{2,1,0:T(8,128)(2,1)S(1)} collective-permute-done((bf16[2,256,256]{2,1,0:T(8,128)(2,1)S(1)}, bf16[2,256,256]{2,1,0:T(8,128)(2,1)S(1)}, u32[]{:S(2)}, u32[]{:S(2)}) %collective-permute-start.13) | collective-permute-done | bytes 262176 | tf_op jit(solution)/shard_map/ppermute | solution.py:147
  144.0 6.5 %collective-permute-done.14 = bf16[2,256,256]{2,1,0:T(8,128)(2,1)S(1)} collective-permute-done((bf16[2,256,256]{2,1,0:T(8,128)(2,1)S(1)}, bf16[2,256,256]{2,1,0:T(8,128)(2,1)S(1)}, u32[]{:S(2)}, u32[]{:S(2)}) %collective-permute-start.14) | collective-permute-done | bytes 262176 | tf_op jit(solution)/shard_map/ppermute | solution.py:147
  150.6 1.4 fusion.20
  152.0 5.1 %collective-permute-start.16 = (bf16[2,256,256]{2,1,0:T(8,128)(2,1)S(1)}, bf16[2,256,256]{2,1,0:T(8,128)(2,1)S(1)}, u32[]{:S(2)}, u32[]{:S(2)}) collective-permute-start(bf16[2,256,256]{2,1,0:T(8,128)(2,1)S(1)} %get-tuple-element.32), channel_id=1, source_target_pairs={{0,32},{32,0},{1,33},{33,1},{2,34},{34,2},{3,35},{35,3},{4,36},{36... | collective-permute-start | bytes 786440 | tf_op jit(solution)/shard_map/ppermute | solution.py:207
  157.1 11.6 %collective-permute-done.16 = bf16[2,256,256]{2,1,0:T(8,128)(2,1)S(1)} collective-permute-done((bf16[2,256,256]{2,1,0:T(8,128)(2,1)S(1)}, bf16[2,256,256]{2,1,0:T(8,128)(2,1)S(1)}, u32[]{:S(2)}, u32[]{:S(2)}) %collective-permute-start.16) | collective-permute-done | bytes 262176 | tf_op jit(solution)/shard_map/ppermute | solution.py:207
  168.7 0.8 multiply_convert_fusion
  169.5 2.5 collective-permute-start.6
  172.6 24.9 %all-gather.5.cloned.1.call-done = bf16[2048,256]{1,0:T(8,128)(2,1)} async-done(((bf16[512,256]{1,0:T(8,128)(2,1)}), bf16[2048,256]{1,0:T(8,128)(2,1)}) %all-gather.5.cloned.1.call-update) | async-done | bytes 1048592 | tf_op jit(solution)/shard_map/all_gather | solution.py:209
  197.6 1.6 collective-permute-start.17
  199.2 1.5 fusion.7
  200.7 2.4 collective-permute-start.10
  203.2 1.3 collective-permute-start.9
  204.5 7.4 %collective-permute-done.10 = bf16[256,256]{1,0:T(8,128)(2,1)S(1)} collective-permute-done((bf16[256,256]{1,0:T(8,128)(2,1)S(1)}, bf16[256,256]{1,0:T(8,128)(2,1)S(1)}, u32[]{:S(2)}, u32[]{:S(2)}) %collective-permute-start.10) | collective-permute-done | bytes 131104 | tf_op jit(solution)/shard_map/ppermute | solution.py:147
  211.9 2.4 collective-permute-done.11
  214.7 2.1 convolution_convert_fusion
  216.8 8.8 %all-to-all-start.2 = ((bf16[16,40,256]{2,1,0:T(8,128)(2,1)}), bf16[16,40,256]{2,1,0:T(8,128)(2,1)S(1)}, u32[]{:S(2)}, u32[]{:S(2)}) async-start(bf16[16,40,256]{2,1,0:T(8,128)(2,1)} %bitcast.16), calls=%async_computation.2 | async-start | bytes 655360 | tf_op jit(solution)/shard_map/all_to_all | solution.py:196
  225.6 15.0 %all-to-all-done.2 = bf16[16,40,256]{2,1,0:T(8,128)(2,1)S(1)} async-done(((bf16[16,40,256]{2,1,0:T(8,128)(2,1)}), bf16[16,40,256]{2,1,0:T(8,128)(2,1)S(1)}, u32[]{:S(2)}, u32[]{:S(2)}) %all-to-all-start.2) | async-done | bytes 327712 | tf_op jit(solution)/shard_map/all_to_all | solution.py:196
  240.6 1.4 broadcast_select_fusion.1
  242.0 1.5 pad_maximum_fusion
  243.4 0.7 copy.11
  (47 shorter events, 3.3 us)
Async XLA Ops:
  7.2 45.7 %copy-start.12 = (bf16[1024]{0:T(1024)(128)(2,1)S(1)}, bf16[1024]{0:T(1024)(128)(2,1)}, u32[]{:S(2)}) copy-start(bf16[1024]{0:T(1024)(128)(2,1)} %param.9) | copy-start | bytes 6148
  7.2 45.7 %copy-start.4 = (bf16[256,1024]{1,0:T(8,128)(2,1)S(1)}, bf16[256,1024]{1,0:T(8,128)(2,1)}, u32[]{:S(2)}) copy-start(bf16[256,1024]{1,0:T(8,128)(2,1)} %hidden.1) | copy-start | bytes 1572868
  7.2 26.0 %all-to-all-start = ((bf16[16,40,256]{2,1,0:T(8,128)(2,1)}), bf16[16,40,256]{2,1,0:T(8,128)(2,1)S(1)}, u32[]{:S(2)}, u32[]{:S(2)}) async-start(bf16[16,40,256]{2,1,0:T(8,128)(2,1)} %bitcast.36), calls=%async_computation | async-start | bytes 655360 | tf_op jit(solution)/shard_map/all_to_all | solution.py:169
  18.0 100.2 %all-gather.3.cloned.1.call-start = ((), (), s32[]{:S(2)}) async-start(), calls=%async_computation.3 | async-start | bytes 2621440 | tf_op jit(solution)/shard_map/all_gather | solution.py:179
  44.8 61.6 %all-to-all-start.1 = ((bf16[16,40,256]{2,1,0:T(8,128)(2,1)}), bf16[16,40,256]{2,1,0:T(8,128)(2,1)}, u32[]{:S(2)}, u32[]{:S(2)}) async-start(bf16[16,40,256]{2,1,0:T(8,128)(2,1)} %bitcast.9), calls=%async_computation.1 | async-start | bytes 655360 | tf_op jit(solution)/shard_map/all_to_all | solution.py:169
  52.8 144.8 %all-gather.5.cloned.1.call-start = ((), (), s32[]{:S(2)}) async-start(), calls=%async_computation.4 | async-start | bytes 1310720 | tf_op jit(solution)/shard_map/all_gather | solution.py:209
  52.9 3.4 %copy-start = (bf16[1024,4096]{1,0:T(8,128)(2,1)S(1)}, bf16[1024,4096]{1,0:T(8,128)(2,1)}, u32[]{:S(2)}) copy-start(bf16[1024,4096]{1,0:T(8,128)(2,1)} %projector.1) | copy-start | bytes 25165828
  61.0 57.2 %copy-start.1 = (bf16[4096,256]{1,0:T(8,128)(2,1)S(1)}, bf16[4096,256]{1,0:T(8,128)(2,1)}, u32[]{:S(2)}) copy-start(bf16[4096,256]{1,0:T(8,128)(2,1)} %param.15) | copy-start | bytes 6291460
  61.0 26.6 %collective-permute-start = (bf16[272,1024]{1,0:T(8,128)(2,1)}, bf16[272,1024]{1,0:T(8,128)(2,1)S(1)}, u32[]{:S(2)}, u32[]{:S(2)}) collective-permute-start(bf16[272,1024]{1,0:T(8,128)(2,1)} %get-tuple-element.17), channel_id=1, source_target_pairs={{0,8},{8,16},{16,24},{24,0},{1,9},{9,17},{17,25},{25,1},{2,10},{10... | collective-permute-start | bytes 1671176 | tf_op jit(solution)/shard_map/ppermute | solution.py:147
  61.0 26.6 %collective-permute-start.1 = (bf16[272,1024]{1,0:T(8,128)(2,1)}, bf16[272,1024]{1,0:T(8,128)(2,1)}, u32[]{:S(2)}, u32[]{:S(2)}) collective-permute-start(bf16[272,1024]{1,0:T(8,128)(2,1)} %get-tuple-element.18), channel_id=1, source_target_pairs={{0,16},{8,24},{16,0},{24,8},{1,17},{9,25},{17,1},{25,9},{2,18},{10... | collective-permute-start | bytes 1671176 | tf_op jit(solution)/shard_map/ppermute | solution.py:147
  63.3 37.3 %collective-permute-start.2 = (bf16[272,1024]{1,0:T(8,128)(2,1)}, bf16[272,1024]{1,0:T(8,128)(2,1)}, u32[]{:S(2)}, u32[]{:S(2)}) collective-permute-start(bf16[272,1024]{1,0:T(8,128)(2,1)} %get-tuple-element.19), channel_id=1, source_target_pairs={{0,24},{8,0},{16,8},{24,16},{1,25},{9,1},{17,9},{25,17},{2,26},{10... | collective-permute-start | bytes 1671176 | tf_op jit(solution)/shard_map/ppermute | solution.py:147
  102.7 5.0 %collective-permute-start.3 = (bf16[272,256]{1,0:T(8,128)(2,1)}, bf16[272,256]{1,0:T(8,128)(2,1)S(1)}, u32[]{:S(2)}, u32[]{:S(2)}) collective-permute-start(bf16[272,256]{1,0:T(8,128)(2,1)} %get-tuple-element.21), channel_id=1, source_target_pairs={{0,2},{2,4},{4,6},{6,0},{1,3},{3,5},{5,7},{7,1},{8,10},{10,12},{12... | collective-permute-start | bytes 417800 | tf_op jit(solution)/shard_map/ppermute | solution.py:147
  104.0 11.7 %collective-permute-start.4 = (bf16[272,256]{1,0:T(8,128)(2,1)}, bf16[272,256]{1,0:T(8,128)(2,1)S(1)}, u32[]{:S(2)}, u32[]{:S(2)}) collective-permute-start(bf16[272,256]{1,0:T(8,128)(2,1)} %get-tuple-element.22), channel_id=1, source_target_pairs={{0,4},{2,6},{4,0},{6,2},{1,5},{3,7},{5,1},{7,3},{8,12},{10,14},{12... | collective-permute-start | bytes 417800 | tf_op jit(solution)/shard_map/ppermute | solution.py:147
  105.0 13.3 %collective-permute-start.5 = (bf16[272,256]{1,0:T(8,128)(2,1)S(1)}, bf16[272,256]{1,0:T(8,128)(2,1)S(1)}, u32[]{:S(2)}, u32[]{:S(2)}) collective-permute-start(bf16[272,256]{1,0:T(8,128)(2,1)S(1)} %get-tuple-element.23), channel_id=1, source_target_pairs={{0,6},{2,0},{4,2},{6,4},{1,7},{3,1},{5,3},{7,5},{8,14},{10,8},{12,... | collective-permute-start | bytes 417800 | tf_op jit(solution)/shard_map/ppermute | solution.py:147
  118.2 1.6 copy-start.2
  124.6 1.4 copy-start.3
  126.0 0.8 copy-start.5
  126.8 0.8 copy-start.7
  127.6 0.8 copy-start.9
  128.4 4.6 %collective-permute-start.12 = (f32[8,256,256]{2,1,0:T(8,128)}, f32[8,256,256]{2,1,0:T(8,128)}, u32[]{:S(2)}, u32[]{:S(2)}) collective-permute-start(f32[8,256,256]{2,1,0:T(8,128)} %get-tuple-element.29), channel_id=1, source_target_pairs={{0,1},{1,0},{2,3},{3,2},{4,5},{5,4},{6,7},{7,6},{8,9},{9,8},{10,11... | collective-permute-start | bytes 6291464 | tf_op jit(solution)/shard_map/ppermute | solution.py:198
  135.0 34.5 %copy-start.10 = (bf16[4,256,256]{2,1,0:T(8,128)(2,1)S(1)}, bf16[4,256,256]{2,1,0:T(8,128)(2,1)}, u32[]{:S(2)}) copy-start(bf16[4,256,256]{2,1,0:T(8,128)(2,1)} %copy-done.9) | copy-start | bytes 1572868
  135.0 36.9 %copy-start.8 = (bf16[4,256,256]{2,1,0:T(8,128)(2,1)S(1)}, bf16[4,256,256]{2,1,0:T(8,128)(2,1)}, u32[]{:S(2)}) copy-start(bf16[4,256,256]{2,1,0:T(8,128)(2,1)} %copy-done.7) | copy-start | bytes 1572868
  135.0 37.4 %copy-start.6 = (bf16[4,256,256]{2,1,0:T(8,128)(2,1)S(1)}, bf16[4,256,256]{2,1,0:T(8,128)(2,1)}, u32[]{:S(2)}) copy-start(bf16[4,256,256]{2,1,0:T(8,128)(2,1)} %copy-done.5) | copy-start | bytes 1572868
  135.0 9.0 %collective-permute-start.13 = (bf16[2,256,256]{2,1,0:T(8,128)(2,1)S(1)}, bf16[2,256,256]{2,1,0:T(8,128)(2,1)S(1)}, u32[]{:S(2)}, u32[]{:S(2)}) collective-permute-start(bf16[2,256,256]{2,1,0:T(8,128)(2,1)S(1)} %get-tuple-element.34), channel_id=1, source_target_pairs={{0,64},{64,128},{128,192},{192,0},{1,65},{65,129},{129,193},{193,1... | collective-permute-start | bytes 786440 | tf_op jit(solution)/shard_map/ppermute | solution.py:147
  136.5 14.1 %collective-permute-start.14 = (bf16[2,256,256]{2,1,0:T(8,128)(2,1)S(1)}, bf16[2,256,256]{2,1,0:T(8,128)(2,1)S(1)}, u32[]{:S(2)}, u32[]{:S(2)}) collective-permute-start(bf16[2,256,256]{2,1,0:T(8,128)(2,1)S(1)} %get-tuple-element.36), channel_id=1, source_target_pairs={{0,128},{64,192},{128,0},{192,64},{1,129},{65,193},{129,1},{193,65... | collective-permute-start | bytes 786440 | tf_op jit(solution)/shard_map/ppermute | solution.py:147
  138.9 11.7 %collective-permute-start.15 = (bf16[2,256,256]{2,1,0:T(8,128)(2,1)S(1)}, bf16[2,256,256]{2,1,0:T(8,128)(2,1)}, u32[]{:S(2)}, u32[]{:S(2)}) collective-permute-start(bf16[2,256,256]{2,1,0:T(8,128)(2,1)S(1)} %get-tuple-element.35), channel_id=1, source_target_pairs={{0,192},{64,0},{128,64},{192,128},{1,193},{65,1},{129,65},{193,129... | collective-permute-start | bytes 786440 | tf_op jit(solution)/shard_map/ppermute | solution.py:147
  152.0 16.7 %collective-permute-start.16 = (bf16[2,256,256]{2,1,0:T(8,128)(2,1)S(1)}, bf16[2,256,256]{2,1,0:T(8,128)(2,1)S(1)}, u32[]{:S(2)}, u32[]{:S(2)}) collective-permute-start(bf16[2,256,256]{2,1,0:T(8,128)(2,1)S(1)} %get-tuple-element.32), channel_id=1, source_target_pairs={{0,32},{32,0},{1,33},{33,1},{2,34},{34,2},{3,35},{35,3},{4,36},{36... | collective-permute-start | bytes 786440 | tf_op jit(solution)/shard_map/ppermute | solution.py:207
  169.5 29.7 %collective-permute-start.6 = (bf16[4,256,256]{2,1,0:T(8,128)(2,1)S(1)}, bf16[4,256,256]{2,1,0:T(8,128)(2,1)S(1)}, u32[]{:S(2)}, u32[]{:S(2)}) collective-permute-start(bf16[4,256,256]{2,1,0:T(8,128)(2,1)S(1)} %copy-done.10), channel_id=1, source_target_pairs={{0,8},{8,16},{16,24},{24,0},{1,9},{9,17},{17,25},{25,1},{2,10},{10... | collective-permute-start | bytes 1572872 | tf_op jit(solution)/shard_map/ppermute | solution.py:147
  171.9 27.2 %collective-permute-start.7 = (bf16[4,256,256]{2,1,0:T(8,128)(2,1)S(1)}, bf16[4,256,256]{2,1,0:T(8,128)(2,1)}, u32[]{:S(2)}, u32[]{:S(2)}) collective-permute-start(bf16[4,256,256]{2,1,0:T(8,128)(2,1)S(1)} %copy-done.8), channel_id=1, source_target_pairs={{0,16},{8,24},{16,0},{24,8},{1,17},{9,25},{17,1},{25,9},{2,18},{10... | collective-permute-start | bytes 1572872 | tf_op jit(solution)/shard_map/ppermute | solution.py:147
  172.4 26.7 %collective-permute-start.8 = (bf16[4,256,256]{2,1,0:T(8,128)(2,1)S(1)}, bf16[4,256,256]{2,1,0:T(8,128)(2,1)}, u32[]{:S(2)}, u32[]{:S(2)}) collective-permute-start(bf16[4,256,256]{2,1,0:T(8,128)(2,1)S(1)} %copy-done.6), channel_id=1, source_target_pairs={{0,24},{8,0},{16,8},{24,16},{1,25},{9,1},{17,9},{25,17},{2,26},{10... | collective-permute-start | bytes 1572872 | tf_op jit(solution)/shard_map/ppermute | solution.py:147
  197.6 43.0 %collective-permute-start.17 = (bf16[2048,256]{1,0:T(8,128)(2,1)}, bf16[2048,256]{1,0:T(8,128)(2,1)}, u32[]{:S(2)}, u32[]{:S(2)}) collective-permute-start(bf16[2048,256]{1,0:T(8,128)(2,1)} %all-gather.5.cloned.1.call-done), channel_id=1, source_target_pairs={{0,1},{1,0},{2,3},{3,2},{4,5},{5,4},{6,7},{7,6},{8,9},{9,8},{10,11... | collective-permute-start | bytes 3145736 | tf_op jit(solution)/shard_map/ppermute | solution.py:210
  199.2 41.5 %copy-start.11 = (bf16[2048,256]{1,0:T(8,128)(2,1)S(1)}, bf16[2048,256]{1,0:T(8,128)(2,1)}, u32[]{:S(2)}) copy-start(bf16[2048,256]{1,0:T(8,128)(2,1)} %all-gather.5.cloned.1.call-done) | copy-start | bytes 3145732
  200.7 11.2 %collective-permute-start.10 = (bf16[256,256]{1,0:T(8,128)(2,1)S(1)}, bf16[256,256]{1,0:T(8,128)(2,1)S(1)}, u32[]{:S(2)}, u32[]{:S(2)}) collective-permute-start(bf16[256,256]{1,0:T(8,128)(2,1)S(1)} %get-tuple-element.41), channel_id=1, source_target_pairs={{0,4},{2,6},{4,0},{6,2},{1,5},{3,7},{5,1},{7,3},{8,12},{10,14},{12... | collective-permute-start | bytes 393224 | tf_op jit(solution)/shard_map/ppermute | solution.py:147
  203.0 11.2 %collective-permute-start.11 = (bf16[256,256]{1,0:T(8,128)(2,1)S(1)}, bf16[256,256]{1,0:T(8,128)(2,1)S(1)}, u32[]{:S(2)}, u32[]{:S(2)}) collective-permute-start(bf16[256,256]{1,0:T(8,128)(2,1)S(1)} %get-tuple-element.40), channel_id=1, source_target_pairs={{0,6},{2,0},{4,2},{6,4},{1,7},{3,1},{5,3},{7,5},{8,14},{10,8},{12,... | collective-permute-start | bytes 393224 | tf_op jit(solution)/shard_map/ppermute | solution.py:147
  203.2 11.5 %collective-permute-start.9 = (bf16[256,256]{1,0:T(8,128)(2,1)S(1)}, bf16[256,256]{1,0:T(8,128)(2,1)S(1)}, u32[]{:S(2)}, u32[]{:S(2)}) collective-permute-start(bf16[256,256]{1,0:T(8,128)(2,1)S(1)} %get-tuple-element.39), channel_id=1, source_target_pairs={{0,2},{2,4},{4,6},{6,0},{1,3},{3,5},{5,7},{7,1},{8,10},{10,12},{12... | collective-permute-start | bytes 393224 | tf_op jit(solution)/shard_map/ppermute | solution.py:147
  216.8 23.8 %all-to-all-start.2 = ((bf16[16,40,256]{2,1,0:T(8,128)(2,1)}), bf16[16,40,256]{2,1,0:T(8,128)(2,1)S(1)}, u32[]{:S(2)}, u32[]{:S(2)}) async-start(bf16[16,40,256]{2,1,0:T(8,128)(2,1)} %bitcast.16), calls=%async_computation.2 | async-start | bytes 655360 | tf_op jit(solution)/shard_map/all_to_all | solution.py:196
Sparse Core Ops, SparseCore 0:
  45.0 53.5 all-gather.2
  169.6 27.9 all-gather.4

commit v2 on v0

v2 whole, which is shorter than its diff:
```python
import functools

import jax
import jax.numpy as jnp
from jax import lax
from jax.experimental import pallas as pl
from jax.experimental.pallas import tpu as pltpu
from jax.sharding import Mesh
from jax.sharding import PartitionSpec as P

DT = 16384
EPS = 1e-05
GROUP = ("x", "zh", "core")
TENSOR = ("y", "zl")
BF = jnp.bfloat16
F32 = jnp.float32
B = 256
VMEM = pl.BlockSpec(memory_space=pltpu.VMEM)
SMEM = pl.BlockSpec(memory_space=pltpu.SMEM)
PARAMS = pltpu.CompilerParams(vmem_limit_bytes=24 * 1024 * 1024)
SWAP = [(0, 1), (1, 0)]


def ring(k):
    return [(i, (i + k) % 4) for i in range(4)]


def tie(*groups):
    return lax.optimization_barrier(groups)


def shape(*dims, dtype=BF):
    return jax.ShapeDtypeStruct(dims, dtype)


def eye_mask(n):
    return lax.broadcasted_iota(jnp.int32, (n, n), 0) == lax.broadcasted_iota(jnp.int32, (n, n), 1)


def power_rows(row, dtype):
    at = lax.broadcasted_iota(jnp.int32, (16, row.shape[1]), 0)
    if dtype == F32:
        return jnp.where(at == 0, row, 0.0)
    high = row.astype(BF).astype(F32)
    rest = row - high
    middle = rest.astype(BF).astype(F32)
    low = rest - middle
    return jnp.where(at == 0, high, jnp.where(at == 1, middle, jnp.where(at == 2, low, 0.0))).astype(BF)


def piece_of(outs, k, j):
    up, down, near_up, near_down, rest_up, rest_down, own = outs
    if k == 0:
        return own, j
    if k == 1:
        return (near_up, j) if j < 2 else (rest_up, j - 2)
    if k == 2:
        return (up, j) if j < 2 else (down, j - 2)
    return (rest_down, j) if j < 2 else (near_down, j - 2)


def piece_shapes(rows):
    return [shape(2, rows, B)] * 2 + [shape(2, rows, B, dtype=F32)] * 2 + [shape(2, rows, B)] * 2 + [shape(4, rows, B, dtype=F32)]


def project_kernel(place, hidden, gain, projector, *rest):
    outs, scaled, blocks, sems = rest[:7], rest[7], rest[8], rest[9]
    y, zl = place[0], place[1]
    width = blocks.shape[2]
    copies = []
    for k in range(4):
        at = pl.ds(pl.multiple_of(((y + k) % 4) * width, width), width)
        copies.append(pltpu.make_async_copy(projector.at[:, at], blocks.at[k], sems.at[k]))
        copies[k].start()
    wide = hidden[...].astype(F32)
    scaled[...] = (wide * gain[...].astype(F32)).astype(BF)
    power = jnp.sum(wide * wide, axis=1, keepdims=True)
    power = jnp.sum(jnp.where(eye_mask(B), power, 0.0), axis=0, keepdims=True)
    for out in outs:
        rows = power_rows(power, out.dtype)
        for i in range(out.shape[0]):
            out[i, B:, :] = rows
    for k in range(4):
        copies[k].wait()
        for j in range(4):
            out, i = piece_of(outs, k, j)
            at = pl.ds(pl.multiple_of(((zl + j) % 4) * B, B), B)
            out[i, :B, :] = jnp.dot(scaled[...], blocks[k, :, at], preferred_element_type=F32).astype(out.dtype)


def project(place, hidden, gain, projector):
    rows, depth = hidden.shape
    width = projector.shape[1] // 4
    return pl.pallas_call(
        project_kernel,
        in_specs=[SMEM, VMEM, VMEM, pl.BlockSpec(memory_space=pltpu.HBM)],
        out_specs=[VMEM] * 7,
        out_shape=piece_shapes(rows + 16),
        scratch_shapes=[
            pltpu.VMEM((rows, depth), BF),
            pltpu.VMEM((4, depth, width), BF),
            pltpu.SemaphoreType.DMA((4,)),
        ],
        compiler_params=pltpu.CompilerParams(vmem_limit_bytes=48 * 1024 * 1024),
        cost_estimate=pl.CostEstimate(
            flops=2 * rows * depth * 4 * width, bytes_accessed=2 * depth * 4 * width, transcendentals=0
        ),
        name="project",
    )(place, hidden, gain.reshape(1, depth), projector)


def put_sum(out, at, terms):
    rows = terms[0].shape[0]
    total = sum(t[:B, :].astype(F32) for t in terms).astype(out.dtype)
    if at is None:
        out[:B, :] = total
    else:
        out[at, :B, :] = total
    if rows > B:
        power = sum(jnp.sum(t[B:, :].astype(F32), axis=0, keepdims=True) for t in terms)
        power = power_rows(power, out.dtype)
        if at is None:
            out[B:, :] = power
        else:
            out[at, B:, :] = power


def relay_kernel(near_up, near_down, rest_up, rest_down, got_up, got_down, up, down):
    for i in range(2):
        put_sum(up, i, [near_up.at[i], got_up.at[i]])
        put_sum(down, 2 + i, [near_down.at[i], got_down.at[i]])
        up[2 + i] = rest_up[i]
        down[i] = rest_down[i]


def relay(*parts):
    rows = parts[0].shape[1]
    return pl.pallas_call(
        relay_kernel,
        in_specs=[VMEM] * 6,
        out_specs=[VMEM] * 2,
        out_shape=[shape(4, rows, B)] * 2,
        compiler_params=PARAMS,
        name="relay",
    )(*parts)


def fold_kernel(own, far_up, far_down, *outs):
    for j, out in enumerate(outs):
        put_sum(out, None, [own.at[j], far_up.at[j], far_down.at[j]])


def fold(*parts):
    rows = parts[0].shape[1]
    return pl.pallas_call(
        fold_kernel,
        in_specs=[VMEM] * 3,
        out_specs=[VMEM] * 4,
        out_shape=[shape(rows, B, dtype=F32)] + [shape(rows, B)] * 3,
        compiler_params=PARAMS,
        name="fold",
    )(*parts)


def middle_kernel(place, a0, a1, a2, a3, weight, resid, t0, t1, t2, t3, *outs):
    pieces, keep, send = outs[:7], outs[7], outs[8]
    y, zl, core = place[0], place[1], place[2]
    attn = (a0, a1, a2, a3)
    parts = (t0, t1, t2, t3)
    total = sum(r[:B, :].astype(F32) for r in parts)
    power = jnp.sum(sum(r[B:, :].astype(F32) for r in parts), axis=0, keepdims=True)
    power = jnp.sum(jnp.where(eye_mask(B), power, 0.0), axis=1, keepdims=True)
    value = resid[...].astype(F32) - total * lax.rsqrt(power / DT + EPS)
    for k in range(4):
        for j in range(4):
            w = weight[((y + 4 - k) % 4) * 4 + (zl + 4 - j) % 4]
            value += jnp.dot(attn[k][j], w, preferred_element_type=F32)
    residual = value.astype(BF)
    for k in range(4):
        for j in range(4):
            out, i = piece_of(pieces, k, j)
            w = weight[((y + k) % 4) * 4 + (zl + j) % 4]
            out[i] = lax.dot_general(
                residual, w, (((1,), (1,)), ((), ())), preferred_element_type=F32
            ).astype(out.dtype)
    for half in range(2):

        @pl.when(core == half)
        def _(half=half):
            for m in range(16):
                out = keep if m // 8 == half else send
                out[m % 8] = lax.dot_general(
                    attn[m // 4][m % 4], residual, (((0,), (0,)), ((), ())), preferred_element_type=F32
                ).astype(out.dtype)


def middle(place, chunks, weight, resid, parts):
    return pl.pallas_call(
        middle_kernel,
        in_specs=[SMEM] + [VMEM] * 10,
        out_specs=[VMEM] * 9,
        out_shape=piece_shapes(B) + [shape(8, B, B, dtype=F32)] * 2,
        compiler_params=PARAMS,
        name="middle",
    )(place, *chunks, weight, resid, *parts)


def pair_kernel(a, b, out):
    out[:, :B] = a[...]
    out[:, B:] = b[...]


def pair(a, b):
    return pl.pallas_call(
        pair_kernel,
        in_specs=[VMEM] * 2,
        out_specs=VMEM,
        out_shape=shape(a.shape[0], 2 * B),
        compiler_params=PARAMS,
        name="pair",
    )(a, b)


def pick_kernel(at, slots, first, second):
    rows = lax.broadcasted_iota(jnp.int32, (B, slots.shape[0]), 0)
    select = jnp.where(rows == at[...], 1.0, 0.0).astype(BF)
    first[...] = jnp.dot(select, slots[:, :B], preferred_element_type=F32).astype(BF)
    second[...] = jnp.dot(select, slots[:, B:], preferred_element_type=F32).astype(BF)


def pick(at, slots):
    return pl.pallas_call(
        pick_kernel,
        in_specs=[VMEM] * 2,
        out_specs=[VMEM] * 2,
        out_shape=[shape(B, B)] * 2,
        compiler_params=PARAMS,
        name="pick",
    )(at.reshape(1, -1), slots.reshape(-1, 2 * B))


def put_kernel(at, a, b, c, d, out):
    grad = sum(r[...].astype(F32) for r in (a, b, c, d)).astype(BF)
    rows = lax.broadcasted_iota(jnp.int32, (out.shape[0], B), 1)
    select = jnp.where(rows == at[...], 1.0, 0.0).astype(BF)
    out[...] = jnp.dot(select, grad, preferred_element_type=F32).astype(BF)


def put(at, parts):
    at = at.reshape(-1)
    return pl.pallas_call(
        put_kernel,
        in_specs=[VMEM] * 5,
        out_specs=VMEM,
        out_shape=shape(at.shape[0], B),
        compiler_params=PARAMS,
        name="put",
    )(at.reshape(-1, 1), *parts)


def join_kernel(*refs):
    out, i = refs[-1], 0
    for ref in refs[:-1]:
        for j in range(ref.shape[0]):
            out[i] = ref[j]
            i += 1


def join(*parts):
    return pl.pallas_call(
        join_kernel,
        in_specs=[VMEM] * len(parts),
        out_specs=VMEM,
        out_shape=shape(sum(p.shape[0] for p in parts), *parts[0].shape[1:]),
        compiler_params=PARAMS,
        name="join",
    )(*parts)


def share_kernel(place, keep, other, *outs):
    for k, out in enumerate(outs):
        for i in range(2):
            at = ((place[3] + k) % 4) * 2 + i
            out[i] = (keep[at] + other[at]).astype(out.dtype)


def share(place, keep, other):
    return pl.pallas_call(
        share_kernel,
        in_specs=[SMEM] + [VMEM] * 2,
        out_specs=[VMEM] * 4,
        out_shape=[shape(2, B, B, dtype=F32)] + [shape(2, B, B)] * 3,
        compiler_params=PARAMS,
        name="share",
    )(place, keep, other)


def total_kernel(scale, *refs):
    refs[-1][...] = (sum(r[...].astype(F32) for r in refs[:-1]) * scale).astype(refs[-1].dtype)


def total(parts, scale=1.0):
    return pl.pallas_call(
        functools.partial(total_kernel, scale),
        in_specs=[VMEM] * len(parts),
        out_specs=VMEM,
        out_shape=shape(*parts[0].shape),
        compiler_params=PARAMS,
        name="total",
    )(*parts)


def assemble_kernel(place, mine, twin, out):
    y, zl, core, x = place[0], place[1], place[2], place[3]
    for s in range(8):
        within = ((x + 4 - s // 2) % 4) * 2 + s % 2
        for source, half in ((mine, core), (twin, 1 - core)):
            m = half * 8 + within
            out[((y + 4 - m // 4) % 4) * 4 + (zl + 4 - m % 4) % 4] = source[s]


def assemble(place, mine, twin):
    return pl.pallas_call(
        assemble_kernel,
        in_specs=[SMEM, VMEM, VMEM],
        out_specs=VMEM,
        out_shape=shape(16, B, B),
        compiler_params=PARAMS,
        name="assemble",
    )(place, mine, twin)


def send_on(piece, axis, k):
    return lax.ppermute(piece, axis, ring(k))


def relay_first(parts):
    return send_on(parts[0], "y", 1), send_on(parts[1], "y", 3)


def relay_second(parts, got):
    up, down = relay(*parts[2:6], *got)
    return send_on(up, "y", 1), send_on(down, "y", 3)


def body(hidden, gain, projector, doc_lengths, doc_student, resid, attn, weight):
    groups, slot = 16, attn.shape[0] // 16
    rows = hidden.shape[0]
    me = lax.axis_index(GROUP)
    x, y, zl, core = (lax.axis_index(a) for a in ("x", "y", "zl", "core"))
    place = jnp.stack([y, zl, core, x])

    offsets = jnp.cumsum(doc_lengths, axis=1) - doc_lengths
    matches = (doc_student[me][:, None] == jnp.arange(groups, dtype=jnp.int32)[None, :]).astype(jnp.int32)
    length = jnp.sum(matches * doc_lengths[me][:, None], axis=0)
    offset = jnp.sum(matches * offsets[me][:, None], axis=0)
    position = jnp.arange(slot, dtype=jnp.int32)
    where = jnp.where(position[None, :] < length[:, None], offset[:, None] + position[None, :], -1)

    both = pair(attn, resid).reshape(groups, slot, 2 * B)
    slots = lax.all_to_all(both, GROUP, 0, 0, tiled=True)
    teacher = project(place, hidden, gain, projector)
    got = relay_first(teacher)
    attn_rows, resid_rows = pick(where, slots)
    got, attn_rows = tie(got, attn_rows)
    along_zl = [attn_rows] + [send_on(attn_rows, "zl", j) for j in (1, 2, 3)]
    far = relay_second(teacher, got)

    chunk = join(*(p[None] for p in along_zl))
    far, chunk = tie(far, chunk)
    chunks = [chunk] + [send_on(chunk, "y", k) for k in (1, 2, 3)]
    folded = fold(teacher[6], *far)
    parts = [folded[0]] + [send_on(folded[j], "zl", j) for j in (1, 2, 3)]

    outs = middle(place, chunks, weight.reshape(16, B, B), resid_rows, parts)
    grads, keep, send = outs[:7], outs[7], outs[8]

    got = relay_first(grads)
    other = lax.ppermute(send, "core", SWAP)
    pieces = share(place, keep, other)
    got, pieces = tie(got, pieces)
    pieces = [pieces[0]] + [send_on(pieces[k], "x", k) for k in (1, 2, 3)]
    far = relay_second(grads, got)

    near = total(pieces)
    away = lax.ppermute(near, "zh", SWAP)
    far, near = tie(far, near)
    folded = fold(grads[6], *far)
    grad_parts = [folded[0]] + [send_on(folded[j], "zl", j) for j in (1, 2, 3)]
    done = total([near, away], 1.0 / (groups * rows))
    after, before = send_on(done, "x", 1), send_on(done, "x", 3)
    grad_parts, after, before = tie(grad_parts, after, before)
    slots = put(where, grad_parts)
    slots = lax.all_to_all(slots.reshape(groups, slot, B), GROUP, 0, 0, tiled=True)
    mine = [done, after, send_on(done, "x", 2), before]
    slots, mine = tie(slots, mine)
    mine = join(*mine)
    twin = lax.ppermute(mine, "core", SWAP)
    weight_grad = assemble(place, mine, twin).reshape(weight.shape)
    return slots.reshape(attn.shape), weight_grad

def solution(mesh):
    fine = Mesh(mesh.devices.reshape(4, 2, 4, 4, 2), ("x", "zh", "y", "zl", "core"))
    return jax.shard_map(
        body,
        mesh=fine,
        in_specs=(
            P(GROUP, TENSOR),
            P(TENSOR),
            P(TENSOR, None),
            P(),
            P(),
            P(GROUP, TENSOR),
            P(GROUP, TENSOR),
            P(None, TENSOR),
        ),
        out_specs=(P(GROUP, TENSOR), P(None, TENSOR)),
        check_vma=False,
    )
```

time: 884 us -> 169 us (0.19)
  waiting for transfers between devices: 774 us -> 99.9 us
  starting transfers between devices: 10.9 us -> 45.2 us
  blocking collectives: 33.4 us -> 0 us
  matrix products: 25.2 us -> 0 us
  Pallas kernels: 0 us -> 15.9 us
  between operations: 13.9 us -> 0.83 us
  other arithmetic: 9.66 us -> 0.43 us
    reduce_scatter x2 -> x0, waiting for transfers between devices: 454 us -> none  [the longest x1 232 us: body(): lax.psum_scatter(partial_value, 'tensor', scatter_dimension=1, tiled=True)]
    psum x1 -> x0, waiting for transfers between devices: 226 us -> none  [body(): summed = lax.psum(local_weight, ('teacher', 'student'))]
    ppermute x0 -> x29, waiting for transfers between devices: none -> 85.7 us  [the longest x26 67.5 us: send_on(): return lax.ppermute(piece, axis, ring(k))]
    all_to_all x1 -> x2, waiting for transfers between devices: 58.1 us -> 14.3 us  [the longest x1 12.8 us: body(): slots = lax.all_to_all(both, GROUP, 0, 0, tiled=True)]
    all_gather x1 -> x0, waiting for transfers between devices: 35.1 us -> none  [body(): gathered = lax.all_gather(student_attn, 'tensor', axis=1, tiled=True)]
    psum x1 -> x0, blocking collectives: 33.4 us -> none  [body(): power = lax.psum(jnp.sum(wide * wide, axis=1), 'tensor')]
    ppermute x0 -> x29, starting transfers between devices: none -> 28.2 us  [the longest x26 23.5 us: send_on(): return lax.ppermute(piece, axis, ring(k))]
    dot_general x4 -> x0, matrix products: 25.2 us -> none  [the longest x1 11.5 us: body(): jnp.dot(normed, projector, preferred_element_type=jnp.float32)]
  transfers between devices with their start and end apart: 5 -> 31, of which waited for: 5 -> 23; matrix products, arithmetic and copies ran while one was open for 4% -> 0% of each run, Pallas kernels for 0% -> 5%
where the time goes in v2:
time: 169 us
  waiting for transfers between devices  99.9 us (59%)
  starting transfers between devices  45.2 us (27%)
  Pallas kernels  15.9 us (9%)
  local copies, waits for them, and re-layouts  6.34 us (4%)
    ppermute x26, waiting for transfers between devices, send_on(): return lax.ppermute(piece, axis, ring(k))  67.5 us
    ppermute x26, starting transfers between devices, send_on(): return lax.ppermute(piece, axis, ring(k))  23.5 us
    ppermute x1, waiting for transfers between devices, body(): away = lax.ppermute(near, 'zh', SWAP)  13.6 us
    all_to_all x1, waiting for transfers between devices, body(): slots = lax.all_to_all(both, GROUP, 0, 0, tiled=True)  12.8 us
    all_to_all x1, starting transfers between devices, body(): slots = lax.all_to_all(both, GROUP, 0, 0, tiled=True)  10.7 us
    all_to_all x1, starting transfers between devices, body(): lax.all_to_all(slots.reshape(groups, slot, B), GROUP, 0, 0, tiled=True)  6.34 us
    unnamed x23, local copies, waits for them, and re-layouts  6.09 us
    pallas_call x1, Pallas kernels, project(): pl.pallas_call(project_kernel, in_specs=[SMEM, VMEM, VMEM, pl.BlockSpec(m...  5.79 us
  transfers between devices with their start and end apart: 31, of which 23 were waited for; matrix products, arithmetic and copies ran while one was open for 0% of the time, Pallas kernels for 5%

profile of v2, /device:TPU:57, one launch (start us, length us, event | category | flops | bytes accessed | tf_op | source)
XLA Modules:
  0.0 168.7 jit_solution(5805388170571664338)
XLA Ops:
  0.7 1.0 copy-done.3
  1.7 1.0 copy-done.4
  2.7 0.9 pair.1
  3.5 10.7 %all-to-all-start = ((bf16[16,40,512]{2,1,0:T(8,128)(2,1)}), bf16[16,40,512]{2,1,0:T(8,128)(2,1)S(1)}, u32[]{:S(2)}, u32[]{:S(2)}) async-start(bf16[16,40,512]{2,1,0:T(8,128)(2,1)} %bitcast.7), calls=%async_computation | async-start | bytes 1310720 | tf_op jit(solution)/shard_map/all_to_all | solution.py:361
  14.4 5.8 %project.1 = (bf16[2,272,256]{2,1,0:T(8,128)(2,1)}, bf16[2,272,256]{2,1,0:T(8,128)(2,1)}, f32[2,272,256]{2,1,0:T(8,128)S(1)}, f32[2,272,256]{2,1,0:T(8,128)S(1)}...) custom-call(s32[4]{0:T(128)S(1)} %pad_add_fusion.place, ...), custom_call_target="tpu_custom_call" | custom-call | flops 2147483648 | bytes 8388608 | tf_op jit(solution)/shard_map/project/pallas_call | solution.py:94
  21.6 1.5 collective-permute-start.1
  23.6 12.8 %all-to-all-done = bf16[16,40,512]{2,1,0:T(8,128)(2,1)S(1)} async-done(((bf16[16,40,512]{2,1,0:T(8,128)(2,1)}), bf16[16,40,512]{2,1,0:T(8,128)(2,1)S(1)}, u32[]{:S(2)}, u32[]{:S(2)}) %all-to-all-start) | async-done | bytes 655392 | tf_op jit(solution)/shard_map/all_to_all | solution.py:361
  36.8 0.9 copy-done.6
  37.7 1.0 copy-done.8
  38.9 1.5 collective-permute-start.3
  41.1 1.2 collective-permute-start.6
  42.3 2.2 %collective-permute-done.4 = bf16[256,256]{1,0:T(8,128)(2,1)S(1)} collective-permute-done((bf16[256,256]{1,0:T(8,128)(2,1)S(1)}, bf16[256,256]{1,0:T(8,128)(2,1)S(1)}, u32[]{:S(2)}, u32[]{:S(2)}) %collective-permute-start.4) | collective-permute-done | bytes 131104 | tf_op jit(solution)/shard_map/ppermute | solution.py:334
  44.5 2.8 %collective-permute-done.5 = bf16[256,256]{1,0:T(8,128)(2,1)S(1)} collective-permute-done((bf16[256,256]{1,0:T(8,128)(2,1)S(1)}, bf16[256,256]{1,0:T(8,128)(2,1)S(1)}, u32[]{:S(2)}, u32[]{:S(2)}) %collective-permute-start.5) | collective-permute-done | bytes 131104 | tf_op jit(solution)/shard_map/ppermute | solution.py:334
  47.4 4.2 %collective-permute-done.6 = bf16[256,256]{1,0:T(8,128)(2,1)S(1)} collective-permute-done((bf16[256,256]{1,0:T(8,128)(2,1)S(1)}, bf16[256,256]{1,0:T(8,128)(2,1)S(1)}, u32[]{:S(2)}, u32[]{:S(2)}) %collective-permute-start.6) | collective-permute-done | bytes 131104 | tf_op jit(solution)/shard_map/ppermute | solution.py:334
  51.9 1.2 collective-permute-done.3.far_down
  53.2 1.7 collective-permute-start.8
  56.5 2.9 %collective-permute-done.10.t1 = bf16[272,256]{1,0:T(8,128)(2,1)S(1)} collective-permute-done((bf16[272,256]{1,0:T(8,128)(2,1)S(1)}, bf16[272,256]{1,0:T(8,128)(2,1)S(1)}, u32[]{:S(2)}, u32[]{:S(2)}) %collective-permute-start.10) | collective-permute-done | bytes 139296 | tf_op jit(solution)/shard_map/ppermute | solution.py:334
  59.4 0.9 collective-permute-start.12
  60.3 1.5 collective-permute-done.11.t2
  61.8 6.3 %collective-permute-done.12.t3 = bf16[272,256]{1,0:T(8,128)(2,1)S(1)} collective-permute-done((bf16[272,256]{1,0:T(8,128)(2,1)S(1)}, bf16[272,256]{1,0:T(8,128)(2,1)S(1)}, u32[]{:S(2)}, u32[]{:S(2)}) %collective-permute-start.12) | collective-permute-done | bytes 139296 | tf_op jit(solution)/shard_map/ppermute | solution.py:334
  68.1 11.7 %collective-permute-done.9.a3 = bf16[4,256,256]{2,1,0:T(8,128)(2,1)S(1)} collective-permute-done((bf16[4,256,256]{2,1,0:T(8,128)(2,1)S(1)}, bf16[4,256,256]{2,1,0:T(8,128)(2,1)S(1)}, u32[]{:S(2)}, u32[]{:S(2)}) %collective-permute-start.9) | collective-permute-done | bytes 524320 | tf_op jit(solution)/shard_map/ppermute | solution.py:334
  79.8 3.7 %middle.1 = (bf16[2,256,256]{2,1,0:T(8,128)(2,1)S(1)}, bf16[2,256,256]{2,1,0:T(8,128)(2,1)S(1)}, f32[2,256,256]{2,1,0:T(8,128)S(1)}, f32[2,256,256]{2,1,0:T(8,12...) custom-call(s32[4]{0:T(128)S(1)} %pad_add_fusion.place, ...), custom_call_target="tpu_custom_call" | custom-call | tf_op jit(solution)/shard_map/middle/pallas_call | solution.py:198
  85.5 2.3 %collective-permute-done.15.other = f32[8,256,256]{2,1,0:T(8,128)S(1)} collective-permute-done((f32[8,256,256]{2,1,0:T(8,128)S(1)}, f32[8,256,256]{2,1,0:T(8,128)S(1)}, u32[]{:S(2)}, u32[]{:S(2)}) %collective-permute-start.15) | collective-permute-done | bytes 2097184 | tf_op jit(solution)/shard_map/ppermute | solution.py:379
  87.8 0.9 share.1
  88.7 3.2 %collective-permute-done.13.got_up = bf16[2,256,256]{2,1,0:T(8,128)(2,1)S(1)} collective-permute-done((bf16[2,256,256]{2,1,0:T(8,128)(2,1)S(1)}, bf16[2,256,256]{2,1,0:T(8,128)(2,1)S(1)}, u32[]{:S(2)}, u32[]{:S(2)}) %collective-permute-start.13) | collective-permute-done | bytes 262176 | tf_op jit(solution)/shard_map/ppermute | solution.py:334
  91.9 1.7 collective-permute-done.14.got_down
  94.3 1.0 collective-permute-start.19
  95.8 1.1 collective-permute-start.17
  97.0 1.6 collective-permute-start.20
  98.5 3.7 %collective-permute-done.18.refs_1_ = bf16[2,256,256]{2,1,0:T(8,128)(2,1)S(1)} collective-permute-done((bf16[2,256,256]{2,1,0:T(8,128)(2,1)S(1)}, bf16[2,256,256]{2,1,0:T(8,128)(2,1)S(1)}, u32[]{:S(2)}, u32[]{:S(2)}) %collective-permute-start.18) | collective-permute-done | bytes 262176 | tf_op jit(solution)/shard_map/ppermute | solution.py:334
  102.3 3.8 %collective-permute-done.19.refs_2_ = bf16[2,256,256]{2,1,0:T(8,128)(2,1)S(1)} collective-permute-done((bf16[2,256,256]{2,1,0:T(8,128)(2,1)S(1)}, bf16[2,256,256]{2,1,0:T(8,128)(2,1)S(1)}, u32[]{:S(2)}, u32[]{:S(2)}) %collective-permute-start.19) | collective-permute-done | bytes 262176 | tf_op jit(solution)/shard_map/ppermute | solution.py:334
  106.1 1.5 collective-permute-done.20.refs_3_
  107.7 2.9 %collective-permute-start.24 = (bf16[2,256,256]{2,1,0:T(8,128)(2,1)S(1)}, bf16[2,256,256]{2,1,0:T(8,128)(2,1)S(1)}, u32[]{:S(2)}, u32[]{:S(2)}) collective-permute-start(bf16[2,256,256]{2,1,0:T(8,128)(2,1)S(1)} %total.2.refs_0_), channel_id=1, source_target_pairs={{0,32},{32,0},{1,33},{33,1},{2,34},{34,2},{3,35},{35,3},{4,36},{36... | collective-permute-start | bytes 786440 | tf_op jit(solution)/shard_map/ppermute | solution.py:386
  110.6 13.6 %collective-permute-done.24.refs_1_ = bf16[2,256,256]{2,1,0:T(8,128)(2,1)S(1)} collective-permute-done((bf16[2,256,256]{2,1,0:T(8,128)(2,1)S(1)}, bf16[2,256,256]{2,1,0:T(8,128)(2,1)S(1)}, u32[]{:S(2)}, u32[]{:S(2)}) %collective-permute-start.24) | collective-permute-done | bytes 262176 | tf_op jit(solution)/shard_map/ppermute | solution.py:386
  124.3 1.7 %collective-permute-start.25 = (bf16[2,256,256]{2,1,0:T(8,128)(2,1)S(1)}, bf16[2,256,256]{2,1,0:T(8,128)(2,1)S(1)}, u32[]{:S(2)}, u32[]{:S(2)}) collective-permute-start(bf16[2,256,256]{2,1,0:T(8,128)(2,1)S(1)} %total.3.refs_0_), channel_id=1, source_target_pairs={{0,64},{64,128},{128,192},{192,0},{1,65},{65,129},{129,193},{193,1... | collective-permute-start | bytes 786440 | tf_op jit(solution)/shard_map/ppermute | solution.py:334
  126.0 1.7 %collective-permute-start.26 = (bf16[2,256,256]{2,1,0:T(8,128)(2,1)S(1)}, bf16[2,256,256]{2,1,0:T(8,128)(2,1)S(1)}, u32[]{:S(2)}, u32[]{:S(2)}) collective-permute-start(bf16[2,256,256]{2,1,0:T(8,128)(2,1)S(1)} %total.3.refs_0_), channel_id=1, source_target_pairs={{0,192},{64,0},{128,64},{192,128},{1,193},{65,1},{129,65},{193,129... | collective-permute-start | bytes 786440 | tf_op jit(solution)/shard_map/ppermute | solution.py:334
  128.3 1.4 collective-permute-start.23
  129.8 2.5 %collective-permute-done.21.b = bf16[256,256]{1,0:T(8,128)(2,1)S(1)} collective-permute-done((bf16[256,256]{1,0:T(8,128)(2,1)S(1)}, bf16[256,256]{1,0:T(8,128)(2,1)S(1)}, u32[]{:S(2)}, u32[]{:S(2)}) %collective-permute-start.21) | collective-permute-done | bytes 131104 | tf_op jit(solution)/shard_map/ppermute | solution.py:334
  132.3 1.0 collective-permute-done.22.c
  133.3 7.3 %collective-permute-done.23.d = bf16[256,256]{1,0:T(8,128)(2,1)S(1)} collective-permute-done((bf16[256,256]{1,0:T(8,128)(2,1)S(1)}, bf16[256,256]{1,0:T(8,128)(2,1)S(1)}, u32[]{:S(2)}, u32[]{:S(2)}) %collective-permute-start.23) | collective-permute-done | bytes 131104 | tf_op jit(solution)/shard_map/ppermute | solution.py:334
  140.6 1.0 put.1
  141.7 6.3 %all-to-all-start.1 = ((bf16[16,40,256]{2,1,0:T(8,128)(2,1)}), bf16[16,40,256]{2,1,0:T(8,128)(2,1)S(1)}, u32[]{:S(2)}, u32[]{:S(2)}) async-start(bf16[16,40,256]{2,1,0:T(8,128)(2,1)} %bitcast.14), calls=%async_computation.1 | async-start | bytes 655360 | tf_op jit(solution)/shard_map/all_to_all | solution.py:394
  148.0 2.9 %collective-permute-start.27 = (bf16[2,256,256]{2,1,0:T(8,128)(2,1)S(1)}, bf16[2,256,256]{2,1,0:T(8,128)(2,1)S(1)}, u32[]{:S(2)}, u32[]{:S(2)}) collective-permute-start(bf16[2,256,256]{2,1,0:T(8,128)(2,1)S(1)} %total.3.refs_0_), channel_id=1, source_target_pairs={{0,128},{64,192},{128,0},{192,64},{1,129},{65,193},{129,1},{193,65... | collective-permute-start | bytes 786440 | tf_op jit(solution)/shard_map/ppermute | solution.py:334
  150.9 9.7 %collective-permute-done.27.refs_2_ = bf16[2,256,256]{2,1,0:T(8,128)(2,1)S(1)} collective-permute-done((bf16[2,256,256]{2,1,0:T(8,128)(2,1)S(1)}, bf16[2,256,256]{2,1,0:T(8,128)(2,1)S(1)}, u32[]{:S(2)}, u32[]{:S(2)}) %collective-permute-start.27) | collective-permute-done | bytes 262176 | tf_op jit(solution)/shard_map/ppermute | solution.py:334
  160.6 1.4 all-to-all-done.1
  162.1 1.3 collective-permute-start.28
  163.4 2.3 %collective-permute-done.28.twin = bf16[8,256,256]{2,1,0:T(8,128)(2,1)S(1)} collective-permute-done((bf16[8,256,256]{2,1,0:T(8,128)(2,1)S(1)}, bf16[8,256,256]{2,1,0:T(8,128)(2,1)S(1)}, u32[]{:S(2)}, u32[]{:S(2)}) %collective-permute-start.28) | collective-permute-done | bytes 1048608 | tf_op jit(solution)/shard_map/ppermute | solution.py:398
  165.7 2.3 %assemble.1 = bf16[16,256,256]{2,1,0:T(8,128)(2,1)} custom-call(s32[4]{0:T(128)S(1)} %pad_add_fusion.place, bf16[8,256,256]{2,1,0:T(8,128)(2,1)S(1)} %join.3.mine, bf16[8,256,256]{2,1,0:T(8,128)(2,1)S(1)} %collective-permute-done.28.twin), custom_call_target="tpu_custom_call" | custom-call | tf_op jit(solution)/shard_map/assemble/pallas_call | solution.py:323
  (61 shorter events, 10.4 us)
Async XLA Ops:
  0.6 22.7 %copy-start = (s32[16,16]{1,0:T(8,128)S(1)}, s32[16,16]{1,0:T(8,128)}, u32[]{:S(2)}) copy-start(s32[16,16]{1,0:T(8,128)} %param.12) | copy-start | bytes 3076
  0.6 13.7 %copy-start.2 = (bf16[256,1024]{1,0:T(8,128)(2,1)S(1)}, bf16[256,1024]{1,0:T(8,128)(2,1)}, u32[]{:S(2)}) copy-start(bf16[256,1024]{1,0:T(8,128)(2,1)} %hidden.1) | copy-start | bytes 1572868
  0.7 1.0 copy-start.3
  1.7 1.0 copy-start.4
  2.7 11.6 %copy-start.10 = (bf16[1024]{0:T(1024)(128)(2,1)S(1)}, bf16[1024]{0:T(1024)(128)(2,1)}, u32[]{:S(2)}) copy-start(bf16[1024]{0:T(1024)(128)(2,1)} %param.9) | copy-start | bytes 6148
  3.5 32.8 %all-to-all-start = ((bf16[16,40,512]{2,1,0:T(8,128)(2,1)}), bf16[16,40,512]{2,1,0:T(8,128)(2,1)S(1)}, u32[]{:S(2)}, u32[]{:S(2)}) async-start(bf16[16,40,512]{2,1,0:T(8,128)(2,1)} %bitcast.7), calls=%async_computation | async-start | bytes 1310720 | tf_op jit(solution)/shard_map/all_to_all | solution.py:361
  14.4 8.7 %copy-start.9 = (s32[16,16]{1,0:T(8,128)S(1)}, s32[16,16]{1,0:T(8,128)}, u32[]{:S(2)}) copy-start(s32[16,16]{1,0:T(8,128)} %param.11) | copy-start | bytes 3076
  20.2 0.7 copy-start.5
  20.9 0.7 copy-start.7
  21.6 15.2 %collective-permute-start = (bf16[2,272,256]{2,1,0:T(8,128)(2,1)}, bf16[2,272,256]{2,1,0:T(8,128)(2,1)S(1)}, u32[]{:S(2)}, u32[]{:S(2)}) collective-permute-start(bf16[2,272,256]{2,1,0:T(8,128)(2,1)} %get-tuple-element.66), channel_id=1, source_target_pairs={{0,8},{8,16},{16,24},{24,0},{1,9},{9,17},{17,25},{25,1},{2,10},{10... | collective-permute-start | bytes 835592 | tf_op jit(solution)/shard_map/ppermute | solution.py:334
  21.6 15.2 %collective-permute-start.1 = (bf16[2,272,256]{2,1,0:T(8,128)(2,1)}, bf16[2,272,256]{2,1,0:T(8,128)(2,1)S(1)}, u32[]{:S(2)}, u32[]{:S(2)}) collective-permute-start(bf16[2,272,256]{2,1,0:T(8,128)(2,1)} %get-tuple-element.67), channel_id=1, source_target_pairs={{0,24},{8,0},{16,8},{24,16},{1,25},{9,1},{17,9},{25,17},{2,26},{10... | collective-permute-start | bytes 835592 | tf_op jit(solution)/shard_map/ppermute | solution.py:334
  36.8 1.0 copy-start.6
  37.7 1.0 copy-start.8
  38.8 40.9 %copy-start.1 = (bf16[4096,256]{1,0:T(8,128)(2,1)S(1)}, bf16[4096,256]{1,0:T(8,128)(2,1)}, u32[]{:S(2)}) copy-start(bf16[4096,256]{1,0:T(8,128)(2,1)} %param.15) | copy-start | bytes 6291460
  38.9 13.0 %collective-permute-start.2 = (bf16[4,272,256]{2,1,0:T(8,128)(2,1)S(1)}, bf16[4,272,256]{2,1,0:T(8,128)(2,1)S(1)}, u32[]{:S(2)}, u32[]{:S(2)}) collective-permute-start(bf16[4,272,256]{2,1,0:T(8,128)(2,1)S(1)} %get-tuple-element.71), channel_id=1, source_target_pairs={{0,8},{8,16},{16,24},{24,0},{1,9},{9,17},{17,25},{25,1},{2,10},{10... | collective-permute-start | bytes 1671176 | tf_op jit(solution)/shard_map/ppermute | solution.py:334
  38.9 14.1 %collective-permute-start.3 = (bf16[4,272,256]{2,1,0:T(8,128)(2,1)S(1)}, bf16[4,272,256]{2,1,0:T(8,128)(2,1)S(1)}, u32[]{:S(2)}, u32[]{:S(2)}) collective-permute-start(bf16[4,272,256]{2,1,0:T(8,128)(2,1)S(1)} %get-tuple-element.72), channel_id=1, source_target_pairs={{0,24},{8,0},{16,8},{24,16},{1,25},{9,1},{17,9},{25,17},{2,26},{10... | collective-permute-start | bytes 1671176 | tf_op jit(solution)/shard_map/ppermute | solution.py:334
  40.4 4.1 %collective-permute-start.4 = (bf16[256,256]{1,0:T(8,128)(2,1)S(1)}, bf16[256,256]{1,0:T(8,128)(2,1)S(1)}, u32[]{:S(2)}, u32[]{:S(2)}) collective-permute-start(bf16[256,256]{1,0:T(8,128)(2,1)S(1)} %get-tuple-element.73), channel_id=1, source_target_pairs={{0,2},{2,4},{4,6},{6,0},{1,3},{3,5},{5,7},{7,1},{8,10},{10,12},{12... | collective-permute-start | bytes 393224 | tf_op jit(solution)/shard_map/ppermute | solution.py:334
  41.1 6.2 %collective-permute-start.5 = (bf16[256,256]{1,0:T(8,128)(2,1)S(1)}, bf16[256,256]{1,0:T(8,128)(2,1)S(1)}, u32[]{:S(2)}, u32[]{:S(2)}) collective-permute-start(bf16[256,256]{1,0:T(8,128)(2,1)S(1)} %get-tuple-element.73), channel_id=1, source_target_pairs={{0,4},{2,6},{4,0},{6,2},{1,5},{3,7},{5,1},{7,3},{8,12},{10,14},{12... | collective-permute-start | bytes 393224 | tf_op jit(solution)/shard_map/ppermute | solution.py:334
  41.1 10.4 %collective-permute-start.6 = (bf16[256,256]{1,0:T(8,128)(2,1)S(1)}, bf16[256,256]{1,0:T(8,128)(2,1)S(1)}, u32[]{:S(2)}, u32[]{:S(2)}) collective-permute-start(bf16[256,256]{1,0:T(8,128)(2,1)S(1)} %get-tuple-element.73), channel_id=1, source_target_pairs={{0,6},{2,0},{4,2},{6,4},{1,7},{3,1},{5,3},{7,5},{8,14},{10,8},{12,... | collective-permute-start | bytes 393224 | tf_op jit(solution)/shard_map/ppermute | solution.py:334
  53.1 15.0 %collective-permute-start.7 = (bf16[4,256,256]{2,1,0:T(8,128)(2,1)S(1)}, bf16[4,256,256]{2,1,0:T(8,128)(2,1)S(1)}, u32[]{:S(2)}, u32[]{:S(2)}) collective-permute-start(bf16[4,256,256]{2,1,0:T(8,128)(2,1)S(1)} %join.2.a0), channel_id=1, source_target_pairs={{0,8},{8,16},{16,24},{24,0},{1,9},{9,17},{17,25},{25,1},{2,10},{10... | collective-permute-start | bytes 1572872 | tf_op jit(solution)/shard_map/ppermute | solution.py:334
  53.2 14.9 %collective-permute-start.8 = (bf16[4,256,256]{2,1,0:T(8,128)(2,1)S(1)}, bf16[4,256,256]{2,1,0:T(8,128)(2,1)S(1)}, u32[]{:S(2)}, u32[]{:S(2)}) collective-permute-start(bf16[4,256,256]{2,1,0:T(8,128)(2,1)S(1)} %join.2.a0), channel_id=1, source_target_pairs={{0,16},{8,24},{16,0},{24,8},{1,17},{9,25},{17,1},{25,9},{2,18},{10... | collective-permute-start | bytes 1572872 | tf_op jit(solution)/shard_map/ppermute | solution.py:334
  54.9 24.9 %collective-permute-start.9 = (bf16[4,256,256]{2,1,0:T(8,128)(2,1)S(1)}, bf16[4,256,256]{2,1,0:T(8,128)(2,1)S(1)}, u32[]{:S(2)}, u32[]{:S(2)}) collective-permute-start(bf16[4,256,256]{2,1,0:T(8,128)(2,1)S(1)} %join.2.a0), channel_id=1, source_target_pairs={{0,24},{8,0},{16,8},{24,16},{1,25},{9,1},{17,9},{25,17},{2,26},{10... | collective-permute-start | bytes 1572872 | tf_op jit(solution)/shard_map/ppermute | solution.py:334
  55.1 4.3 %collective-permute-start.10 = (bf16[272,256]{1,0:T(8,128)(2,1)S(1)}, bf16[272,256]{1,0:T(8,128)(2,1)S(1)}, u32[]{:S(2)}, u32[]{:S(2)}) collective-permute-start(bf16[272,256]{1,0:T(8,128)(2,1)S(1)} %get-tuple-element.80), channel_id=1, source_target_pairs={{0,2},{2,4},{4,6},{6,0},{1,3},{3,5},{5,7},{7,1},{8,10},{10,12},{12... | collective-permute-start | bytes 417800 | tf_op jit(solution)/shard_map/ppermute | solution.py:334
  55.9 5.9 %collective-permute-start.11 = (bf16[272,256]{1,0:T(8,128)(2,1)S(1)}, bf16[272,256]{1,0:T(8,128)(2,1)S(1)}, u32[]{:S(2)}, u32[]{:S(2)}) collective-permute-start(bf16[272,256]{1,0:T(8,128)(2,1)S(1)} %get-tuple-element.81), channel_id=1, source_target_pairs={{0,4},{2,6},{4,0},{6,2},{1,5},{3,7},{5,1},{7,3},{8,12},{10,14},{12... | collective-permute-start | bytes 417800 | tf_op jit(solution)/shard_map/ppermute | solution.py:334
  59.4 8.7 %collective-permute-start.12 = (bf16[272,256]{1,0:T(8,128)(2,1)S(1)}, bf16[272,256]{1,0:T(8,128)(2,1)S(1)}, u32[]{:S(2)}, u32[]{:S(2)}) collective-permute-start(bf16[272,256]{1,0:T(8,128)(2,1)S(1)} %get-tuple-element.82), channel_id=1, source_target_pairs={{0,6},{2,0},{4,2},{6,4},{1,7},{3,1},{5,3},{7,5},{8,14},{10,8},{12,... | collective-permute-start | bytes 417800 | tf_op jit(solution)/shard_map/ppermute | solution.py:334
  83.4 4.3 %collective-permute-start.15 = (f32[8,256,256]{2,1,0:T(8,128)S(1)}, f32[8,256,256]{2,1,0:T(8,128)S(1)}, u32[]{:S(2)}, u32[]{:S(2)}) collective-permute-start(f32[8,256,256]{2,1,0:T(8,128)S(1)} %get-tuple-element.91), channel_id=1, source_target_pairs={{0,1},{1,0},{2,3},{3,2},{4,5},{5,4},{6,7},{7,6},{8,9},{9,8},{10,11... | collective-permute-start | bytes 6291464 | tf_op jit(solution)/shard_map/ppermute | solution.py:379
  84.0 7.9 %collective-permute-start.13 = (bf16[2,256,256]{2,1,0:T(8,128)(2,1)S(1)}, bf16[2,256,256]{2,1,0:T(8,128)(2,1)S(1)}, u32[]{:S(2)}, u32[]{:S(2)}) collective-permute-start(bf16[2,256,256]{2,1,0:T(8,128)(2,1)S(1)} %get-tuple-element.88), channel_id=1, source_target_pairs={{0,8},{8,16},{16,24},{24,0},{1,9},{9,17},{17,25},{25,1},{2,10},{10... | collective-permute-start | bytes 786440 | tf_op jit(solution)/shard_map/ppermute | solution.py:334
  84.8 8.7 %collective-permute-start.14 = (bf16[2,256,256]{2,1,0:T(8,128)(2,1)S(1)}, bf16[2,256,256]{2,1,0:T(8,128)(2,1)S(1)}, u32[]{:S(2)}, u32[]{:S(2)}) collective-permute-start(bf16[2,256,256]{2,1,0:T(8,128)(2,1)S(1)} %get-tuple-element.89), channel_id=1, source_target_pairs={{0,24},{8,0},{16,8},{24,16},{1,25},{9,1},{17,9},{25,17},{2,26},{10... | collective-permute-start | bytes 786440 | tf_op jit(solution)/shard_map/ppermute | solution.py:334
  93.5 8.7 %collective-permute-start.18 = (bf16[2,256,256]{2,1,0:T(8,128)(2,1)S(1)}, bf16[2,256,256]{2,1,0:T(8,128)(2,1)S(1)}, u32[]{:S(2)}, u32[]{:S(2)}) collective-permute-start(bf16[2,256,256]{2,1,0:T(8,128)(2,1)S(1)} %get-tuple-element.101), channel_id=1, source_target_pairs={{0,64},{64,128},{128,192},{192,0},{1,65},{65,129},{129,193},{193,1... | collective-permute-start | bytes 786440 | tf_op jit(solution)/shard_map/ppermute | solution.py:334
  94.3 11.8 %collective-permute-start.19 = (bf16[2,256,256]{2,1,0:T(8,128)(2,1)S(1)}, bf16[2,256,256]{2,1,0:T(8,128)(2,1)S(1)}, u32[]{:S(2)}, u32[]{:S(2)}) collective-permute-start(bf16[2,256,256]{2,1,0:T(8,128)(2,1)S(1)} %get-tuple-element.102), channel_id=1, source_target_pairs={{0,128},{64,192},{128,0},{192,64},{1,129},{65,193},{129,1},{193,65... | collective-permute-start | bytes 786440 | tf_op jit(solution)/shard_map/ppermute | solution.py:334
  95.4 15.2 %collective-permute-start.16 = (bf16[4,256,256]{2,1,0:T(8,128)(2,1)S(1)}, bf16[4,256,256]{2,1,0:T(8,128)(2,1)S(1)}, u32[]{:S(2)}, u32[]{:S(2)}) collective-permute-start(bf16[4,256,256]{2,1,0:T(8,128)(2,1)S(1)} %get-tuple-element.98), channel_id=1, source_target_pairs={{0,8},{8,16},{16,24},{24,0},{1,9},{9,17},{17,25},{25,1},{2,10},{10... | collective-permute-start | bytes 1572872 | tf_op jit(solution)/shard_map/ppermute | solution.py:334
  95.8 14.8 %collective-permute-start.17 = (bf16[4,256,256]{2,1,0:T(8,128)(2,1)S(1)}, bf16[4,256,256]{2,1,0:T(8,128)(2,1)S(1)}, u32[]{:S(2)}, u32[]{:S(2)}) collective-permute-start(bf16[4,256,256]{2,1,0:T(8,128)(2,1)S(1)} %get-tuple-element.99), channel_id=1, source_target_pairs={{0,24},{8,0},{16,8},{24,16},{1,25},{9,1},{17,9},{25,17},{2,26},{10... | collective-permute-start | bytes 1572872 | tf_op jit(solution)/shard_map/ppermute | solution.py:334
  97.0 10.6 %collective-permute-start.20 = (bf16[2,256,256]{2,1,0:T(8,128)(2,1)S(1)}, bf16[2,256,256]{2,1,0:T(8,128)(2,1)S(1)}, u32[]{:S(2)}, u32[]{:S(2)}) collective-permute-start(bf16[2,256,256]{2,1,0:T(8,128)(2,1)S(1)} %get-tuple-element.103), channel_id=1, source_target_pairs={{0,192},{64,0},{128,64},{192,128},{1,193},{65,1},{129,65},{193,129... | collective-permute-start | bytes 786440 | tf_op jit(solution)/shard_map/ppermute | solution.py:334
  107.7 16.5 %collective-permute-start.24 = (bf16[2,256,256]{2,1,0:T(8,128)(2,1)S(1)}, bf16[2,256,256]{2,1,0:T(8,128)(2,1)S(1)}, u32[]{:S(2)}, u32[]{:S(2)}) collective-permute-start(bf16[2,256,256]{2,1,0:T(8,128)(2,1)S(1)} %total.2.refs_0_), channel_id=1, source_target_pairs={{0,32},{32,0},{1,33},{33,1},{2,34},{34,2},{3,35},{35,3},{4,36},{36... | collective-permute-start | bytes 786440 | tf_op jit(solution)/shard_map/ppermute | solution.py:386
  124.3 16.3 %collective-permute-start.25 = (bf16[2,256,256]{2,1,0:T(8,128)(2,1)S(1)}, bf16[2,256,256]{2,1,0:T(8,128)(2,1)S(1)}, u32[]{:S(2)}, u32[]{:S(2)}) collective-permute-start(bf16[2,256,256]{2,1,0:T(8,128)(2,1)S(1)} %total.3.refs_0_), channel_id=1, source_target_pairs={{0,64},{64,128},{128,192},{192,0},{1,65},{65,129},{129,193},{193,1... | collective-permute-start | bytes 786440 | tf_op jit(solution)/shard_map/ppermute | solution.py:334
  126.0 14.6 %collective-permute-start.26 = (bf16[2,256,256]{2,1,0:T(8,128)(2,1)S(1)}, bf16[2,256,256]{2,1,0:T(8,128)(2,1)S(1)}, u32[]{:S(2)}, u32[]{:S(2)}) collective-permute-start(bf16[2,256,256]{2,1,0:T(8,128)(2,1)S(1)} %total.3.refs_0_), channel_id=1, source_target_pairs={{0,192},{64,0},{128,64},{192,128},{1,193},{65,1},{129,65},{193,129... | collective-permute-start | bytes 786440 | tf_op jit(solution)/shard_map/ppermute | solution.py:334
  127.9 4.4 %collective-permute-start.21 = (bf16[256,256]{1,0:T(8,128)(2,1)S(1)}, bf16[256,256]{1,0:T(8,128)(2,1)S(1)}, u32[]{:S(2)}, u32[]{:S(2)}) collective-permute-start(bf16[256,256]{1,0:T(8,128)(2,1)S(1)} %get-tuple-element.107), channel_id=1, source_target_pairs={{0,2},{2,4},{4,6},{6,0},{1,3},{3,5},{5,7},{7,1},{8,10},{10,12},{12... | collective-permute-start | bytes 393224 | tf_op jit(solution)/shard_map/ppermute | solution.py:334
  128.2 5.1 %collective-permute-start.22 = (bf16[256,256]{1,0:T(8,128)(2,1)S(1)}, bf16[256,256]{1,0:T(8,128)(2,1)S(1)}, u32[]{:S(2)}, u32[]{:S(2)}) collective-permute-start(bf16[256,256]{1,0:T(8,128)(2,1)S(1)} %get-tuple-element.108), channel_id=1, source_target_pairs={{0,4},{2,6},{4,0},{6,2},{1,5},{3,7},{5,1},{7,3},{8,12},{10,14},{12... | collective-permute-start | bytes 393224 | tf_op jit(solution)/shard_map/ppermute | solution.py:334
  128.3 12.3 %collective-permute-start.23 = (bf16[256,256]{1,0:T(8,128)(2,1)S(1)}, bf16[256,256]{1,0:T(8,128)(2,1)S(1)}, u32[]{:S(2)}, u32[]{:S(2)}) collective-permute-start(bf16[256,256]{1,0:T(8,128)(2,1)S(1)} %get-tuple-element.109), channel_id=1, source_target_pairs={{0,6},{2,0},{4,2},{6,4},{1,7},{3,1},{5,3},{7,5},{8,14},{10,8},{12,... | collective-permute-start | bytes 393224 | tf_op jit(solution)/shard_map/ppermute | solution.py:334
  141.7 20.4 %all-to-all-start.1 = ((bf16[16,40,256]{2,1,0:T(8,128)(2,1)}), bf16[16,40,256]{2,1,0:T(8,128)(2,1)S(1)}, u32[]{:S(2)}, u32[]{:S(2)}) async-start(bf16[16,40,256]{2,1,0:T(8,128)(2,1)} %bitcast.14), calls=%async_computation.1 | async-start | bytes 655360 | tf_op jit(solution)/shard_map/all_to_all | solution.py:394
  148.0 12.6 %collective-permute-start.27 = (bf16[2,256,256]{2,1,0:T(8,128)(2,1)S(1)}, bf16[2,256,256]{2,1,0:T(8,128)(2,1)S(1)}, u32[]{:S(2)}, u32[]{:S(2)}) collective-permute-start(bf16[2,256,256]{2,1,0:T(8,128)(2,1)S(1)} %total.3.refs_0_), channel_id=1, source_target_pairs={{0,128},{64,192},{128,0},{192,64},{1,129},{65,193},{129,1},{193,65... | collective-permute-start | bytes 786440 | tf_op jit(solution)/shard_map/ppermute | solution.py:334
  162.1 3.5 %collective-permute-start.28 = (bf16[8,256,256]{2,1,0:T(8,128)(2,1)S(1)}, bf16[8,256,256]{2,1,0:T(8,128)(2,1)S(1)}, u32[]{:S(2)}, u32[]{:S(2)}) collective-permute-start(bf16[8,256,256]{2,1,0:T(8,128)(2,1)S(1)} %join.3.mine), channel_id=1, source_target_pairs={{0,1},{1,0},{2,3},{3,2},{4,5},{5,4},{6,7},{7,6},{8,9},{9,8},{10,11... | collective-permute-start | bytes 3145736 | tf_op jit(solution)/shard_map/ppermute | solution.py:398

commit v3 on v2

--- a/solution.py
+++ b/solution.py
@@ -59,21 +59,41 @@
     return (rest_down, j) if j < 2 else (near_down, j - 2)
 
 
+def heavy_piece_of(outs, k, j):
+    up, down, near_up, near_down, own = outs
+    if k == 0:
+        return own, j
+    if k == 1:
+        return (near_up, j) if j < 2 else (up, j)
+    if k == 2:
+        return (up, j) if j < 2 else (down, j - 2)
+    return (down, 2 + j) if j < 2 else (near_down, j - 2)
+
+
+def heavy_shapes(rows):
+    return [shape(4, rows, B)] * 2 + [shape(2, rows, B, dtype=F32)] * 2 + [shape(4, rows, B, dtype=F32)]
+
+
 def piece_shapes(rows):
     return [shape(2, rows, B)] * 2 + [shape(2, rows, B, dtype=F32)] * 2 + [shape(2, rows, B)] * 2 + [shape(4, rows, B, dtype=F32)]
 
 
 def project_kernel(place, hidden, gain, projector, *rest):
-    outs, scaled, blocks, sems = rest[:7], rest[7], rest[8], rest[9]
+    outs, scaled, held, blocks, sems = rest[:7], rest[7], rest[8], rest[9], rest[10]
     y, zl = place[0], place[1]
     width = blocks.shape[2]
+    first = pltpu.make_async_copy(hidden, held, sems.at[4])
+    first.start()
     copies = []
     for k in range(4):
         at = pl.ds(pl.multiple_of(((y + k) % 4) * width, width), width)
         copies.append(pltpu.make_async_copy(projector.at[:, at], blocks.at[k], sems.at[k]))
         copies[k].start()
-    wide = hidden[...].astype(F32)
-    scaled[...] = (wide * gain[...].astype(F32)).astype(BF)
+    scale = gain[...].astype(F32)
+    scale = jnp.concatenate([scale[i : i + 1, :] for i in range(scale.shape[0])], axis=1)
+    first.wait()
+    wide = held[...].astype(F32)
+    scaled[...] = (wide * scale).astype(BF)
     power = jnp.sum(wide * wide, axis=1, keepdims=True)
     power = jnp.sum(jnp.where(eye_mask(B), power, 0.0), axis=0, keepdims=True)
     for out in outs:
@@ -91,22 +111,24 @@
 def project(place, hidden, gain, projector):
     rows, depth = hidden.shape
     width = projector.shape[1] // 4
+    hbm = pl.BlockSpec(memory_space=pltpu.HBM)
     return pl.pallas_call(
         project_kernel,
-        in_specs=[SMEM, VMEM, VMEM, pl.BlockSpec(memory_space=pltpu.HBM)],
+        in_specs=[SMEM, hbm, VMEM, hbm],
         out_specs=[VMEM] * 7,
         out_shape=piece_shapes(rows + 16),
         scratch_shapes=[
             pltpu.VMEM((rows, depth), BF),
+            pltpu.VMEM((rows, depth), BF),
             pltpu.VMEM((4, depth, width), BF),
-            pltpu.SemaphoreType.DMA((4,)),
+            pltpu.SemaphoreType.DMA((5,)),
         ],
         compiler_params=pltpu.CompilerParams(vmem_limit_bytes=48 * 1024 * 1024),
         cost_estimate=pl.CostEstimate(
             flops=2 * rows * depth * 4 * width, bytes_accessed=2 * depth * 4 * width, transcendentals=0
         ),
         name="project",
-    )(place, hidden, gain.reshape(1, depth), projector)
+    )(place, hidden, gain.reshape(depth // 128, 128), projector)
 
 
 def put_sum(out, at, terms):
@@ -145,6 +167,40 @@
     )(*parts)
 
 
+def heavy_relay_kernel(near_up, near_down, got_up, got_down, up, down):
+    for i in range(2):
+        put_sum(up, i, [near_up.at[i], got_up.at[i]])
+        put_sum(down, i, [near_down.at[i], got_down.at[i]])
+
+
+def heavy_relay(*parts):
+    return pl.pallas_call(
+        heavy_relay_kernel,
+        in_specs=[VMEM] * 4,
+        out_specs=[VMEM] * 2,
+        out_shape=[shape(2, B, B)] * 2,
+        compiler_params=PARAMS,
+        name="heavy_relay",
+    )(*parts)
+
+
+def heavy_fold_kernel(own, got_up, got_down, far_up, far_down, *outs):
+    for j, out in enumerate(outs):
+        got, far = (got_down.at[2 + j], far_up.at[j]) if j < 2 else (got_up.at[j], far_down.at[j - 2])
+        put_sum(out, None, [own.at[j], got, far])
+
+
+def heavy_fold(*parts):
+    return pl.pallas_call(
+        heavy_fold_kernel,
+        in_specs=[VMEM] * 5,
+        out_specs=[VMEM] * 4,
+        out_shape=[shape(B, B, dtype=F32)] + [shape(B, B)] * 3,
+        compiler_params=PARAMS,
+        name="heavy_fold",
+    )(*parts)
+
+
 def fold_kernel(own, far_up, far_down, *outs):
     for j, out in enumerate(outs):
         put_sum(out, None, [own.at[j], far_up.at[j], far_down.at[j]])
@@ -162,15 +218,17 @@
     )(*parts)
 
 
-def middle_kernel(place, a0, a1, a2, a3, weight, resid, t0, t1, t2, t3, *outs):
-    pieces, keep, send = outs[:7], outs[7], outs[8]
+def middle_kernel(place, a0, a1, a2, a3, weight, at, resid, t0, t1, t2, t3, *outs):
+    pieces, keep, send = outs[:5], outs[5], outs[6]
     y, zl, core = place[0], place[1], place[2]
     attn = (a0, a1, a2, a3)
     parts = (t0, t1, t2, t3)
     total = sum(r[:B, :].astype(F32) for r in parts)
     power = jnp.sum(sum(r[B:, :].astype(F32) for r in parts), axis=0, keepdims=True)
     power = jnp.sum(jnp.where(eye_mask(B), power, 0.0), axis=1, keepdims=True)
-    value = resid[...].astype(F32) - total * lax.rsqrt(power / DT + EPS)
+    rows = lax.broadcasted_iota(jnp.int32, (B, resid.shape[0]), 0)
+    select = jnp.where(rows == at[...], 1.0, 0.0).astype(BF)
+    value = jnp.dot(select, resid[...], preferred_element_type=F32) - total * lax.rsqrt(power / DT + EPS)
     for k in range(4):
         for j in range(4):
             w = weight[((y + 4 - k) % 4) * 4 + (zl + 4 - j) % 4]
@@ -178,7 +236,7 @@
     residual = value.astype(BF)
     for k in range(4):
         for j in range(4):
-            out, i = piece_of(pieces, k, j)
+            out, i = heavy_piece_of(pieces, k, j)
             w = weight[((y + k) % 4) * 4 + (zl + j) % 4]
             out[i] = lax.dot_general(
                 residual, w, (((1,), (1,)), ((), ())), preferred_element_type=F32
@@ -194,49 +252,32 @@
                 ).astype(out.dtype)
 
 
-def middle(place, chunks, weight, resid, parts):
+def middle(place, chunks, weight, at, resid, parts):
     return pl.pallas_call(
         middle_kernel,
-        in_specs=[SMEM] + [VMEM] * 10,
-        out_specs=[VMEM] * 9,
-        out_shape=piece_shapes(B) + [shape(8, B, B, dtype=F32)] * 2,
+        in_specs=[SMEM] + [VMEM] * 11,
+        out_specs=[VMEM] * 7,
+        out_shape=heavy_shapes(B) + [shape(8, B, B, dtype=F32)] * 2,
         compiler_params=PARAMS,
         name="middle",
-    )(place, *chunks, weight, resid, *parts)
-
-
-def pair_kernel(a, b, out):
-    out[:, :B] = a[...]
-    out[:, B:] = b[...]
-
-
-def pair(a, b):
-    return pl.pallas_call(
-        pair_kernel,
+    )(place, *chunks, weight, at.reshape(1, -1), resid.reshape(-1, B), *parts)
+
+
+def pick_kernel(at, slots, out):
+    rows = lax.broadcasted_iota(jnp.int32, (B, slots.shape[0]), 0)
+    select = jnp.where(rows == at[...], 1.0, 0.0).astype(BF)
+    out[...] = jnp.dot(select, slots[...], preferred_element_type=F32).astype(BF)
+
+
+def pick(at, slots):
+    return pl.pallas_call(
+        pick_kernel,
         in_specs=[VMEM] * 2,
         out_specs=VMEM,
-        out_shape=shape(a.shape[0], 2 * B),
-        compiler_params=PARAMS,
-        name="pair",
-    )(a, b)
-
-
-def pick_kernel(at, slots, first, second):
-    rows = lax.broadcasted_iota(jnp.int32, (B, slots.shape[0]), 0)
-    select = jnp.where(rows == at[...], 1.0, 0.0).astype(BF)
-    first[...] = jnp.dot(select, slots[:, :B], preferred_element_type=F32).astype(BF)
-    second[...] = jnp.dot(select, slots[:, B:], preferred_element_type=F32).astype(BF)
-
-
-def pick(at, slots):
-    return pl.pallas_call(
-        pick_kernel,
-        in_specs=[VMEM] * 2,
-        out_specs=[VMEM] * 2,
-        out_shape=[shape(B, B)] * 2,
+        out_shape=shape(B, B),
         compiler_params=PARAMS,
         name="pick",
-    )(at.reshape(1, -1), slots.reshape(-1, 2 * B))
+    )(at.reshape(1, -1), slots.reshape(-1, B))
 
 
 def put_kernel(at, a, b, c, d, out):
@@ -310,24 +351,31 @@
     )(*parts)
 
 
-def assemble_kernel(place, mine, twin, out):
+def assemble_kernel(place, *refs):
+    mine, twin, out, sems = refs[:4], refs[4:8], refs[8], refs[9]
     y, zl, core, x = place[0], place[1], place[2], place[3]
+    copies = []
     for s in range(8):
         within = ((x + 4 - s // 2) % 4) * 2 + s % 2
         for source, half in ((mine, core), (twin, 1 - core)):
             m = half * 8 + within
-            out[((y + 4 - m // 4) % 4) * 4 + (zl + 4 - m % 4) % 4] = source[s]
+            to = out.at[((y + 4 - m // 4) % 4) * 4 + (zl + 4 - m % 4) % 4]
+            copies.append(pltpu.make_async_copy(source[s // 2].at[s % 2], to, sems.at[len(copies)]))
+            copies[-1].start()
+    for copy in copies:
+        copy.wait()
 
 
 def assemble(place, mine, twin):
     return pl.pallas_call(
         assemble_kernel,
-        in_specs=[SMEM, VMEM, VMEM],
-        out_specs=VMEM,
+        in_specs=[SMEM] + [VMEM] * 8,
+        out_specs=pl.BlockSpec(memory_space=pltpu.HBM),
         out_shape=shape(16, B, B),
+        scratch_shapes=[pltpu.SemaphoreType.DMA((16,))],
         compiler_params=PARAMS,
         name="assemble",
-    )(place, mine, twin)
+    )(place, *mine, *twin)
 
 
 def send_on(piece, axis, k):
@@ -357,47 +405,48 @@
     position = jnp.arange(slot, dtype=jnp.int32)
     where = jnp.where(position[None, :] < length[:, None], offset[:, None] + position[None, :], -1)
 
-    both = pair(attn, resid).reshape(groups, slot, 2 * B)
-    slots = lax.all_to_all(both, GROUP, 0, 0, tiled=True)
+    slots = lax.all_to_all(attn.reshape(groups, slot, B), GROUP, 0, 0, tiled=True)
     teacher = project(place, hidden, gain, projector)
     got = relay_first(teacher)
-    attn_rows, resid_rows = pick(where, slots)
-    got, attn_rows = tie(got, attn_rows)
+    attn_rows = pick(where, slots)
+    got, _ = tie(got, attn_rows)
     along_zl = [attn_rows] + [send_on(attn_rows, "zl", j) for j in (1, 2, 3)]
-    far = relay_second(teacher, got)
+    up, down = relay(*teacher[2:6], *got)
+    far = send_on(up, "y", 1), send_on(down, "y", 3)
+    resid, _ = tie(resid, up)
+    resid_slots = lax.all_to_all(resid.reshape(groups, slot, B), GROUP, 0, 0, tiled=True)
 
     chunk = join(*(p[None] for p in along_zl))
-    far, chunk = tie(far, chunk)
+    far, _ = tie(far, chunk)
     chunks = [chunk] + [send_on(chunk, "y", k) for k in (1, 2, 3)]
     folded = fold(teacher[6], *far)
     parts = [folded[0]] + [send_on(folded[j], "zl", j) for j in (1, 2, 3)]
 
-    outs = middle(place, chunks, weight.reshape(16, B, B), resid_rows, parts)
-    grads, keep, send = outs[:7], outs[7], outs[8]
+    outs = middle(place, chunks, weight.reshape(16, B, B), where, resid_slots, parts)
+    grads, keep, send = outs[:5], outs[5], outs[6]
 
     got = relay_first(grads)
     other = lax.ppermute(send, "core", SWAP)
     pieces = share(place, keep, other)
-    got, pieces = tie(got, pieces)
+    got, _ = tie(got, pieces)
     pieces = [pieces[0]] + [send_on(pieces[k], "x", k) for k in (1, 2, 3)]
-    far = relay_second(grads, got)
+    up, down = heavy_relay(grads[2], grads[3], *got)
+    far = send_on(up, "y", 1), send_on(down, "y", 3)
 
     near = total(pieces)
     away = lax.ppermute(near, "zh", SWAP)
     far, near = tie(far, near)
-    folded = fold(grads[6], *far)
+    folded = heavy_fold(grads[4], *got, *far)
     grad_parts = [folded[0]] + [send_on(folded[j], "zl", j) for j in (1, 2, 3)]
     done = total([near, away], 1.0 / (groups * rows))
-    after, before = send_on(done, "x", 1), send_on(done, "x", 3)
-    grad_parts, after, before = tie(grad_parts, after, before)
+    grad_parts, _ = tie(grad_parts, done)
     slots = put(where, grad_parts)
     slots = lax.all_to_all(slots.reshape(groups, slot, B), GROUP, 0, 0, tiled=True)
-    mine = [done, after, send_on(done, "x", 2), before]
-    slots, mine = tie(slots, mine)
-    mine = join(*mine)
-    twin = lax.ppermute(mine, "core", SWAP)
+    mine = [done] + [send_on(done, "x", k) for k in (1, 2, 3)]
+    twin = [lax.ppermute(p, "core", SWAP) for p in mine]
     weight_grad = assemble(place, mine, twin).reshape(weight.shape)
     return slots.reshape(attn.shape), weight_grad
+
 
 def solution(mesh):
     fine = Mesh(mesh.devices.reshape(4, 2, 4, 4, 2), ("x", "zh", "y", "zl", "core"))

time: 169 us -> 161 us (0.953)
  waiting for transfers between devices: 99.9 us -> 77.1 us
  starting transfers between devices: 45.2 us -> 57.6 us
    ppermute x26, waiting for transfers between devices: 67.5 us -> 43.9 us  [send_on(): return lax.ppermute(piece, axis, ring(k))]
    all_to_all x1 -> x2, starting transfers between devices: 10.7 us -> 19.9 us  [the longest x1 10.7 us: body(): lax.all_to_all(attn.reshape(groups, slot, B), GROUP, 0, 0, tiled=True)]
    ppermute x1, starting transfers between devices: 2.92 us -> 5.17 us  [body(): away = lax.ppermute(near, 'zh', SWAP)]
    all_to_all x1 -> x2, waiting for transfers between devices: 12.8 us -> 15.1 us  [the longest x1 9.84 us: body(): lax.all_to_all(resid.reshape(groups, slot, B), GROUP, 0, 0, tiled=True)]
    ppermute x1 -> x4, starting transfers between devices: 1.25 us -> 3.11 us  [body(): twin = [lax.ppermute(p, 'core', SWAP) for p in mine]]
    pallas_call x5 -> x6, Pallas kernels: 13 us -> 12.2 us  [the longest x1 5.11 us: project(): pl.pallas_call(project_kernel, in_specs=[SMEM, hbm, VMEM, hbm], out_specs...]
    unnamed x23 -> x19, local copies, waits for them, and re-layouts: 6.09 us -> 6.35 us
  transfers between devices with their start and end apart: 31 -> 35, of which waited for: 23 -> 17; matrix products, arithmetic and copies ran while one was open for 0% -> 0% of each run, Pallas kernels for 5% -> 7%
where the time goes in v3:
time: 161 us; the launch traced here: 160 us
  waiting for transfers between devices  77.1 us (48%)
  starting transfers between devices  57.6 us (36%)
  Pallas kernels  17.2 us (11%)
  local copies, waits for them, and re-layouts  6.6 us (4%)
    ppermute x26, waiting for transfers between devices, send_on(): return lax.ppermute(piece, axis, ring(k))  43.9 us
    ppermute x26, starting transfers between devices, send_on(): return lax.ppermute(piece, axis, ring(k))  23.9 us
    ppermute x1, waiting for transfers between devices, body(): away = lax.ppermute(near, 'zh', SWAP)  14.3 us
    all_to_all x1, starting transfers between devices, body(): lax.all_to_all(attn.reshape(groups, slot, B), GROUP, 0, 0, tiled=True)  10.7 us
    all_to_all x1, waiting for transfers between devices, body(): lax.all_to_all(resid.reshape(groups, slot, B), GROUP, 0, 0, tiled=True)  9.84 us
    all_to_all x1, starting transfers between devices, body(): lax.all_to_all(resid.reshape(groups, slot, B), GROUP, 0, 0, tiled=True)  9.22 us
    unnamed x19, local copies, waits for them, and re-layouts  6.35 us
    all_to_all x1, waiting for transfers between devices, body(): lax.all_to_all(attn.reshape(groups, slot, B), GROUP, 0, 0, tiled=True)  5.23 us
  transfers between devices with their start and end apart: 35, of which 17 were waited for; matrix products, arithmetic and copies ran while one was open for 0% of the time, Pallas kernels for 7%

profile of v3, /device:TPU:57, one launch (start us, length us, event | category | flops | bytes accessed | tf_op | source)
XLA Modules:
  0.0 159.7 jit_solution(3704674552715026177)
XLA Ops:
  0.6 10.7 %all-to-all-start = ((bf16[16,40,256]{2,1,0:T(8,128)(2,1)}), bf16[16,40,256]{2,1,0:T(8,128)(2,1)S(1)}, u32[]{:S(2)}, u32[]{:S(2)}) async-start(bf16[16,40,256]{2,1,0:T(8,128)(2,1)} %bitcast.33), calls=%async_computation | async-start | bytes 655360 | tf_op jit(solution)/shard_map/all_to_all | solution.py:408
  11.4 1.0 copy-done.4
  13.2 5.1 %project.1 = (bf16[2,272,256]{2,1,0:T(8,128)(2,1)S(1)}, bf16[2,272,256]{2,1,0:T(8,128)(2,1)S(1)}, f32[2,272,256]{2,1,0:T(8,128)S(1)}, f32[2,272,256]{2,1,0:T(8,1...) custom-call(s32[4]{0:T(128)S(1)} %pad_add_fusion.place, ...), custom_call_target="tpu_custom_call" | custom-call | flops 2147483648 | bytes 8388608 | tf_op jit(solution)/shard_map/project/pallas_call | solution.py:115
  18.3 1.0 copy-done.2
  19.3 1.5 collective-permute-start.7
  21.2 5.2 %all-to-all-done = bf16[16,40,256]{2,1,0:T(8,128)(2,1)S(1)} async-done(((bf16[16,40,256]{2,1,0:T(8,128)(2,1)}), bf16[16,40,256]{2,1,0:T(8,128)(2,1)S(1)}, u32[]{:S(2)}, u32[]{:S(2)}) %all-to-all-start) | async-done | bytes 327712 | tf_op jit(solution)/shard_map/all_to_all | solution.py:408
  26.8 0.8 collective-permute-start
  27.6 1.3 collective-permute-start.2
  28.9 1.1 relay.1
  30.0 1.5 collective-permute-start.9
  31.5 6.0 %collective-permute-done.1 = bf16[256,256]{1,0:T(8,128)(2,1)S(1)} collective-permute-done((bf16[256,256]{1,0:T(8,128)(2,1)S(1)}, bf16[256,256]{1,0:T(8,128)(2,1)S(1)}, u32[]{:S(2)}, u32[]{:S(2)}) %collective-permute-start.1) | collective-permute-done | bytes 131104 | tf_op jit(solution)/shard_map/ppermute | solution.py:382
  37.5 1.2 collective-permute-done.2
  38.8 9.2 %all-to-all-start.1 = ((bf16[16,40,256]{2,1,0:T(8,128)(2,1)}), bf16[16,40,256]{2,1,0:T(8,128)(2,1)S(1)}, u32[]{:S(2)}, u32[]{:S(2)}) async-start(bf16[16,40,256]{2,1,0:T(8,128)(2,1)} %bitcast.34), calls=%async_computation.1 | async-start | bytes 655360 | tf_op jit(solution)/shard_map/all_to_all | solution.py:417
  48.0 1.0 collective-permute-start.4
  49.1 1.2 copy-done.3
  50.3 1.9 %fold.1 = (f32[272,256]{1,0:T(8,128)S(1)}, bf16[272,256]{1,0:T(8,128)(2,1)}, bf16[272,256]{1,0:T(8,128)(2,1)}, bf16[272,256]{1,0:T(8,128)(2,1)}) custom-call(f32[4,272,256]{2,1,0:T(8,128)S(1)} %copy-done.3, bf16[4,272,256]{2,1,0:T(8,128)(2,1)S(1)} %collective-permute-done.8.far_up, bf16[4,272,256]{2,1,0:T(8,128)(2,1)} %collective-permute-done.9.far_down), custom_call_target="tpu_custom_call" | custom-call | tf_op jit(solution)/shard_map/fold/pallas_call | solution.py:211
  53.9 2.0 %collective-permute-start.12 = (bf16[272,256]{1,0:T(8,128)(2,1)}, bf16[272,256]{1,0:T(8,128)(2,1)S(1)}, u32[]{:S(2)}, u32[]{:S(2)}) collective-permute-start(bf16[272,256]{1,0:T(8,128)(2,1)} %get-tuple-element.63), channel_id=1, source_target_pairs={{0,6},{2,0},{4,2},{6,4},{1,7},{3,1},{5,3},{7,5},{8,14},{10,8},{12,... | collective-permute-start | bytes 417800 | tf_op jit(solution)/shard_map/ppermute | solution.py:382
  55.9 9.8 %all-to-all-done.1 = bf16[16,40,256]{2,1,0:T(8,128)(2,1)S(1)} async-done(((bf16[16,40,256]{2,1,0:T(8,128)(2,1)}), bf16[16,40,256]{2,1,0:T(8,128)(2,1)S(1)}, u32[]{:S(2)}, u32[]{:S(2)}) %all-to-all-start.1) | async-done | bytes 327712 | tf_op jit(solution)/shard_map/all_to_all | solution.py:417
  65.8 8.9 %collective-permute-done.5.a3 = bf16[4,256,256]{2,1,0:T(8,128)(2,1)} collective-permute-done((bf16[4,256,256]{2,1,0:T(8,128)(2,1)S(1)}, bf16[4,256,256]{2,1,0:T(8,128)(2,1)}, u32[]{:S(2)}, u32[]{:S(2)}) %collective-permute-start.5) | collective-permute-done | bytes 524320 | tf_op jit(solution)/shard_map/ppermute | solution.py:382
  74.7 0.9 copy-done.6
  75.7 4.5 %middle.1 = (bf16[4,256,256]{2,1,0:T(8,128)(2,1)S(1)}, bf16[4,256,256]{2,1,0:T(8,128)(2,1)S(1)}, f32[2,256,256]{2,1,0:T(8,128)S(1)}, f32[2,256,256]{2,1,0:T(8,12...) custom-call(s32[4]{0:T(128)S(1)} %pad_add_fusion.place, ...), custom_call_target="tpu_custom_call" | custom-call | tf_op jit(solution)/shard_map/middle/pallas_call | solution.py:256
  81.1 1.1 collective-permute-start.14
  82.2 2.3 %collective-permute-done.15.other = f32[8,256,256]{2,1,0:T(8,128)S(1)} collective-permute-done((f32[8,256,256]{2,1,0:T(8,128)S(1)}, f32[8,256,256]{2,1,0:T(8,128)S(1)}, u32[]{:S(2)}, u32[]{:S(2)}) %collective-permute-start.15) | collective-permute-done | bytes 2097184 | tf_op jit(solution)/shard_map/ppermute | solution.py:429
  84.5 0.7 share.1
  85.3 1.5 collective-permute-start.18
  86.8 2.4 %collective-permute-start.19 = (bf16[2,256,256]{2,1,0:T(8,128)(2,1)S(1)}, bf16[2,256,256]{2,1,0:T(8,128)(2,1)S(1)}, u32[]{:S(2)}, u32[]{:S(2)}) collective-permute-start(bf16[2,256,256]{2,1,0:T(8,128)(2,1)S(1)} %get-tuple-element.71), channel_id=1, source_target_pairs={{0,128},{64,192},{128,0},{192,64},{1,129},{65,193},{129,1},{193,65... | collective-permute-start | bytes 786440 | tf_op jit(solution)/shard_map/ppermute | solution.py:382
  89.2 1.2 collective-permute-start.20
  90.3 3.9 %collective-permute-done.13.got_up = bf16[4,256,256]{2,1,0:T(8,128)(2,1)S(1)} collective-permute-done((bf16[4,256,256]{2,1,0:T(8,128)(2,1)S(1)}, bf16[4,256,256]{2,1,0:T(8,128)(2,1)S(1)}, u32[]{:S(2)}, u32[]{:S(2)}) %collective-permute-start.13) | collective-permute-done | bytes 524320 | tf_op jit(solution)/shard_map/ppermute | solution.py:382
  94.2 1.2 collective-permute-done.14.got_down
  96.0 1.1 collective-permute-start.17
  97.1 3.7 %collective-permute-done.19.refs_2_ = bf16[2,256,256]{2,1,0:T(8,128)(2,1)S(1)} collective-permute-done((bf16[2,256,256]{2,1,0:T(8,128)(2,1)S(1)}, bf16[2,256,256]{2,1,0:T(8,128)(2,1)S(1)}, u32[]{:S(2)}, u32[]{:S(2)}) %collective-permute-start.19) | collective-permute-done | bytes 262176 | tf_op jit(solution)/shard_map/ppermute | solution.py:382
  101.0 5.2 %collective-permute-start.24 = (bf16[2,256,256]{2,1,0:T(8,128)(2,1)S(1)}, bf16[2,256,256]{2,1,0:T(8,128)(2,1)S(1)}, u32[]{:S(2)}, u32[]{:S(2)}) collective-permute-start(bf16[2,256,256]{2,1,0:T(8,128)(2,1)S(1)} %total.2.refs_0_), channel_id=1, source_target_pairs={{0,32},{32,0},{1,33},{33,1},{2,34},{34,2},{3,35},{35,3},{4,36},{36... | collective-permute-start | bytes 786440 | tf_op jit(solution)/shard_map/ppermute | solution.py:437
  107.1 1.2 collective-permute-start.23
  108.4 14.3 %collective-permute-done.24.refs_1_ = bf16[2,256,256]{2,1,0:T(8,128)(2,1)S(1)} collective-permute-done((bf16[2,256,256]{2,1,0:T(8,128)(2,1)S(1)}, bf16[2,256,256]{2,1,0:T(8,128)(2,1)S(1)}, u32[]{:S(2)}, u32[]{:S(2)}) %collective-permute-start.24) | collective-permute-done | bytes 262176 | tf_op jit(solution)/shard_map/ppermute | solution.py:437
  122.9 4.2 %collective-permute-done.22.c = bf16[256,256]{1,0:T(8,128)(2,1)S(1)} collective-permute-done((bf16[256,256]{1,0:T(8,128)(2,1)S(1)}, bf16[256,256]{1,0:T(8,128)(2,1)S(1)}, u32[]{:S(2)}, u32[]{:S(2)}) %collective-permute-start.22) | collective-permute-done | bytes 131104 | tf_op jit(solution)/shard_map/ppermute | solution.py:382
  127.1 2.9 %collective-permute-done.23.d = bf16[256,256]{1,0:T(8,128)(2,1)S(1)} collective-permute-done((bf16[256,256]{1,0:T(8,128)(2,1)S(1)}, bf16[256,256]{1,0:T(8,128)(2,1)S(1)}, u32[]{:S(2)}, u32[]{:S(2)}) %collective-permute-start.23) | collective-permute-done | bytes 131104 | tf_op jit(solution)/shard_map/ppermute | solution.py:382
  130.0 1.0 put.1
  131.1 4.9 %all-to-all-start.2 = ((bf16[16,40,256]{2,1,0:T(8,128)(2,1)}), bf16[16,40,256]{2,1,0:T(8,128)(2,1)S(1)}, u32[]{:S(2)}, u32[]{:S(2)}) async-start(bf16[16,40,256]{2,1,0:T(8,128)(2,1)} %bitcast.17), calls=%async_computation.2 | async-start | bytes 655360 | tf_op jit(solution)/shard_map/all_to_all | solution.py:444
  135.9 1.4 collective-permute-start.25
  137.3 2.4 %collective-permute-start.26 = (bf16[2,256,256]{2,1,0:T(8,128)(2,1)S(1)}, bf16[2,256,256]{2,1,0:T(8,128)(2,1)S(1)}, u32[]{:S(2)}, u32[]{:S(2)}) collective-permute-start(bf16[2,256,256]{2,1,0:T(8,128)(2,1)S(1)} %total.3.refs_0_), channel_id=1, source_target_pairs={{0,128},{64,192},{128,0},{192,64},{1,129},{65,193},{129,1},{193,65... | collective-permute-start | bytes 786440 | tf_op jit(solution)/shard_map/ppermute | solution.py:382
  139.7 1.2 collective-permute-start.27
  140.9 1.2 collective-permute-start.28
  142.1 4.9 %collective-permute-done.25.refs_1_ = bf16[2,256,256]{2,1,0:T(8,128)(2,1)S(1)} collective-permute-done((bf16[2,256,256]{2,1,0:T(8,128)(2,1)S(1)}, bf16[2,256,256]{2,1,0:T(8,128)(2,1)S(1)}, u32[]{:S(2)}, u32[]{:S(2)}) %collective-permute-start.25) | collective-permute-done | bytes 262176 | tf_op jit(solution)/shard_map/ppermute | solution.py:382
  147.0 1.0 collective-permute-start.29
  148.0 6.5 %collective-permute-done.26.refs_2_ = bf16[2,256,256]{2,1,0:T(8,128)(2,1)S(1)} collective-permute-done((bf16[2,256,256]{2,1,0:T(8,128)(2,1)S(1)}, bf16[2,256,256]{2,1,0:T(8,128)(2,1)S(1)}, u32[]{:S(2)}, u32[]{:S(2)}) %collective-permute-start.26) | collective-permute-done | bytes 262176 | tf_op jit(solution)/shard_map/ppermute | solution.py:382
  154.5 0.9 collective-permute-start.30
  155.4 1.1 collective-permute-done.30.refs_6_
  156.9 2.0 %assemble.1 = bf16[16,256,256]{2,1,0:T(8,128)(2,1)} custom-call(s32[4]{0:T(128)S(1)} %pad_add_fusion.place, bf16[2,256,256]{2,1,0:T(8,128)(2,1)S(1)} %total.3.refs_0_, bf16[2,256,256]{2,1,0:T(8,128)(2,1)S(1)} %collective-permute-done.25.refs_1_, bf16[2,256,256]{2,1,0:T(8,128)(2,1)S(1)} %collective-permute-done.26.refs_2_, ...), custom_call_target="tpu_custom_call" | custom-call | tf_op jit(solution)/shard_map/assemble/pallas_call | solution.py:370
  (62 shorter events, 7.2 us)
Async XLA Ops:
  0.6 20.3 %copy-start = (s32[16,16]{1,0:T(8,128)S(1)}, s32[16,16]{1,0:T(8,128)}, u32[]{:S(2)}) copy-start(s32[16,16]{1,0:T(8,128)} %param.12) | copy-start | bytes 3076
  0.6 25.8 %all-to-all-start = ((bf16[16,40,256]{2,1,0:T(8,128)(2,1)}), bf16[16,40,256]{2,1,0:T(8,128)(2,1)S(1)}, u32[]{:S(2)}, u32[]{:S(2)}) async-start(bf16[16,40,256]{2,1,0:T(8,128)(2,1)} %bitcast.33), calls=%async_computation | async-start | bytes 655360 | tf_op jit(solution)/shard_map/all_to_all | solution.py:408
  11.4 1.0 copy-start.4
  12.5 0.7 copy-start.7
  13.2 7.6 %copy-start.8 = (s32[16,16]{1,0:T(8,128)S(1)}, s32[16,16]{1,0:T(8,128)}, u32[]{:S(2)}) copy-start(s32[16,16]{1,0:T(8,128)} %param.11) | copy-start | bytes 3076
  18.3 1.0 copy-start.2
  19.3 9.6 %collective-permute-start.6 = (bf16[2,272,256]{2,1,0:T(8,128)(2,1)S(1)}, bf16[2,272,256]{2,1,0:T(8,128)(2,1)S(1)}, u32[]{:S(2)}, u32[]{:S(2)}) collective-permute-start(bf16[2,272,256]{2,1,0:T(8,128)(2,1)S(1)} %get-tuple-element.50), channel_id=1, source_target_pairs={{0,8},{8,16},{16,24},{24,0},{1,9},{9,17},{17,25},{25,1},{2,10},{10... | collective-permute-start | bytes 835592 | tf_op jit(solution)/shard_map/ppermute | solution.py:382
  19.3 9.6 %collective-permute-start.7 = (bf16[2,272,256]{2,1,0:T(8,128)(2,1)S(1)}, bf16[2,272,256]{2,1,0:T(8,128)(2,1)S(1)}, u32[]{:S(2)}, u32[]{:S(2)}) collective-permute-start(bf16[2,272,256]{2,1,0:T(8,128)(2,1)S(1)} %get-tuple-element.51), channel_id=1, source_target_pairs={{0,24},{8,0},{16,8},{24,16},{1,25},{9,1},{17,9},{25,17},{2,26},{10... | collective-permute-start | bytes 835592 | tf_op jit(solution)/shard_map/ppermute | solution.py:382
  26.8 4.7 %collective-permute-start = (bf16[256,256]{1,0:T(8,128)(2,1)S(1)}, bf16[256,256]{1,0:T(8,128)(2,1)S(1)}, u32[]{:S(2)}, u32[]{:S(2)}) collective-permute-start(bf16[256,256]{1,0:T(8,128)(2,1)S(1)} %pick.1), channel_id=1, source_target_pairs={{0,2},{2,4},{4,6},{6,0},{1,3},{3,5},{5,7},{7,1},{8,10},{10,12},{12... | collective-permute-start | bytes 393224 | tf_op jit(solution)/shard_map/ppermute | solution.py:382
  27.6 9.9 %collective-permute-start.1 = (bf16[256,256]{1,0:T(8,128)(2,1)S(1)}, bf16[256,256]{1,0:T(8,128)(2,1)S(1)}, u32[]{:S(2)}, u32[]{:S(2)}) collective-permute-start(bf16[256,256]{1,0:T(8,128)(2,1)S(1)} %pick.1), channel_id=1, source_target_pairs={{0,4},{2,6},{4,0},{6,2},{1,5},{3,7},{5,1},{7,3},{8,12},{10,14},{12... | collective-permute-start | bytes 393224 | tf_op jit(solution)/shard_map/ppermute | solution.py:382
  27.6 11.1 %collective-permute-start.2 = (bf16[256,256]{1,0:T(8,128)(2,1)S(1)}, bf16[256,256]{1,0:T(8,128)(2,1)S(1)}, u32[]{:S(2)}, u32[]{:S(2)}) collective-permute-start(bf16[256,256]{1,0:T(8,128)(2,1)S(1)} %pick.1), channel_id=1, source_target_pairs={{0,6},{2,0},{4,2},{6,4},{1,7},{3,1},{5,3},{7,5},{8,14},{10,8},{12,... | collective-permute-start | bytes 393224 | tf_op jit(solution)/shard_map/ppermute | solution.py:382
  30.0 44.7 %copy-start.1 = (bf16[4096,256]{1,0:T(8,128)(2,1)S(1)}, bf16[4096,256]{1,0:T(8,128)(2,1)}, u32[]{:S(2)}) copy-start(bf16[4096,256]{1,0:T(8,128)(2,1)} %param.15) | copy-start | bytes 6291460
  30.0 19.0 %collective-permute-start.8 = (bf16[4,272,256]{2,1,0:T(8,128)(2,1)}, bf16[4,272,256]{2,1,0:T(8,128)(2,1)S(1)}, u32[]{:S(2)}, u32[]{:S(2)}) collective-permute-start(bf16[4,272,256]{2,1,0:T(8,128)(2,1)} %get-tuple-element.54), channel_id=1, source_target_pairs={{0,8},{8,16},{16,24},{24,0},{1,9},{9,17},{17,25},{25,1},{2,10},{10... | collective-permute-start | bytes 1671176 | tf_op jit(solution)/shard_map/ppermute | solution.py:382
  30.0 19.0 %collective-permute-start.9 = (bf16[4,272,256]{2,1,0:T(8,128)(2,1)}, bf16[4,272,256]{2,1,0:T(8,128)(2,1)}, u32[]{:S(2)}, u32[]{:S(2)}) collective-permute-start(bf16[4,272,256]{2,1,0:T(8,128)(2,1)} %get-tuple-element.57), channel_id=1, source_target_pairs={{0,24},{8,0},{16,8},{24,16},{1,25},{9,1},{17,9},{25,17},{2,26},{10... | collective-permute-start | bytes 1671176 | tf_op jit(solution)/shard_map/ppermute | solution.py:382
  38.7 15.3 %collective-permute-start.3 = (bf16[4,256,256]{2,1,0:T(8,128)(2,1)S(1)}, bf16[4,256,256]{2,1,0:T(8,128)(2,1)}, u32[]{:S(2)}, u32[]{:S(2)}) collective-permute-start(bf16[4,256,256]{2,1,0:T(8,128)(2,1)S(1)} %join.1.a0), channel_id=1, source_target_pairs={{0,8},{8,16},{16,24},{24,0},{1,9},{9,17},{17,25},{25,1},{2,10},{10... | collective-permute-start | bytes 1572872 | tf_op jit(solution)/shard_map/ppermute | solution.py:382
  38.8 27.0 %all-to-all-start.1 = ((bf16[16,40,256]{2,1,0:T(8,128)(2,1)}), bf16[16,40,256]{2,1,0:T(8,128)(2,1)S(1)}, u32[]{:S(2)}, u32[]{:S(2)}) async-start(bf16[16,40,256]{2,1,0:T(8,128)(2,1)} %bitcast.34), calls=%async_computation.1 | async-start | bytes 655360 | tf_op jit(solution)/shard_map/all_to_all | solution.py:417
  48.0 17.8 %collective-permute-start.4 = (bf16[4,256,256]{2,1,0:T(8,128)(2,1)S(1)}, bf16[4,256,256]{2,1,0:T(8,128)(2,1)}, u32[]{:S(2)}, u32[]{:S(2)}) collective-permute-start(bf16[4,256,256]{2,1,0:T(8,128)(2,1)S(1)} %join.1.a0), channel_id=1, source_target_pairs={{0,16},{8,24},{16,0},{24,8},{1,17},{9,25},{17,1},{25,9},{2,18},{10... | collective-permute-start | bytes 1572872 | tf_op jit(solution)/shard_map/ppermute | solution.py:382
  49.0 25.7 %collective-permute-start.5 = (bf16[4,256,256]{2,1,0:T(8,128)(2,1)S(1)}, bf16[4,256,256]{2,1,0:T(8,128)(2,1)}, u32[]{:S(2)}, u32[]{:S(2)}) collective-permute-start(bf16[4,256,256]{2,1,0:T(8,128)(2,1)S(1)} %join.1.a0), channel_id=1, source_target_pairs={{0,24},{8,0},{16,8},{24,16},{1,25},{9,1},{17,9},{25,17},{2,26},{10... | collective-permute-start | bytes 1572872 | tf_op jit(solution)/shard_map/ppermute | solution.py:382
  49.1 1.3 copy-start.3
  52.2 0.7 copy-start.5
  52.9 21.8 %collective-permute-start.10 = (bf16[272,256]{1,0:T(8,128)(2,1)}, bf16[272,256]{1,0:T(8,128)(2,1)S(1)}, u32[]{:S(2)}, u32[]{:S(2)}) collective-permute-start(bf16[272,256]{1,0:T(8,128)(2,1)} %get-tuple-element.61), channel_id=1, source_target_pairs={{0,2},{2,4},{4,6},{6,0},{1,3},{3,5},{5,7},{7,1},{8,10},{10,12},{12... | collective-permute-start | bytes 417800 | tf_op jit(solution)/shard_map/ppermute | solution.py:382
  52.9 21.8 %collective-permute-start.11 = (bf16[272,256]{1,0:T(8,128)(2,1)}, bf16[272,256]{1,0:T(8,128)(2,1)S(1)}, u32[]{:S(2)}, u32[]{:S(2)}) collective-permute-start(bf16[272,256]{1,0:T(8,128)(2,1)} %get-tuple-element.62), channel_id=1, source_target_pairs={{0,4},{2,6},{4,0},{6,2},{1,5},{3,7},{5,1},{7,3},{8,12},{10,14},{12... | collective-permute-start | bytes 417800 | tf_op jit(solution)/shard_map/ppermute | solution.py:382
  53.9 20.8 %collective-permute-start.12 = (bf16[272,256]{1,0:T(8,128)(2,1)}, bf16[272,256]{1,0:T(8,128)(2,1)S(1)}, u32[]{:S(2)}, u32[]{:S(2)}) collective-permute-start(bf16[272,256]{1,0:T(8,128)(2,1)} %get-tuple-element.63), channel_id=1, source_target_pairs={{0,6},{2,0},{4,2},{6,4},{1,7},{3,1},{5,3},{7,5},{8,14},{10,8},{12,... | collective-permute-start | bytes 417800 | tf_op jit(solution)/shard_map/ppermute | solution.py:382
  74.7 1.0 copy-start.6
  80.2 4.3 %collective-permute-start.15 = (f32[8,256,256]{2,1,0:T(8,128)S(1)}, f32[8,256,256]{2,1,0:T(8,128)S(1)}, u32[]{:S(2)}, u32[]{:S(2)}) collective-permute-start(f32[8,256,256]{2,1,0:T(8,128)S(1)} %get-tuple-element.68), channel_id=1, source_target_pairs={{0,1},{1,0},{2,3},{3,2},{4,5},{5,4},{6,7},{7,6},{8,9},{9,8},{10,11... | collective-permute-start | bytes 6291464 | tf_op jit(solution)/shard_map/ppermute | solution.py:429
  80.8 13.5 %collective-permute-start.13 = (bf16[4,256,256]{2,1,0:T(8,128)(2,1)S(1)}, bf16[4,256,256]{2,1,0:T(8,128)(2,1)S(1)}, u32[]{:S(2)}, u32[]{:S(2)}) collective-permute-start(bf16[4,256,256]{2,1,0:T(8,128)(2,1)S(1)} %get-tuple-element.65), channel_id=1, source_target_pairs={{0,8},{8,16},{16,24},{24,0},{1,9},{9,17},{17,25},{25,1},{2,10},{10... | collective-permute-start | bytes 1572872 | tf_op jit(solution)/shard_map/ppermute | solution.py:382
  81.1 14.4 %collective-permute-start.14 = (bf16[4,256,256]{2,1,0:T(8,128)(2,1)S(1)}, bf16[4,256,256]{2,1,0:T(8,128)(2,1)S(1)}, u32[]{:S(2)}, u32[]{:S(2)}) collective-permute-start(bf16[4,256,256]{2,1,0:T(8,128)(2,1)S(1)} %get-tuple-element.66), channel_id=1, source_target_pairs={{0,24},{8,0},{16,8},{24,16},{1,25},{9,1},{17,9},{25,17},{2,26},{10... | collective-permute-start | bytes 1572872 | tf_op jit(solution)/shard_map/ppermute | solution.py:382
  85.3 11.8 %collective-permute-start.18 = (bf16[2,256,256]{2,1,0:T(8,128)(2,1)S(1)}, bf16[2,256,256]{2,1,0:T(8,128)(2,1)S(1)}, u32[]{:S(2)}, u32[]{:S(2)}) collective-permute-start(bf16[2,256,256]{2,1,0:T(8,128)(2,1)S(1)} %get-tuple-element.70), channel_id=1, source_target_pairs={{0,64},{64,128},{128,192},{192,0},{1,65},{65,129},{129,193},{193,1... | collective-permute-start | bytes 786440 | tf_op jit(solution)/shard_map/ppermute | solution.py:382
  86.8 14.1 %collective-permute-start.19 = (bf16[2,256,256]{2,1,0:T(8,128)(2,1)S(1)}, bf16[2,256,256]{2,1,0:T(8,128)(2,1)S(1)}, u32[]{:S(2)}, u32[]{:S(2)}) collective-permute-start(bf16[2,256,256]{2,1,0:T(8,128)(2,1)S(1)} %get-tuple-element.71), channel_id=1, source_target_pairs={{0,128},{64,192},{128,0},{192,64},{1,129},{65,193},{129,1},{193,65... | collective-permute-start | bytes 786440 | tf_op jit(solution)/shard_map/ppermute | solution.py:382
  89.2 11.7 %collective-permute-start.20 = (bf16[2,256,256]{2,1,0:T(8,128)(2,1)S(1)}, bf16[2,256,256]{2,1,0:T(8,128)(2,1)S(1)}, u32[]{:S(2)}, u32[]{:S(2)}) collective-permute-start(bf16[2,256,256]{2,1,0:T(8,128)(2,1)S(1)} %get-tuple-element.72), channel_id=1, source_target_pairs={{0,192},{64,0},{128,64},{192,128},{1,193},{65,1},{129,65},{193,129... | collective-permute-start | bytes 786440 | tf_op jit(solution)/shard_map/ppermute | solution.py:382
  95.6 10.6 %collective-permute-start.16 = (bf16[2,256,256]{2,1,0:T(8,128)(2,1)S(1)}, bf16[2,256,256]{2,1,0:T(8,128)(2,1)S(1)}, u32[]{:S(2)}, u32[]{:S(2)}) collective-permute-start(bf16[2,256,256]{2,1,0:T(8,128)(2,1)S(1)} %get-tuple-element.77), channel_id=1, source_target_pairs={{0,8},{8,16},{16,24},{24,0},{1,9},{9,17},{17,25},{25,1},{2,10},{10... | collective-permute-start | bytes 786440 | tf_op jit(solution)/shard_map/ppermute | solution.py:382
  96.0 10.2 %collective-permute-start.17 = (bf16[2,256,256]{2,1,0:T(8,128)(2,1)S(1)}, bf16[2,256,256]{2,1,0:T(8,128)(2,1)S(1)}, u32[]{:S(2)}, u32[]{:S(2)}) collective-permute-start(bf16[2,256,256]{2,1,0:T(8,128)(2,1)S(1)} %get-tuple-element.78), channel_id=1, source_target_pairs={{0,24},{8,0},{16,8},{24,16},{1,25},{9,1},{17,9},{25,17},{2,26},{10... | collective-permute-start | bytes 786440 | tf_op jit(solution)/shard_map/ppermute | solution.py:382
  101.0 21.8 %collective-permute-start.24 = (bf16[2,256,256]{2,1,0:T(8,128)(2,1)S(1)}, bf16[2,256,256]{2,1,0:T(8,128)(2,1)S(1)}, u32[]{:S(2)}, u32[]{:S(2)}) collective-permute-start(bf16[2,256,256]{2,1,0:T(8,128)(2,1)S(1)} %total.2.refs_0_), channel_id=1, source_target_pairs={{0,32},{32,0},{1,33},{33,1},{2,34},{34,2},{3,35},{35,3},{4,36},{36... | collective-permute-start | bytes 786440 | tf_op jit(solution)/shard_map/ppermute | solution.py:437
  106.3 16.6 %collective-permute-start.21 = (bf16[256,256]{1,0:T(8,128)(2,1)S(1)}, bf16[256,256]{1,0:T(8,128)(2,1)S(1)}, u32[]{:S(2)}, u32[]{:S(2)}) collective-permute-start(bf16[256,256]{1,0:T(8,128)(2,1)S(1)} %get-tuple-element.82), channel_id=1, source_target_pairs={{0,2},{2,4},{4,6},{6,0},{1,3},{3,5},{5,7},{7,1},{8,10},{10,12},{12... | collective-permute-start | bytes 393224 | tf_op jit(solution)/shard_map/ppermute | solution.py:382
  106.4 20.7 %collective-permute-start.22 = (bf16[256,256]{1,0:T(8,128)(2,1)S(1)}, bf16[256,256]{1,0:T(8,128)(2,1)S(1)}, u32[]{:S(2)}, u32[]{:S(2)}) collective-permute-start(bf16[256,256]{1,0:T(8,128)(2,1)S(1)} %get-tuple-element.83), channel_id=1, source_target_pairs={{0,4},{2,6},{4,0},{6,2},{1,5},{3,7},{5,1},{7,3},{8,12},{10,14},{12... | collective-permute-start | bytes 393224 | tf_op jit(solution)/shard_map/ppermute | solution.py:382
  107.1 22.9 %collective-permute-start.23 = (bf16[256,256]{1,0:T(8,128)(2,1)S(1)}, bf16[256,256]{1,0:T(8,128)(2,1)S(1)}, u32[]{:S(2)}, u32[]{:S(2)}) collective-permute-start(bf16[256,256]{1,0:T(8,128)(2,1)S(1)} %get-tuple-element.84), channel_id=1, source_target_pairs={{0,6},{2,0},{4,2},{6,4},{1,7},{3,1},{5,3},{7,5},{8,14},{10,8},{12,... | collective-permute-start | bytes 393224 | tf_op jit(solution)/shard_map/ppermute | solution.py:382
  131.1 27.9 %all-to-all-start.2 = ((bf16[16,40,256]{2,1,0:T(8,128)(2,1)}), bf16[16,40,256]{2,1,0:T(8,128)(2,1)S(1)}, u32[]{:S(2)}, u32[]{:S(2)}) async-start(bf16[16,40,256]{2,1,0:T(8,128)(2,1)} %bitcast.17), calls=%async_computation.2 | async-start | bytes 655360 | tf_op jit(solution)/shard_map/all_to_all | solution.py:444
  135.9 11.1 %collective-permute-start.25 = (bf16[2,256,256]{2,1,0:T(8,128)(2,1)S(1)}, bf16[2,256,256]{2,1,0:T(8,128)(2,1)S(1)}, u32[]{:S(2)}, u32[]{:S(2)}) collective-permute-start(bf16[2,256,256]{2,1,0:T(8,128)(2,1)S(1)} %total.3.refs_0_), channel_id=1, source_target_pairs={{0,64},{64,128},{128,192},{192,0},{1,65},{65,129},{129,193},{193,1... | collective-permute-start | bytes 786440 | tf_op jit(solution)/shard_map/ppermute | solution.py:382
  137.3 17.2 %collective-permute-start.26 = (bf16[2,256,256]{2,1,0:T(8,128)(2,1)S(1)}, bf16[2,256,256]{2,1,0:T(8,128)(2,1)S(1)}, u32[]{:S(2)}, u32[]{:S(2)}) collective-permute-start(bf16[2,256,256]{2,1,0:T(8,128)(2,1)S(1)} %total.3.refs_0_), channel_id=1, source_target_pairs={{0,128},{64,192},{128,0},{192,64},{1,129},{65,193},{129,1},{193,65... | collective-permute-start | bytes 786440 | tf_op jit(solution)/shard_map/ppermute | solution.py:382
  139.7 15.7 %collective-permute-start.27 = (bf16[2,256,256]{2,1,0:T(8,128)(2,1)S(1)}, bf16[2,256,256]{2,1,0:T(8,128)(2,1)S(1)}, u32[]{:S(2)}, u32[]{:S(2)}) collective-permute-start(bf16[2,256,256]{2,1,0:T(8,128)(2,1)S(1)} %total.3.refs_0_), channel_id=1, source_target_pairs={{0,192},{64,0},{128,64},{192,128},{1,193},{65,1},{129,65},{193,129... | collective-permute-start | bytes 786440 | tf_op jit(solution)/shard_map/ppermute | solution.py:382
  140.9 14.5 %collective-permute-start.28 = (bf16[2,256,256]{2,1,0:T(8,128)(2,1)S(1)}, bf16[2,256,256]{2,1,0:T(8,128)(2,1)S(1)}, u32[]{:S(2)}, u32[]{:S(2)}) collective-permute-start(bf16[2,256,256]{2,1,0:T(8,128)(2,1)S(1)} %total.3.refs_0_), channel_id=1, source_target_pairs={{0,1},{1,0},{2,3},{3,2},{4,5},{5,4},{6,7},{7,6},{8,9},{9,8},{10,11... | collective-permute-start | bytes 786440 | tf_op jit(solution)/shard_map/ppermute | solution.py:446
  147.0 8.4 %collective-permute-start.29 = (bf16[2,256,256]{2,1,0:T(8,128)(2,1)S(1)}, bf16[2,256,256]{2,1,0:T(8,128)(2,1)S(1)}, u32[]{:S(2)}, u32[]{:S(2)}) collective-permute-start(bf16[2,256,256]{2,1,0:T(8,128)(2,1)S(1)} %collective-permute-done.25.refs_1_), channel_id=1, source_target_pairs={{0,1},{1,0},{2,3},{3,2},{4,5},{5,4},{6,7},{7,6},{8,9},{9,8},{10,11... | collective-permute-start | bytes 786440 | tf_op jit(solution)/shard_map/ppermute | solution.py:446
  154.5 2.0 %collective-permute-start.30 = (bf16[2,256,256]{2,1,0:T(8,128)(2,1)S(1)}, bf16[2,256,256]{2,1,0:T(8,128)(2,1)S(1)}, u32[]{:S(2)}, u32[]{:S(2)}) collective-permute-start(bf16[2,256,256]{2,1,0:T(8,128)(2,1)S(1)} %collective-permute-done.26.refs_2_), channel_id=1, source_target_pairs={{0,1},{1,0},{2,3},{3,2},{4,5},{5,4},{6,7},{7,6},{8,9},{9,8},{10,11... | collective-permute-start | bytes 786440 | tf_op jit(solution)/shard_map/ppermute | solution.py:446
  155.4 1.5 collective-permute-start.31

commit v4 on v3

--- a/solution.py
+++ b/solution.py
@@ -74,8 +74,8 @@
     return [shape(4, rows, B)] * 2 + [shape(2, rows, B, dtype=F32)] * 2 + [shape(4, rows, B, dtype=F32)]
 
 
-def piece_shapes(rows):
-    return [shape(2, rows, B)] * 2 + [shape(2, rows, B, dtype=F32)] * 2 + [shape(2, rows, B)] * 2 + [shape(4, rows, B, dtype=F32)]
+def piece_shapes(rows, own=F32):
+    return [shape(2, rows, B)] * 2 + [shape(2, rows, B, dtype=F32)] * 2 + [shape(2, rows, B)] * 2 + [shape(4, rows, B, dtype=own)]
 
 
 def project_kernel(place, hidden, gain, projector, *rest):
@@ -116,7 +116,7 @@
         project_kernel,
         in_specs=[SMEM, hbm, VMEM, hbm],
         out_specs=[VMEM] * 7,
-        out_shape=piece_shapes(rows + 16),
+        out_shape=piece_shapes(rows + 16, BF),
         scratch_shapes=[
             pltpu.VMEM((rows, depth), BF),
             pltpu.VMEM((rows, depth), BF),
@@ -218,7 +218,7 @@
     )(*parts)
 
 
-def middle_kernel(place, a0, a1, a2, a3, weight, at, resid, t0, t1, t2, t3, *outs):
+def middle_kernel(place, a0, a1, a2, a3, weight, resid, t0, t1, t2, t3, *outs):
     pieces, keep, send = outs[:5], outs[5], outs[6]
     y, zl, core = place[0], place[1], place[2]
     attn = (a0, a1, a2, a3)
@@ -226,9 +226,7 @@
     total = sum(r[:B, :].astype(F32) for r in parts)
     power = jnp.sum(sum(r[B:, :].astype(F32) for r in parts), axis=0, keepdims=True)
     power = jnp.sum(jnp.where(eye_mask(B), power, 0.0), axis=1, keepdims=True)
-    rows = lax.broadcasted_iota(jnp.int32, (B, resid.shape[0]), 0)
-    select = jnp.where(rows == at[...], 1.0, 0.0).astype(BF)
-    value = jnp.dot(select, resid[...], preferred_element_type=F32) - total * lax.rsqrt(power / DT + EPS)
+    value = resid[...].astype(F32) - total * lax.rsqrt(power / DT + EPS)
     for k in range(4):
         for j in range(4):
             w = weight[((y + 4 - k) % 4) * 4 + (zl + 4 - j) % 4]
@@ -252,15 +250,15 @@
                 ).astype(out.dtype)
 
 
-def middle(place, chunks, weight, at, resid, parts):
+def middle(place, chunks, weight, resid, parts):
     return pl.pallas_call(
         middle_kernel,
-        in_specs=[SMEM] + [VMEM] * 11,
+        in_specs=[SMEM] + [VMEM] * 10,
         out_specs=[VMEM] * 7,
         out_shape=heavy_shapes(B) + [shape(8, B, B, dtype=F32)] * 2,
         compiler_params=PARAMS,
         name="middle",
-    )(place, *chunks, weight, at.reshape(1, -1), resid.reshape(-1, B), *parts)
+    )(place, *chunks, weight, resid, *parts)
 
 
 def pick_kernel(at, slots, out):
@@ -414,7 +412,7 @@
     up, down = relay(*teacher[2:6], *got)
     far = send_on(up, "y", 1), send_on(down, "y", 3)
     resid, _ = tie(resid, up)
-    resid_slots = lax.all_to_all(resid.reshape(groups, slot, B), GROUP, 0, 0, tiled=True)
+    resid_rows = pick(where, lax.all_to_all(resid.reshape(groups, slot, B), GROUP, 0, 0, tiled=True))
 
     chunk = join(*(p[None] for p in along_zl))
     far, _ = tie(far, chunk)
@@ -422,7 +420,7 @@
     folded = fold(teacher[6], *far)
     parts = [folded[0]] + [send_on(folded[j], "zl", j) for j in (1, 2, 3)]
 
-    outs = middle(place, chunks, weight.reshape(16, B, B), where, resid_slots, parts)
+    outs = middle(place, chunks, weight.reshape(16, B, B), resid_rows, parts)
     grads, keep, send = outs[:5], outs[5], outs[6]
 
     got = relay_first(grads)

time: 161 us -> 161 us (level)
  local copies, waits for them, and re-layouts: 6.6 us -> 4.37 us
    unnamed x19 -> x15, local copies, waits for them, and re-layouts: 6.35 us -> 4.13 us
  transfers between devices with their start and end apart: 35 -> 35, of which waited for: 17 -> 17; matrix products, arithmetic and copies ran while one was open for 0% -> 0% of each run, Pallas kernels for 7% -> 8%
where the time goes in v4:
time: 161 us; the launch traced here: 159 us
  waiting for transfers between devices  78.4 us (49%)
  starting transfers between devices  57.2 us (36%)
  Pallas kernels  18.2 us (11%)
  local copies, waits for them, and re-layouts  4.37 us (3%)
    ppermute x26, waiting for transfers between devices, send_on(): return lax.ppermute(piece, axis, ring(k))  44.7 us
    ppermute x26, starting transfers between devices, send_on(): return lax.ppermute(piece, axis, ring(k))  23.8 us
    ppermute x1, waiting for transfers between devices, body(): away = lax.ppermute(near, 'zh', SWAP)  14.4 us
    all_to_all x1, starting transfers between devices, body(): lax.all_to_all(attn.reshape(groups, slot, B), GROUP, 0, 0, tiled=True)  10.7 us
    all_to_all x1, waiting for transfers between devices, body(): lax.all_to_all(resid.reshape(groups, slot, B), GROUP, 0, 0, tiled=True)  9.84 us
    all_to_all x1, starting transfers between devices, body(): lax.all_to_all(resid.reshape(groups, slot, B), GROUP, 0, 0, tiled=True)  8.98 us
    pallas_call x1, Pallas kernels, project(): pl.pallas_call(project_kernel, in_specs=[SMEM, hbm, VMEM, hbm], out_specs...  5.7 us
    all_to_all x1, waiting for transfers between devices, body(): lax.all_to_all(attn.reshape(groups, slot, B), GROUP, 0, 0, tiled=True)  5.58 us
  transfers between devices with their start and end apart: 35, of which 17 were waited for; matrix products, arithmetic and copies ran while one was open for 0% of the time, Pallas kernels for 8%

profile of v4, /device:TPU:57, one launch (start us, length us, event | category | flops | bytes accessed | tf_op | source)
XLA Modules:
  0.0 159.4 jit_solution(4984092685248573471)
XLA Ops:
  0.6 10.7 %all-to-all-start = ((bf16[16,40,256]{2,1,0:T(8,128)(2,1)}), bf16[16,40,256]{2,1,0:T(8,128)(2,1)S(1)}, u32[]{:S(2)}, u32[]{:S(2)}) async-start(bf16[16,40,256]{2,1,0:T(8,128)(2,1)} %bitcast.33), calls=%async_computation | async-start | bytes 655360 | tf_op jit(solution)/shard_map/all_to_all | solution.py:406
  11.4 1.0 copy-done.2
  13.2 5.7 %project.1 = (bf16[2,272,256]{2,1,0:T(8,128)(2,1)}, bf16[2,272,256]{2,1,0:T(8,128)(2,1)}, f32[2,272,256]{2,1,0:T(8,128)S(1)}, f32[2,272,256]{2,1,0:T(8,128)S(1)}...) custom-call(s32[4]{0:T(128)S(1)} %pad_add_fusion.place, ...), custom_call_target="tpu_custom_call" | custom-call | flops 2147483648 | bytes 8388608 | tf_op jit(solution)/shard_map/project/pallas_call | solution.py:115
  19.0 1.5 collective-permute-start.7
  20.9 5.6 %all-to-all-done = bf16[16,40,256]{2,1,0:T(8,128)(2,1)S(1)} async-done(((bf16[16,40,256]{2,1,0:T(8,128)(2,1)}), bf16[16,40,256]{2,1,0:T(8,128)(2,1)S(1)}, u32[]{:S(2)}, u32[]{:S(2)}) %all-to-all-start) | async-done | bytes 327712 | tf_op jit(solution)/shard_map/all_to_all | solution.py:406
  26.8 0.8 collective-permute-start
  27.6 1.3 collective-permute-start.2
  28.9 1.1 relay.1
  30.0 1.5 collective-permute-start.9
  31.5 6.0 %collective-permute-done.1 = bf16[256,256]{1,0:T(8,128)(2,1)S(1)} collective-permute-done((bf16[256,256]{1,0:T(8,128)(2,1)S(1)}, bf16[256,256]{1,0:T(8,128)(2,1)S(1)}, u32[]{:S(2)}, u32[]{:S(2)}) %collective-permute-start.1) | collective-permute-done | bytes 131104 | tf_op jit(solution)/shard_map/ppermute | solution.py:380
  37.5 1.2 collective-permute-done.2
  38.8 9.0 %all-to-all-start.1 = ((bf16[16,40,256]{2,1,0:T(8,128)(2,1)}), bf16[16,40,256]{2,1,0:T(8,128)(2,1)S(1)}, u32[]{:S(2)}, u32[]{:S(2)}) async-start(bf16[16,40,256]{2,1,0:T(8,128)(2,1)} %bitcast.34), calls=%async_computation.1 | async-start | bytes 655360 | tf_op jit(solution)/shard_map/all_to_all | solution.py:415
  47.8 0.9 collective-permute-start.4
  48.7 2.1 %fold.1 = (f32[272,256]{1,0:T(8,128)S(1)}, bf16[272,256]{1,0:T(8,128)(2,1)}, bf16[272,256]{1,0:T(8,128)(2,1)}, bf16[272,256]{1,0:T(8,128)(2,1)}) custom-call(bf16[4,272,256]{2,1,0:T(8,128)(2,1)S(1)} %get-tuple-element.56.own, bf16[4,272,256]{2,1,0:T(8,128)(2,1)} %collective-permute-done.8.far_up, bf16[4,272,256]{2,1,0:T(8,128)(2,1)} %collective-permute-done.9.far_down), custom_call_target="tpu_custom_call" | custom-call | tf_op jit(solution)/shard_map/fold/pallas_call | solution.py:211
  52.2 1.8 %collective-permute-done.3.a1 = bf16[4,256,256]{2,1,0:T(8,128)(2,1)} collective-permute-done((bf16[4,256,256]{2,1,0:T(8,128)(2,1)S(1)}, bf16[4,256,256]{2,1,0:T(8,128)(2,1)}, u32[]{:S(2)}, u32[]{:S(2)}) %collective-permute-start.3) | collective-permute-done | bytes 524320 | tf_op jit(solution)/shard_map/ppermute | solution.py:380
  54.0 2.0 %collective-permute-start.12 = (bf16[272,256]{1,0:T(8,128)(2,1)}, bf16[272,256]{1,0:T(8,128)(2,1)S(1)}, u32[]{:S(2)}, u32[]{:S(2)}) collective-permute-start(bf16[272,256]{1,0:T(8,128)(2,1)} %get-tuple-element.63), channel_id=1, source_target_pairs={{0,6},{2,0},{4,2},{6,4},{1,7},{3,1},{5,3},{7,5},{8,14},{10,8},{12,... | collective-permute-start | bytes 417800 | tf_op jit(solution)/shard_map/ppermute | solution.py:380
  55.9 9.8 %all-to-all-done.1 = bf16[16,40,256]{2,1,0:T(8,128)(2,1)S(1)} async-done(((bf16[16,40,256]{2,1,0:T(8,128)(2,1)}), bf16[16,40,256]{2,1,0:T(8,128)(2,1)S(1)}, u32[]{:S(2)}, u32[]{:S(2)}) %all-to-all-start.1) | async-done | bytes 327712 | tf_op jit(solution)/shard_map/all_to_all | solution.py:415
  66.1 8.4 %collective-permute-done.5.a3 = bf16[4,256,256]{2,1,0:T(8,128)(2,1)} collective-permute-done((bf16[4,256,256]{2,1,0:T(8,128)(2,1)S(1)}, bf16[4,256,256]{2,1,0:T(8,128)(2,1)}, u32[]{:S(2)}, u32[]{:S(2)}) %collective-permute-start.5) | collective-permute-done | bytes 524320 | tf_op jit(solution)/shard_map/ppermute | solution.py:380
  74.5 0.9 copy-done.4
  75.5 4.5 %middle.1 = (bf16[4,256,256]{2,1,0:T(8,128)(2,1)S(1)}, bf16[4,256,256]{2,1,0:T(8,128)(2,1)S(1)}, f32[2,256,256]{2,1,0:T(8,128)S(1)}, f32[2,256,256]{2,1,0:T(8,12...) custom-call(s32[4]{0:T(128)S(1)} %pad_add_fusion.place, ...), custom_call_target="tpu_custom_call" | custom-call | tf_op jit(solution)/shard_map/middle/pallas_call | solution.py:254
  80.8 1.1 collective-permute-start.14
  82.0 2.3 %collective-permute-done.15.other = f32[8,256,256]{2,1,0:T(8,128)S(1)} collective-permute-done((f32[8,256,256]{2,1,0:T(8,128)S(1)}, f32[8,256,256]{2,1,0:T(8,128)S(1)}, u32[]{:S(2)}, u32[]{:S(2)}) %collective-permute-start.15) | collective-permute-done | bytes 2097184 | tf_op jit(solution)/shard_map/ppermute | solution.py:427
  84.3 0.7 share.1
  85.0 1.5 collective-permute-start.18
  86.5 2.4 %collective-permute-start.19 = (bf16[2,256,256]{2,1,0:T(8,128)(2,1)S(1)}, bf16[2,256,256]{2,1,0:T(8,128)(2,1)S(1)}, u32[]{:S(2)}, u32[]{:S(2)}) collective-permute-start(bf16[2,256,256]{2,1,0:T(8,128)(2,1)S(1)} %get-tuple-element.71), channel_id=1, source_target_pairs={{0,128},{64,192},{128,0},{192,64},{1,129},{65,193},{129,1},{193,65... | collective-permute-start | bytes 786440 | tf_op jit(solution)/shard_map/ppermute | solution.py:380
  88.9 1.2 collective-permute-start.20
  90.1 3.9 %collective-permute-done.13.got_up = bf16[4,256,256]{2,1,0:T(8,128)(2,1)S(1)} collective-permute-done((bf16[4,256,256]{2,1,0:T(8,128)(2,1)S(1)}, bf16[4,256,256]{2,1,0:T(8,128)(2,1)S(1)}, u32[]{:S(2)}, u32[]{:S(2)}) %collective-permute-start.13) | collective-permute-done | bytes 524320 | tf_op jit(solution)/shard_map/ppermute | solution.py:380
  94.0 1.2 collective-permute-done.14.got_down
  95.7 1.1 collective-permute-start.17
  96.8 3.7 %collective-permute-done.19.refs_2_ = bf16[2,256,256]{2,1,0:T(8,128)(2,1)S(1)} collective-permute-done((bf16[2,256,256]{2,1,0:T(8,128)(2,1)S(1)}, bf16[2,256,256]{2,1,0:T(8,128)(2,1)S(1)}, u32[]{:S(2)}, u32[]{:S(2)}) %collective-permute-start.19) | collective-permute-done | bytes 262176 | tf_op jit(solution)/shard_map/ppermute | solution.py:380
  100.7 5.2 %collective-permute-start.24 = (bf16[2,256,256]{2,1,0:T(8,128)(2,1)S(1)}, bf16[2,256,256]{2,1,0:T(8,128)(2,1)S(1)}, u32[]{:S(2)}, u32[]{:S(2)}) collective-permute-start(bf16[2,256,256]{2,1,0:T(8,128)(2,1)S(1)} %total.2.refs_0_), channel_id=1, source_target_pairs={{0,32},{32,0},{1,33},{33,1},{2,34},{34,2},{3,35},{35,3},{4,36},{36... | collective-permute-start | bytes 786440 | tf_op jit(solution)/shard_map/ppermute | solution.py:435
  106.1 0.7 collective-permute-start.22
  106.9 1.1 collective-permute-start.23
  108.2 14.4 %collective-permute-done.24.refs_1_ = bf16[2,256,256]{2,1,0:T(8,128)(2,1)S(1)} collective-permute-done((bf16[2,256,256]{2,1,0:T(8,128)(2,1)S(1)}, bf16[2,256,256]{2,1,0:T(8,128)(2,1)S(1)}, u32[]{:S(2)}, u32[]{:S(2)}) %collective-permute-start.24) | collective-permute-done | bytes 262176 | tf_op jit(solution)/shard_map/ppermute | solution.py:435
  122.6 4.2 %collective-permute-done.22.c = bf16[256,256]{1,0:T(8,128)(2,1)S(1)} collective-permute-done((bf16[256,256]{1,0:T(8,128)(2,1)S(1)}, bf16[256,256]{1,0:T(8,128)(2,1)S(1)}, u32[]{:S(2)}, u32[]{:S(2)}) %collective-permute-start.22) | collective-permute-done | bytes 131104 | tf_op jit(solution)/shard_map/ppermute | solution.py:380
  126.8 2.9 %collective-permute-done.23.d = bf16[256,256]{1,0:T(8,128)(2,1)S(1)} collective-permute-done((bf16[256,256]{1,0:T(8,128)(2,1)S(1)}, bf16[256,256]{1,0:T(8,128)(2,1)S(1)}, u32[]{:S(2)}, u32[]{:S(2)}) %collective-permute-start.23) | collective-permute-done | bytes 131104 | tf_op jit(solution)/shard_map/ppermute | solution.py:380
  129.8 1.0 put.1
  130.8 4.8 %all-to-all-start.2 = ((bf16[16,40,256]{2,1,0:T(8,128)(2,1)}), bf16[16,40,256]{2,1,0:T(8,128)(2,1)S(1)}, u32[]{:S(2)}, u32[]{:S(2)}) async-start(bf16[16,40,256]{2,1,0:T(8,128)(2,1)} %bitcast.17), calls=%async_computation.2 | async-start | bytes 655360 | tf_op jit(solution)/shard_map/all_to_all | solution.py:442
  135.6 1.4 collective-permute-start.25
  137.0 2.4 %collective-permute-start.26 = (bf16[2,256,256]{2,1,0:T(8,128)(2,1)S(1)}, bf16[2,256,256]{2,1,0:T(8,128)(2,1)S(1)}, u32[]{:S(2)}, u32[]{:S(2)}) collective-permute-start(bf16[2,256,256]{2,1,0:T(8,128)(2,1)S(1)} %total.3.refs_0_), channel_id=1, source_target_pairs={{0,128},{64,192},{128,0},{192,64},{1,129},{65,193},{129,1},{193,65... | collective-permute-start | bytes 786440 | tf_op jit(solution)/shard_map/ppermute | solution.py:380
  139.4 1.2 collective-permute-start.27
  140.6 1.2 collective-permute-start.28
  141.8 4.9 %collective-permute-done.25.refs_1_ = bf16[2,256,256]{2,1,0:T(8,128)(2,1)S(1)} collective-permute-done((bf16[2,256,256]{2,1,0:T(8,128)(2,1)S(1)}, bf16[2,256,256]{2,1,0:T(8,128)(2,1)S(1)}, u32[]{:S(2)}, u32[]{:S(2)}) %collective-permute-start.25) | collective-permute-done | bytes 262176 | tf_op jit(solution)/shard_map/ppermute | solution.py:380
  146.7 1.0 collective-permute-start.29
  147.7 6.5 %collective-permute-done.26.refs_2_ = bf16[2,256,256]{2,1,0:T(8,128)(2,1)S(1)} collective-permute-done((bf16[2,256,256]{2,1,0:T(8,128)(2,1)S(1)}, bf16[2,256,256]{2,1,0:T(8,128)(2,1)S(1)}, u32[]{:S(2)}, u32[]{:S(2)}) %collective-permute-start.26) | collective-permute-done | bytes 262176 | tf_op jit(solution)/shard_map/ppermute | solution.py:380
  154.2 0.9 collective-permute-start.30
  155.1 1.1 collective-permute-done.30.refs_6_
  156.7 2.0 %assemble.1 = bf16[16,256,256]{2,1,0:T(8,128)(2,1)} custom-call(s32[4]{0:T(128)S(1)} %pad_add_fusion.place, bf16[2,256,256]{2,1,0:T(8,128)(2,1)S(1)} %total.3.refs_0_, bf16[2,256,256]{2,1,0:T(8,128)(2,1)S(1)} %collective-permute-done.25.refs_1_, bf16[2,256,256]{2,1,0:T(8,128)(2,1)S(1)} %collective-permute-done.26.refs_2_, ...), custom_call_target="tpu_custom_call" | custom-call | tf_op jit(solution)/shard_map/assemble/pallas_call | solution.py:368
  (59 shorter events, 6.5 us)
Async XLA Ops:
  0.6 20.0 %copy-start = (s32[16,16]{1,0:T(8,128)S(1)}, s32[16,16]{1,0:T(8,128)}, u32[]{:S(2)}) copy-start(s32[16,16]{1,0:T(8,128)} %param.12) | copy-start | bytes 3076
  0.6 25.8 %all-to-all-start = ((bf16[16,40,256]{2,1,0:T(8,128)(2,1)}), bf16[16,40,256]{2,1,0:T(8,128)(2,1)S(1)}, u32[]{:S(2)}, u32[]{:S(2)}) async-start(bf16[16,40,256]{2,1,0:T(8,128)(2,1)} %bitcast.33), calls=%async_computation | async-start | bytes 655360 | tf_op jit(solution)/shard_map/all_to_all | solution.py:406
  11.4 1.0 copy-start.2
  12.5 0.7 copy-start.5
  13.2 7.3 %copy-start.6 = (s32[16,16]{1,0:T(8,128)S(1)}, s32[16,16]{1,0:T(8,128)}, u32[]{:S(2)}) copy-start(s32[16,16]{1,0:T(8,128)} %param.11) | copy-start | bytes 3076
  18.9 10.0 %collective-permute-start.6 = (bf16[2,272,256]{2,1,0:T(8,128)(2,1)}, bf16[2,272,256]{2,1,0:T(8,128)(2,1)S(1)}, u32[]{:S(2)}, u32[]{:S(2)}) collective-permute-start(bf16[2,272,256]{2,1,0:T(8,128)(2,1)} %get-tuple-element.50), channel_id=1, source_target_pairs={{0,8},{8,16},{16,24},{24,0},{1,9},{9,17},{17,25},{25,1},{2,10},{10... | collective-permute-start | bytes 835592 | tf_op jit(solution)/shard_map/ppermute | solution.py:380
  19.0 9.9 %collective-permute-start.7 = (bf16[2,272,256]{2,1,0:T(8,128)(2,1)}, bf16[2,272,256]{2,1,0:T(8,128)(2,1)S(1)}, u32[]{:S(2)}, u32[]{:S(2)}) collective-permute-start(bf16[2,272,256]{2,1,0:T(8,128)(2,1)} %get-tuple-element.51), channel_id=1, source_target_pairs={{0,24},{8,0},{16,8},{24,16},{1,25},{9,1},{17,9},{25,17},{2,26},{10... | collective-permute-start | bytes 835592 | tf_op jit(solution)/shard_map/ppermute | solution.py:380
  26.8 4.7 %collective-permute-start = (bf16[256,256]{1,0:T(8,128)(2,1)S(1)}, bf16[256,256]{1,0:T(8,128)(2,1)S(1)}, u32[]{:S(2)}, u32[]{:S(2)}) collective-permute-start(bf16[256,256]{1,0:T(8,128)(2,1)S(1)} %pick.2), channel_id=1, source_target_pairs={{0,2},{2,4},{4,6},{6,0},{1,3},{3,5},{5,7},{7,1},{8,10},{10,12},{12... | collective-permute-start | bytes 393224 | tf_op jit(solution)/shard_map/ppermute | solution.py:380
  27.6 9.9 %collective-permute-start.1 = (bf16[256,256]{1,0:T(8,128)(2,1)S(1)}, bf16[256,256]{1,0:T(8,128)(2,1)S(1)}, u32[]{:S(2)}, u32[]{:S(2)}) collective-permute-start(bf16[256,256]{1,0:T(8,128)(2,1)S(1)} %pick.2), channel_id=1, source_target_pairs={{0,4},{2,6},{4,0},{6,2},{1,5},{3,7},{5,1},{7,3},{8,12},{10,14},{12... | collective-permute-start | bytes 393224 | tf_op jit(solution)/shard_map/ppermute | solution.py:380
  27.6 11.1 %collective-permute-start.2 = (bf16[256,256]{1,0:T(8,128)(2,1)S(1)}, bf16[256,256]{1,0:T(8,128)(2,1)S(1)}, u32[]{:S(2)}, u32[]{:S(2)}) collective-permute-start(bf16[256,256]{1,0:T(8,128)(2,1)S(1)} %pick.2), channel_id=1, source_target_pairs={{0,6},{2,0},{4,2},{6,4},{1,7},{3,1},{5,3},{7,5},{8,14},{10,8},{12,... | collective-permute-start | bytes 393224 | tf_op jit(solution)/shard_map/ppermute | solution.py:380
  30.0 44.5 %copy-start.1 = (bf16[4096,256]{1,0:T(8,128)(2,1)S(1)}, bf16[4096,256]{1,0:T(8,128)(2,1)}, u32[]{:S(2)}) copy-start(bf16[4096,256]{1,0:T(8,128)(2,1)} %param.15) | copy-start | bytes 6291460
  30.0 18.7 %collective-permute-start.8 = (bf16[4,272,256]{2,1,0:T(8,128)(2,1)}, bf16[4,272,256]{2,1,0:T(8,128)(2,1)}, u32[]{:S(2)}, u32[]{:S(2)}) collective-permute-start(bf16[4,272,256]{2,1,0:T(8,128)(2,1)} %get-tuple-element.54), channel_id=1, source_target_pairs={{0,8},{8,16},{16,24},{24,0},{1,9},{9,17},{17,25},{25,1},{2,10},{10... | collective-permute-start | bytes 1671176 | tf_op jit(solution)/shard_map/ppermute | solution.py:380
  30.0 18.7 %collective-permute-start.9 = (bf16[4,272,256]{2,1,0:T(8,128)(2,1)}, bf16[4,272,256]{2,1,0:T(8,128)(2,1)}, u32[]{:S(2)}, u32[]{:S(2)}) collective-permute-start(bf16[4,272,256]{2,1,0:T(8,128)(2,1)} %get-tuple-element.57), channel_id=1, source_target_pairs={{0,24},{8,0},{16,8},{24,16},{1,25},{9,1},{17,9},{25,17},{2,26},{10... | collective-permute-start | bytes 1671176 | tf_op jit(solution)/shard_map/ppermute | solution.py:380
  38.7 15.3 %collective-permute-start.3 = (bf16[4,256,256]{2,1,0:T(8,128)(2,1)S(1)}, bf16[4,256,256]{2,1,0:T(8,128)(2,1)}, u32[]{:S(2)}, u32[]{:S(2)}) collective-permute-start(bf16[4,256,256]{2,1,0:T(8,128)(2,1)S(1)} %join.1.a0), channel_id=1, source_target_pairs={{0,8},{8,16},{16,24},{24,0},{1,9},{9,17},{17,25},{25,1},{2,10},{10... | collective-permute-start | bytes 1572872 | tf_op jit(solution)/shard_map/ppermute | solution.py:380
  38.8 27.0 %all-to-all-start.1 = ((bf16[16,40,256]{2,1,0:T(8,128)(2,1)}), bf16[16,40,256]{2,1,0:T(8,128)(2,1)S(1)}, u32[]{:S(2)}, u32[]{:S(2)}) async-start(bf16[16,40,256]{2,1,0:T(8,128)(2,1)} %bitcast.34), calls=%async_computation.1 | async-start | bytes 655360 | tf_op jit(solution)/shard_map/all_to_all | solution.py:415
  47.8 18.3 %collective-permute-start.4 = (bf16[4,256,256]{2,1,0:T(8,128)(2,1)S(1)}, bf16[4,256,256]{2,1,0:T(8,128)(2,1)}, u32[]{:S(2)}, u32[]{:S(2)}) collective-permute-start(bf16[4,256,256]{2,1,0:T(8,128)(2,1)S(1)} %join.1.a0), channel_id=1, source_target_pairs={{0,16},{8,24},{16,0},{24,8},{1,17},{9,25},{17,1},{25,9},{2,18},{10... | collective-permute-start | bytes 1572872 | tf_op jit(solution)/shard_map/ppermute | solution.py:380
  48.7 25.8 %collective-permute-start.5 = (bf16[4,256,256]{2,1,0:T(8,128)(2,1)S(1)}, bf16[4,256,256]{2,1,0:T(8,128)(2,1)}, u32[]{:S(2)}, u32[]{:S(2)}) collective-permute-start(bf16[4,256,256]{2,1,0:T(8,128)(2,1)S(1)} %join.1.a0), channel_id=1, source_target_pairs={{0,24},{8,0},{16,8},{24,16},{1,25},{9,1},{17,9},{25,17},{2,26},{10... | collective-permute-start | bytes 1572872 | tf_op jit(solution)/shard_map/ppermute | solution.py:380
  50.8 0.7 copy-start.3
  51.5 23.0 %collective-permute-start.10 = (bf16[272,256]{1,0:T(8,128)(2,1)}, bf16[272,256]{1,0:T(8,128)(2,1)S(1)}, u32[]{:S(2)}, u32[]{:S(2)}) collective-permute-start(bf16[272,256]{1,0:T(8,128)(2,1)} %get-tuple-element.61), channel_id=1, source_target_pairs={{0,2},{2,4},{4,6},{6,0},{1,3},{3,5},{5,7},{7,1},{8,10},{10,12},{12... | collective-permute-start | bytes 417800 | tf_op jit(solution)/shard_map/ppermute | solution.py:380
  51.5 23.0 %collective-permute-start.11 = (bf16[272,256]{1,0:T(8,128)(2,1)}, bf16[272,256]{1,0:T(8,128)(2,1)S(1)}, u32[]{:S(2)}, u32[]{:S(2)}) collective-permute-start(bf16[272,256]{1,0:T(8,128)(2,1)} %get-tuple-element.62), channel_id=1, source_target_pairs={{0,4},{2,6},{4,0},{6,2},{1,5},{3,7},{5,1},{7,3},{8,12},{10,14},{12... | collective-permute-start | bytes 417800 | tf_op jit(solution)/shard_map/ppermute | solution.py:380
  54.0 20.5 %collective-permute-start.12 = (bf16[272,256]{1,0:T(8,128)(2,1)}, bf16[272,256]{1,0:T(8,128)(2,1)S(1)}, u32[]{:S(2)}, u32[]{:S(2)}) collective-permute-start(bf16[272,256]{1,0:T(8,128)(2,1)} %get-tuple-element.63), channel_id=1, source_target_pairs={{0,6},{2,0},{4,2},{6,4},{1,7},{3,1},{5,3},{7,5},{8,14},{10,8},{12,... | collective-permute-start | bytes 417800 | tf_op jit(solution)/shard_map/ppermute | solution.py:380
  74.5 1.0 copy-start.4
  80.0 4.3 %collective-permute-start.15 = (f32[8,256,256]{2,1,0:T(8,128)S(1)}, f32[8,256,256]{2,1,0:T(8,128)S(1)}, u32[]{:S(2)}, u32[]{:S(2)}) collective-permute-start(f32[8,256,256]{2,1,0:T(8,128)S(1)} %get-tuple-element.68), channel_id=1, source_target_pairs={{0,1},{1,0},{2,3},{3,2},{4,5},{5,4},{6,7},{7,6},{8,9},{9,8},{10,11... | collective-permute-start | bytes 6291464 | tf_op jit(solution)/shard_map/ppermute | solution.py:427
  80.5 13.5 %collective-permute-start.13 = (bf16[4,256,256]{2,1,0:T(8,128)(2,1)S(1)}, bf16[4,256,256]{2,1,0:T(8,128)(2,1)S(1)}, u32[]{:S(2)}, u32[]{:S(2)}) collective-permute-start(bf16[4,256,256]{2,1,0:T(8,128)(2,1)S(1)} %get-tuple-element.65), channel_id=1, source_target_pairs={{0,8},{8,16},{16,24},{24,0},{1,9},{9,17},{17,25},{25,1},{2,10},{10... | collective-permute-start | bytes 1572872 | tf_op jit(solution)/shard_map/ppermute | solution.py:380
  80.8 14.4 %collective-permute-start.14 = (bf16[4,256,256]{2,1,0:T(8,128)(2,1)S(1)}, bf16[4,256,256]{2,1,0:T(8,128)(2,1)S(1)}, u32[]{:S(2)}, u32[]{:S(2)}) collective-permute-start(bf16[4,256,256]{2,1,0:T(8,128)(2,1)S(1)} %get-tuple-element.66), channel_id=1, source_target_pairs={{0,24},{8,0},{16,8},{24,16},{1,25},{9,1},{17,9},{25,17},{2,26},{10... | collective-permute-start | bytes 1572872 | tf_op jit(solution)/shard_map/ppermute | solution.py:380
  85.0 11.8 %collective-permute-start.18 = (bf16[2,256,256]{2,1,0:T(8,128)(2,1)S(1)}, bf16[2,256,256]{2,1,0:T(8,128)(2,1)S(1)}, u32[]{:S(2)}, u32[]{:S(2)}) collective-permute-start(bf16[2,256,256]{2,1,0:T(8,128)(2,1)S(1)} %get-tuple-element.70), channel_id=1, source_target_pairs={{0,64},{64,128},{128,192},{192,0},{1,65},{65,129},{129,193},{193,1... | collective-permute-start | bytes 786440 | tf_op jit(solution)/shard_map/ppermute | solution.py:380
  86.5 14.1 %collective-permute-start.19 = (bf16[2,256,256]{2,1,0:T(8,128)(2,1)S(1)}, bf16[2,256,256]{2,1,0:T(8,128)(2,1)S(1)}, u32[]{:S(2)}, u32[]{:S(2)}) collective-permute-start(bf16[2,256,256]{2,1,0:T(8,128)(2,1)S(1)} %get-tuple-element.71), channel_id=1, source_target_pairs={{0,128},{64,192},{128,0},{192,64},{1,129},{65,193},{129,1},{193,65... | collective-permute-start | bytes 786440 | tf_op jit(solution)/shard_map/ppermute | solution.py:380
  88.9 11.7 %collective-permute-start.20 = (bf16[2,256,256]{2,1,0:T(8,128)(2,1)S(1)}, bf16[2,256,256]{2,1,0:T(8,128)(2,1)S(1)}, u32[]{:S(2)}, u32[]{:S(2)}) collective-permute-start(bf16[2,256,256]{2,1,0:T(8,128)(2,1)S(1)} %get-tuple-element.72), channel_id=1, source_target_pairs={{0,192},{64,0},{128,64},{192,128},{1,193},{65,1},{129,65},{193,129... | collective-permute-start | bytes 786440 | tf_op jit(solution)/shard_map/ppermute | solution.py:380
  95.3 10.6 %collective-permute-start.16 = (bf16[2,256,256]{2,1,0:T(8,128)(2,1)S(1)}, bf16[2,256,256]{2,1,0:T(8,128)(2,1)S(1)}, u32[]{:S(2)}, u32[]{:S(2)}) collective-permute-start(bf16[2,256,256]{2,1,0:T(8,128)(2,1)S(1)} %get-tuple-element.77), channel_id=1, source_target_pairs={{0,8},{8,16},{16,24},{24,0},{1,9},{9,17},{17,25},{25,1},{2,10},{10... | collective-permute-start | bytes 786440 | tf_op jit(solution)/shard_map/ppermute | solution.py:380
  95.7 10.2 %collective-permute-start.17 = (bf16[2,256,256]{2,1,0:T(8,128)(2,1)S(1)}, bf16[2,256,256]{2,1,0:T(8,128)(2,1)S(1)}, u32[]{:S(2)}, u32[]{:S(2)}) collective-permute-start(bf16[2,256,256]{2,1,0:T(8,128)(2,1)S(1)} %get-tuple-element.78), channel_id=1, source_target_pairs={{0,24},{8,0},{16,8},{24,16},{1,25},{9,1},{17,9},{25,17},{2,26},{10... | collective-permute-start | bytes 786440 | tf_op jit(solution)/shard_map/ppermute | solution.py:380
  100.7 21.9 %collective-permute-start.24 = (bf16[2,256,256]{2,1,0:T(8,128)(2,1)S(1)}, bf16[2,256,256]{2,1,0:T(8,128)(2,1)S(1)}, u32[]{:S(2)}, u32[]{:S(2)}) collective-permute-start(bf16[2,256,256]{2,1,0:T(8,128)(2,1)S(1)} %total.2.refs_0_), channel_id=1, source_target_pairs={{0,32},{32,0},{1,33},{33,1},{2,34},{34,2},{3,35},{35,3},{4,36},{36... | collective-permute-start | bytes 786440 | tf_op jit(solution)/shard_map/ppermute | solution.py:435
  106.0 16.6 %collective-permute-start.21 = (bf16[256,256]{1,0:T(8,128)(2,1)S(1)}, bf16[256,256]{1,0:T(8,128)(2,1)S(1)}, u32[]{:S(2)}, u32[]{:S(2)}) collective-permute-start(bf16[256,256]{1,0:T(8,128)(2,1)S(1)} %get-tuple-element.82), channel_id=1, source_target_pairs={{0,2},{2,4},{4,6},{6,0},{1,3},{3,5},{5,7},{7,1},{8,10},{10,12},{12... | collective-permute-start | bytes 393224 | tf_op jit(solution)/shard_map/ppermute | solution.py:380
  106.1 20.7 %collective-permute-start.22 = (bf16[256,256]{1,0:T(8,128)(2,1)S(1)}, bf16[256,256]{1,0:T(8,128)(2,1)S(1)}, u32[]{:S(2)}, u32[]{:S(2)}) collective-permute-start(bf16[256,256]{1,0:T(8,128)(2,1)S(1)} %get-tuple-element.83), channel_id=1, source_target_pairs={{0,4},{2,6},{4,0},{6,2},{1,5},{3,7},{5,1},{7,3},{8,12},{10,14},{12... | collective-permute-start | bytes 393224 | tf_op jit(solution)/shard_map/ppermute | solution.py:380
  106.9 22.9 %collective-permute-start.23 = (bf16[256,256]{1,0:T(8,128)(2,1)S(1)}, bf16[256,256]{1,0:T(8,128)(2,1)S(1)}, u32[]{:S(2)}, u32[]{:S(2)}) collective-permute-start(bf16[256,256]{1,0:T(8,128)(2,1)S(1)} %get-tuple-element.84), channel_id=1, source_target_pairs={{0,6},{2,0},{4,2},{6,4},{1,7},{3,1},{5,3},{7,5},{8,14},{10,8},{12,... | collective-permute-start | bytes 393224 | tf_op jit(solution)/shard_map/ppermute | solution.py:380
  130.8 27.9 %all-to-all-start.2 = ((bf16[16,40,256]{2,1,0:T(8,128)(2,1)}), bf16[16,40,256]{2,1,0:T(8,128)(2,1)S(1)}, u32[]{:S(2)}, u32[]{:S(2)}) async-start(bf16[16,40,256]{2,1,0:T(8,128)(2,1)} %bitcast.17), calls=%async_computation.2 | async-start | bytes 655360 | tf_op jit(solution)/shard_map/all_to_all | solution.py:442
  135.6 11.1 %collective-permute-start.25 = (bf16[2,256,256]{2,1,0:T(8,128)(2,1)S(1)}, bf16[2,256,256]{2,1,0:T(8,128)(2,1)S(1)}, u32[]{:S(2)}, u32[]{:S(2)}) collective-permute-start(bf16[2,256,256]{2,1,0:T(8,128)(2,1)S(1)} %total.3.refs_0_), channel_id=1, source_target_pairs={{0,64},{64,128},{128,192},{192,0},{1,65},{65,129},{129,193},{193,1... | collective-permute-start | bytes 786440 | tf_op jit(solution)/shard_map/ppermute | solution.py:380
  137.0 17.2 %collective-permute-start.26 = (bf16[2,256,256]{2,1,0:T(8,128)(2,1)S(1)}, bf16[2,256,256]{2,1,0:T(8,128)(2,1)S(1)}, u32[]{:S(2)}, u32[]{:S(2)}) collective-permute-start(bf16[2,256,256]{2,1,0:T(8,128)(2,1)S(1)} %total.3.refs_0_), channel_id=1, source_target_pairs={{0,128},{64,192},{128,0},{192,64},{1,129},{65,193},{129,1},{193,65... | collective-permute-start | bytes 786440 | tf_op jit(solution)/shard_map/ppermute | solution.py:380
  139.4 15.7 %collective-permute-start.27 = (bf16[2,256,256]{2,1,0:T(8,128)(2,1)S(1)}, bf16[2,256,256]{2,1,0:T(8,128)(2,1)S(1)}, u32[]{:S(2)}, u32[]{:S(2)}) collective-permute-start(bf16[2,256,256]{2,1,0:T(8,128)(2,1)S(1)} %total.3.refs_0_), channel_id=1, source_target_pairs={{0,192},{64,0},{128,64},{192,128},{1,193},{65,1},{129,65},{193,129... | collective-permute-start | bytes 786440 | tf_op jit(solution)/shard_map/ppermute | solution.py:380
  140.6 14.5 %collective-permute-start.28 = (bf16[2,256,256]{2,1,0:T(8,128)(2,1)S(1)}, bf16[2,256,256]{2,1,0:T(8,128)(2,1)S(1)}, u32[]{:S(2)}, u32[]{:S(2)}) collective-permute-start(bf16[2,256,256]{2,1,0:T(8,128)(2,1)S(1)} %total.3.refs_0_), channel_id=1, source_target_pairs={{0,1},{1,0},{2,3},{3,2},{4,5},{5,4},{6,7},{7,6},{8,9},{9,8},{10,11... | collective-permute-start | bytes 786440 | tf_op jit(solution)/shard_map/ppermute | solution.py:444
  146.7 8.4 %collective-permute-start.29 = (bf16[2,256,256]{2,1,0:T(8,128)(2,1)S(1)}, bf16[2,256,256]{2,1,0:T(8,128)(2,1)S(1)}, u32[]{:S(2)}, u32[]{:S(2)}) collective-permute-start(bf16[2,256,256]{2,1,0:T(8,128)(2,1)S(1)} %collective-permute-done.25.refs_1_), channel_id=1, source_target_pairs={{0,1},{1,0},{2,3},{3,2},{4,5},{5,4},{6,7},{7,6},{8,9},{9,8},{10,11... | collective-permute-start | bytes 786440 | tf_op jit(solution)/shard_map/ppermute | solution.py:444
  154.2 2.0 %collective-permute-start.30 = (bf16[2,256,256]{2,1,0:T(8,128)(2,1)S(1)}, bf16[2,256,256]{2,1,0:T(8,128)(2,1)S(1)}, u32[]{:S(2)}, u32[]{:S(2)}) collective-permute-start(bf16[2,256,256]{2,1,0:T(8,128)(2,1)S(1)} %collective-permute-done.26.refs_2_), channel_id=1, source_target_pairs={{0,1},{1,0},{2,3},{3,2},{4,5},{5,4},{6,7},{7,6},{8,9},{9,8},{10,11... | collective-permute-start | bytes 786440 | tf_op jit(solution)/shard_map/ppermute | solution.py:444
  155.1 1.5 collective-permute-start.31

commit v5 on v4

--- a/solution.py
+++ b/solution.py
@@ -255,7 +255,7 @@
         middle_kernel,
         in_specs=[SMEM] + [VMEM] * 10,
         out_specs=[VMEM] * 7,
-        out_shape=heavy_shapes(B) + [shape(8, B, B, dtype=F32)] * 2,
+        out_shape=heavy_shapes(B) + [shape(8, B, B, dtype=F32), shape(8, B, B)],
         compiler_params=PARAMS,
         name="middle",
     )(place, *chunks, weight, resid, *parts)
@@ -320,7 +320,7 @@
     for k, out in enumerate(outs):
         for i in range(2):
             at = ((place[3] + k) % 4) * 2 + i
-            out[i] = (keep[at] + other[at]).astype(out.dtype)
+            out[i] = (keep[at] + other[at].astype(F32)).astype(out.dtype)
 
 
 def share(place, keep, other):
@@ -426,7 +426,6 @@
     got = relay_first(grads)
     other = lax.ppermute(send, "core", SWAP)
     pieces = share(place, keep, other)
-    got, _ = tie(got, pieces)
     pieces = [pieces[0]] + [send_on(pieces[k], "x", k) for k in (1, 2, 3)]
     up, down = heavy_relay(grads[2], grads[3], *got)
     far = send_on(up, "y", 1), send_on(down, "y", 3)

time: 161 us -> 159 us (0.988)
  no operation moved by 1% of the time
where the time goes in v5:
time: 159 us; the launch traced here: 158 us
  waiting for transfers between devices  76.8 us (48%)
  starting transfers between devices  57.3 us (36%)
  Pallas kernels  18.2 us (11%)
  local copies, waits for them, and re-layouts  4.37 us (3%)
    ppermute x26, waiting for transfers between devices, send_on(): return lax.ppermute(piece, axis, ring(k))  44.8 us
    ppermute x26, starting transfers between devices, send_on(): return lax.ppermute(piece, axis, ring(k))  23.9 us
    ppermute x1, waiting for transfers between devices, body(): away = lax.ppermute(near, 'zh', SWAP)  14.2 us
    all_to_all x1, starting transfers between devices, body(): lax.all_to_all(attn.reshape(groups, slot, B), GROUP, 0, 0, tiled=True)  10.7 us
    all_to_all x1, waiting for transfers between devices, body(): lax.all_to_all(resid.reshape(groups, slot, B), GROUP, 0, 0, tiled=True)  9.84 us
    all_to_all x1, starting transfers between devices, body(): lax.all_to_all(resid.reshape(groups, slot, B), GROUP, 0, 0, tiled=True)  8.98 us
    pallas_call x1, Pallas kernels, project(): pl.pallas_call(project_kernel, in_specs=[SMEM, hbm, VMEM, hbm], out_specs...  5.7 us
    all_to_all x1, waiting for transfers between devices, body(): lax.all_to_all(attn.reshape(groups, slot, B), GROUP, 0, 0, tiled=True)  5.58 us
  transfers between devices with their start and end apart: 35, of which 17 were waited for; matrix products, arithmetic and copies ran while one was open for 0% of the time, Pallas kernels for 8%

profile of v5, /device:TPU:57, one launch (start us, length us, event | category | flops | bytes accessed | tf_op | source)
XLA Modules:
  0.0 157.9 jit_solution(5778528453822343620)
XLA Ops:
  0.6 10.7 %all-to-all-start = ((bf16[16,40,256]{2,1,0:T(8,128)(2,1)}), bf16[16,40,256]{2,1,0:T(8,128)(2,1)S(1)}, u32[]{:S(2)}, u32[]{:S(2)}) async-start(bf16[16,40,256]{2,1,0:T(8,128)(2,1)} %bitcast.33), calls=%async_computation | async-start | bytes 655360 | tf_op jit(solution)/shard_map/all_to_all | solution.py:406
  11.4 1.0 copy-done.2
  13.2 5.7 %project.1 = (bf16[2,272,256]{2,1,0:T(8,128)(2,1)}, bf16[2,272,256]{2,1,0:T(8,128)(2,1)}, f32[2,272,256]{2,1,0:T(8,128)S(1)}, f32[2,272,256]{2,1,0:T(8,128)S(1)}...) custom-call(s32[4]{0:T(128)S(1)} %pad_add_fusion.place, ...), custom_call_target="tpu_custom_call" | custom-call | flops 2147483648 | bytes 8388608 | tf_op jit(solution)/shard_map/project/pallas_call | solution.py:115
  19.0 1.5 collective-permute-start.7
  20.9 5.6 %all-to-all-done = bf16[16,40,256]{2,1,0:T(8,128)(2,1)S(1)} async-done(((bf16[16,40,256]{2,1,0:T(8,128)(2,1)}), bf16[16,40,256]{2,1,0:T(8,128)(2,1)S(1)}, u32[]{:S(2)}, u32[]{:S(2)}) %all-to-all-start) | async-done | bytes 327712 | tf_op jit(solution)/shard_map/all_to_all | solution.py:406
  26.8 0.8 collective-permute-start
  27.6 1.3 collective-permute-start.2
  28.9 1.1 relay.1
  30.0 1.5 collective-permute-start.9
  31.5 6.0 %collective-permute-done.1 = bf16[256,256]{1,0:T(8,128)(2,1)S(1)} collective-permute-done((bf16[256,256]{1,0:T(8,128)(2,1)S(1)}, bf16[256,256]{1,0:T(8,128)(2,1)S(1)}, u32[]{:S(2)}, u32[]{:S(2)}) %collective-permute-start.1) | collective-permute-done | bytes 131104 | tf_op jit(solution)/shard_map/ppermute | solution.py:380
  37.5 1.2 collective-permute-done.2
  38.8 9.0 %all-to-all-start.1 = ((bf16[16,40,256]{2,1,0:T(8,128)(2,1)}), bf16[16,40,256]{2,1,0:T(8,128)(2,1)S(1)}, u32[]{:S(2)}, u32[]{:S(2)}) async-start(bf16[16,40,256]{2,1,0:T(8,128)(2,1)} %bitcast.34), calls=%async_computation.1 | async-start | bytes 655360 | tf_op jit(solution)/shard_map/all_to_all | solution.py:415
  47.8 0.9 collective-permute-start.4
  48.7 2.1 %fold.1 = (f32[272,256]{1,0:T(8,128)S(1)}, bf16[272,256]{1,0:T(8,128)(2,1)}, bf16[272,256]{1,0:T(8,128)(2,1)}, bf16[272,256]{1,0:T(8,128)(2,1)}) custom-call(bf16[4,272,256]{2,1,0:T(8,128)(2,1)S(1)} %get-tuple-element.54.own, bf16[4,272,256]{2,1,0:T(8,128)(2,1)} %collective-permute-done.8.far_up, bf16[4,272,256]{2,1,0:T(8,128)(2,1)} %collective-permute-done.9.far_down), custom_call_target="tpu_custom_call" | custom-call | tf_op jit(solution)/shard_map/fold/pallas_call | solution.py:211
  52.2 1.8 %collective-permute-done.3.a1 = bf16[4,256,256]{2,1,0:T(8,128)(2,1)} collective-permute-done((bf16[4,256,256]{2,1,0:T(8,128)(2,1)S(1)}, bf16[4,256,256]{2,1,0:T(8,128)(2,1)}, u32[]{:S(2)}, u32[]{:S(2)}) %collective-permute-start.3) | collective-permute-done | bytes 524320 | tf_op jit(solution)/shard_map/ppermute | solution.py:380
  54.0 2.0 %collective-permute-start.12 = (bf16[272,256]{1,0:T(8,128)(2,1)}, bf16[272,256]{1,0:T(8,128)(2,1)S(1)}, u32[]{:S(2)}, u32[]{:S(2)}) collective-permute-start(bf16[272,256]{1,0:T(8,128)(2,1)} %get-tuple-element.61), channel_id=1, source_target_pairs={{0,6},{2,0},{4,2},{6,4},{1,7},{3,1},{5,3},{7,5},{8,14},{10,8},{12,... | collective-permute-start | bytes 417800 | tf_op jit(solution)/shard_map/ppermute | solution.py:380
  55.9 9.8 %all-to-all-done.1 = bf16[16,40,256]{2,1,0:T(8,128)(2,1)S(1)} async-done(((bf16[16,40,256]{2,1,0:T(8,128)(2,1)}), bf16[16,40,256]{2,1,0:T(8,128)(2,1)S(1)}, u32[]{:S(2)}, u32[]{:S(2)}) %all-to-all-start.1) | async-done | bytes 327712 | tf_op jit(solution)/shard_map/all_to_all | solution.py:415
  66.1 8.4 %collective-permute-done.5.a3 = bf16[4,256,256]{2,1,0:T(8,128)(2,1)} collective-permute-done((bf16[4,256,256]{2,1,0:T(8,128)(2,1)S(1)}, bf16[4,256,256]{2,1,0:T(8,128)(2,1)}, u32[]{:S(2)}, u32[]{:S(2)}) %collective-permute-start.5) | collective-permute-done | bytes 524320 | tf_op jit(solution)/shard_map/ppermute | solution.py:380
  74.5 0.9 copy-done.4
  75.5 4.5 %middle.1 = (bf16[4,256,256]{2,1,0:T(8,128)(2,1)S(1)}, bf16[4,256,256]{2,1,0:T(8,128)(2,1)S(1)}, f32[2,256,256]{2,1,0:T(8,128)S(1)}, f32[2,256,256]{2,1,0:T(8,12...) custom-call(s32[4]{0:T(128)S(1)} %pad_add_fusion.place, ...), custom_call_target="tpu_custom_call" | custom-call | tf_op jit(solution)/shard_map/middle/pallas_call | solution.py:254
  80.8 1.1 collective-permute-start.14
  82.0 0.8 collective-permute-done.17.other
  83.5 1.5 collective-permute-start.18
  85.0 2.4 %collective-permute-start.19 = (bf16[2,256,256]{2,1,0:T(8,128)(2,1)S(1)}, bf16[2,256,256]{2,1,0:T(8,128)(2,1)S(1)}, u32[]{:S(2)}, u32[]{:S(2)}) collective-permute-start(bf16[2,256,256]{2,1,0:T(8,128)(2,1)S(1)} %get-tuple-element.73), channel_id=1, source_target_pairs={{0,128},{64,192},{128,0},{192,64},{1,129},{65,193},{129,1},{193,65... | collective-permute-start | bytes 786440 | tf_op jit(solution)/shard_map/ppermute | solution.py:380
  87.4 1.2 collective-permute-start.20
  88.6 5.4 %collective-permute-done.13.got_up = bf16[4,256,256]{2,1,0:T(8,128)(2,1)S(1)} collective-permute-done((bf16[4,256,256]{2,1,0:T(8,128)(2,1)S(1)}, bf16[4,256,256]{2,1,0:T(8,128)(2,1)S(1)}, u32[]{:S(2)}, u32[]{:S(2)}) %collective-permute-start.13) | collective-permute-done | bytes 524320 | tf_op jit(solution)/shard_map/ppermute | solution.py:380
  94.0 1.2 collective-permute-done.14.got_down
  95.7 1.1 collective-permute-start.16
  96.9 2.2 %collective-permute-done.19.refs_2_ = bf16[2,256,256]{2,1,0:T(8,128)(2,1)S(1)} collective-permute-done((bf16[2,256,256]{2,1,0:T(8,128)(2,1)S(1)}, bf16[2,256,256]{2,1,0:T(8,128)(2,1)S(1)}, u32[]{:S(2)}, u32[]{:S(2)}) %collective-permute-start.19) | collective-permute-done | bytes 262176 | tf_op jit(solution)/shard_map/ppermute | solution.py:380
  99.2 5.2 %collective-permute-start.24 = (bf16[2,256,256]{2,1,0:T(8,128)(2,1)S(1)}, bf16[2,256,256]{2,1,0:T(8,128)(2,1)S(1)}, u32[]{:S(2)}, u32[]{:S(2)}) collective-permute-start(bf16[2,256,256]{2,1,0:T(8,128)(2,1)S(1)} %total.2.refs_0_), channel_id=1, source_target_pairs={{0,32},{32,0},{1,33},{33,1},{2,34},{34,2},{3,35},{35,3},{4,36},{36... | collective-permute-start | bytes 786440 | tf_op jit(solution)/shard_map/ppermute | solution.py:434
  104.6 1.2 collective-permute-start.22
  105.8 0.7 collective-permute-start.23
  106.7 14.2 %collective-permute-done.24.refs_1_ = bf16[2,256,256]{2,1,0:T(8,128)(2,1)S(1)} collective-permute-done((bf16[2,256,256]{2,1,0:T(8,128)(2,1)S(1)}, bf16[2,256,256]{2,1,0:T(8,128)(2,1)S(1)}, u32[]{:S(2)}, u32[]{:S(2)}) %collective-permute-start.24) | collective-permute-done | bytes 262176 | tf_op jit(solution)/shard_map/ppermute | solution.py:434
  121.0 4.3 %collective-permute-done.22.c = bf16[256,256]{1,0:T(8,128)(2,1)S(1)} collective-permute-done((bf16[256,256]{1,0:T(8,128)(2,1)S(1)}, bf16[256,256]{1,0:T(8,128)(2,1)S(1)}, u32[]{:S(2)}, u32[]{:S(2)}) %collective-permute-start.22) | collective-permute-done | bytes 131104 | tf_op jit(solution)/shard_map/ppermute | solution.py:380
  125.3 2.9 %collective-permute-done.23.d = bf16[256,256]{1,0:T(8,128)(2,1)S(1)} collective-permute-done((bf16[256,256]{1,0:T(8,128)(2,1)S(1)}, bf16[256,256]{1,0:T(8,128)(2,1)S(1)}, u32[]{:S(2)}, u32[]{:S(2)}) %collective-permute-start.23) | collective-permute-done | bytes 131104 | tf_op jit(solution)/shard_map/ppermute | solution.py:380
  128.3 1.0 put.1
  129.3 4.8 %all-to-all-start.2 = ((bf16[16,40,256]{2,1,0:T(8,128)(2,1)}), bf16[16,40,256]{2,1,0:T(8,128)(2,1)S(1)}, u32[]{:S(2)}, u32[]{:S(2)}) async-start(bf16[16,40,256]{2,1,0:T(8,128)(2,1)} %bitcast.17), calls=%async_computation.2 | async-start | bytes 655360 | tf_op jit(solution)/shard_map/all_to_all | solution.py:441
  134.1 1.4 collective-permute-start.25
  135.5 2.4 %collective-permute-start.26 = (bf16[2,256,256]{2,1,0:T(8,128)(2,1)S(1)}, bf16[2,256,256]{2,1,0:T(8,128)(2,1)S(1)}, u32[]{:S(2)}, u32[]{:S(2)}) collective-permute-start(bf16[2,256,256]{2,1,0:T(8,128)(2,1)S(1)} %total.3.refs_0_), channel_id=1, source_target_pairs={{0,128},{64,192},{128,0},{192,64},{1,129},{65,193},{129,1},{193,65... | collective-permute-start | bytes 786440 | tf_op jit(solution)/shard_map/ppermute | solution.py:380
  137.9 1.2 collective-permute-start.27
  139.1 1.2 collective-permute-start.28
  140.3 5.0 %collective-permute-done.25.refs_1_ = bf16[2,256,256]{2,1,0:T(8,128)(2,1)S(1)} collective-permute-done((bf16[2,256,256]{2,1,0:T(8,128)(2,1)S(1)}, bf16[2,256,256]{2,1,0:T(8,128)(2,1)S(1)}, u32[]{:S(2)}, u32[]{:S(2)}) %collective-permute-start.25) | collective-permute-done | bytes 262176 | tf_op jit(solution)/shard_map/ppermute | solution.py:380
  145.3 1.0 collective-permute-start.29
  146.3 6.4 %collective-permute-done.26.refs_2_ = bf16[2,256,256]{2,1,0:T(8,128)(2,1)S(1)} collective-permute-done((bf16[2,256,256]{2,1,0:T(8,128)(2,1)S(1)}, bf16[2,256,256]{2,1,0:T(8,128)(2,1)S(1)}, u32[]{:S(2)}, u32[]{:S(2)}) %collective-permute-start.26) | collective-permute-done | bytes 262176 | tf_op jit(solution)/shard_map/ppermute | solution.py:380
  152.7 0.9 collective-permute-start.30
  153.6 1.1 collective-permute-done.30.refs_6_
  155.1 2.0 %assemble.1 = bf16[16,256,256]{2,1,0:T(8,128)(2,1)} custom-call(s32[4]{0:T(128)S(1)} %pad_add_fusion.place, bf16[2,256,256]{2,1,0:T(8,128)(2,1)S(1)} %total.3.refs_0_, bf16[2,256,256]{2,1,0:T(8,128)(2,1)S(1)} %collective-permute-done.25.refs_1_, bf16[2,256,256]{2,1,0:T(8,128)(2,1)S(1)} %collective-permute-done.26.refs_2_, ...), custom_call_target="tpu_custom_call" | custom-call | tf_op jit(solution)/shard_map/assemble/pallas_call | solution.py:368
  157.2 0.7 copy.13
  (59 shorter events, 6.5 us)
Async XLA Ops:
  0.6 20.0 %copy-start = (s32[16,16]{1,0:T(8,128)S(1)}, s32[16,16]{1,0:T(8,128)}, u32[]{:S(2)}) copy-start(s32[16,16]{1,0:T(8,128)} %param.12) | copy-start | bytes 3076
  0.6 25.8 %all-to-all-start = ((bf16[16,40,256]{2,1,0:T(8,128)(2,1)}), bf16[16,40,256]{2,1,0:T(8,128)(2,1)S(1)}, u32[]{:S(2)}, u32[]{:S(2)}) async-start(bf16[16,40,256]{2,1,0:T(8,128)(2,1)} %bitcast.33), calls=%async_computation | async-start | bytes 655360 | tf_op jit(solution)/shard_map/all_to_all | solution.py:406
  11.4 1.0 copy-start.2
  12.5 0.7 copy-start.5
  13.2 7.3 %copy-start.6 = (s32[16,16]{1,0:T(8,128)S(1)}, s32[16,16]{1,0:T(8,128)}, u32[]{:S(2)}) copy-start(s32[16,16]{1,0:T(8,128)} %param.11) | copy-start | bytes 3076
  18.9 10.0 %collective-permute-start.6 = (bf16[2,272,256]{2,1,0:T(8,128)(2,1)}, bf16[2,272,256]{2,1,0:T(8,128)(2,1)S(1)}, u32[]{:S(2)}, u32[]{:S(2)}) collective-permute-start(bf16[2,272,256]{2,1,0:T(8,128)(2,1)} %get-tuple-element.48), channel_id=1, source_target_pairs={{0,8},{8,16},{16,24},{24,0},{1,9},{9,17},{17,25},{25,1},{2,10},{10... | collective-permute-start | bytes 835592 | tf_op jit(solution)/shard_map/ppermute | solution.py:380
  19.0 9.9 %collective-permute-start.7 = (bf16[2,272,256]{2,1,0:T(8,128)(2,1)}, bf16[2,272,256]{2,1,0:T(8,128)(2,1)S(1)}, u32[]{:S(2)}, u32[]{:S(2)}) collective-permute-start(bf16[2,272,256]{2,1,0:T(8,128)(2,1)} %get-tuple-element.49), channel_id=1, source_target_pairs={{0,24},{8,0},{16,8},{24,16},{1,25},{9,1},{17,9},{25,17},{2,26},{10... | collective-permute-start | bytes 835592 | tf_op jit(solution)/shard_map/ppermute | solution.py:380
  26.8 4.7 %collective-permute-start = (bf16[256,256]{1,0:T(8,128)(2,1)S(1)}, bf16[256,256]{1,0:T(8,128)(2,1)S(1)}, u32[]{:S(2)}, u32[]{:S(2)}) collective-permute-start(bf16[256,256]{1,0:T(8,128)(2,1)S(1)} %pick.2), channel_id=1, source_target_pairs={{0,2},{2,4},{4,6},{6,0},{1,3},{3,5},{5,7},{7,1},{8,10},{10,12},{12... | collective-permute-start | bytes 393224 | tf_op jit(solution)/shard_map/ppermute | solution.py:380
  27.6 9.9 %collective-permute-start.1 = (bf16[256,256]{1,0:T(8,128)(2,1)S(1)}, bf16[256,256]{1,0:T(8,128)(2,1)S(1)}, u32[]{:S(2)}, u32[]{:S(2)}) collective-permute-start(bf16[256,256]{1,0:T(8,128)(2,1)S(1)} %pick.2), channel_id=1, source_target_pairs={{0,4},{2,6},{4,0},{6,2},{1,5},{3,7},{5,1},{7,3},{8,12},{10,14},{12... | collective-permute-start | bytes 393224 | tf_op jit(solution)/shard_map/ppermute | solution.py:380
  27.6 11.1 %collective-permute-start.2 = (bf16[256,256]{1,0:T(8,128)(2,1)S(1)}, bf16[256,256]{1,0:T(8,128)(2,1)S(1)}, u32[]{:S(2)}, u32[]{:S(2)}) collective-permute-start(bf16[256,256]{1,0:T(8,128)(2,1)S(1)} %pick.2), channel_id=1, source_target_pairs={{0,6},{2,0},{4,2},{6,4},{1,7},{3,1},{5,3},{7,5},{8,14},{10,8},{12,... | collective-permute-start | bytes 393224 | tf_op jit(solution)/shard_map/ppermute | solution.py:380
  30.0 44.5 %copy-start.1 = (bf16[4096,256]{1,0:T(8,128)(2,1)S(1)}, bf16[4096,256]{1,0:T(8,128)(2,1)}, u32[]{:S(2)}) copy-start(bf16[4096,256]{1,0:T(8,128)(2,1)} %param.15) | copy-start | bytes 6291460
  30.0 18.7 %collective-permute-start.8 = (bf16[4,272,256]{2,1,0:T(8,128)(2,1)}, bf16[4,272,256]{2,1,0:T(8,128)(2,1)}, u32[]{:S(2)}, u32[]{:S(2)}) collective-permute-start(bf16[4,272,256]{2,1,0:T(8,128)(2,1)} %get-tuple-element.52), channel_id=1, source_target_pairs={{0,8},{8,16},{16,24},{24,0},{1,9},{9,17},{17,25},{25,1},{2,10},{10... | collective-permute-start | bytes 1671176 | tf_op jit(solution)/shard_map/ppermute | solution.py:380
  30.0 18.7 %collective-permute-start.9 = (bf16[4,272,256]{2,1,0:T(8,128)(2,1)}, bf16[4,272,256]{2,1,0:T(8,128)(2,1)}, u32[]{:S(2)}, u32[]{:S(2)}) collective-permute-start(bf16[4,272,256]{2,1,0:T(8,128)(2,1)} %get-tuple-element.55), channel_id=1, source_target_pairs={{0,24},{8,0},{16,8},{24,16},{1,25},{9,1},{17,9},{25,17},{2,26},{10... | collective-permute-start | bytes 1671176 | tf_op jit(solution)/shard_map/ppermute | solution.py:380
  38.7 15.3 %collective-permute-start.3 = (bf16[4,256,256]{2,1,0:T(8,128)(2,1)S(1)}, bf16[4,256,256]{2,1,0:T(8,128)(2,1)}, u32[]{:S(2)}, u32[]{:S(2)}) collective-permute-start(bf16[4,256,256]{2,1,0:T(8,128)(2,1)S(1)} %join.1.a0), channel_id=1, source_target_pairs={{0,8},{8,16},{16,24},{24,0},{1,9},{9,17},{17,25},{25,1},{2,10},{10... | collective-permute-start | bytes 1572872 | tf_op jit(solution)/shard_map/ppermute | solution.py:380
  38.8 27.0 %all-to-all-start.1 = ((bf16[16,40,256]{2,1,0:T(8,128)(2,1)}), bf16[16,40,256]{2,1,0:T(8,128)(2,1)S(1)}, u32[]{:S(2)}, u32[]{:S(2)}) async-start(bf16[16,40,256]{2,1,0:T(8,128)(2,1)} %bitcast.34), calls=%async_computation.1 | async-start | bytes 655360 | tf_op jit(solution)/shard_map/all_to_all | solution.py:415
  47.8 18.3 %collective-permute-start.4 = (bf16[4,256,256]{2,1,0:T(8,128)(2,1)S(1)}, bf16[4,256,256]{2,1,0:T(8,128)(2,1)}, u32[]{:S(2)}, u32[]{:S(2)}) collective-permute-start(bf16[4,256,256]{2,1,0:T(8,128)(2,1)S(1)} %join.1.a0), channel_id=1, source_target_pairs={{0,16},{8,24},{16,0},{24,8},{1,17},{9,25},{17,1},{25,9},{2,18},{10... | collective-permute-start | bytes 1572872 | tf_op jit(solution)/shard_map/ppermute | solution.py:380
  48.7 25.8 %collective-permute-start.5 = (bf16[4,256,256]{2,1,0:T(8,128)(2,1)S(1)}, bf16[4,256,256]{2,1,0:T(8,128)(2,1)}, u32[]{:S(2)}, u32[]{:S(2)}) collective-permute-start(bf16[4,256,256]{2,1,0:T(8,128)(2,1)S(1)} %join.1.a0), channel_id=1, source_target_pairs={{0,24},{8,0},{16,8},{24,16},{1,25},{9,1},{17,9},{25,17},{2,26},{10... | collective-permute-start | bytes 1572872 | tf_op jit(solution)/shard_map/ppermute | solution.py:380
  50.8 0.7 copy-start.3
  51.5 23.0 %collective-permute-start.10 = (bf16[272,256]{1,0:T(8,128)(2,1)}, bf16[272,256]{1,0:T(8,128)(2,1)S(1)}, u32[]{:S(2)}, u32[]{:S(2)}) collective-permute-start(bf16[272,256]{1,0:T(8,128)(2,1)} %get-tuple-element.59), channel_id=1, source_target_pairs={{0,2},{2,4},{4,6},{6,0},{1,3},{3,5},{5,7},{7,1},{8,10},{10,12},{12... | collective-permute-start | bytes 417800 | tf_op jit(solution)/shard_map/ppermute | solution.py:380
  51.5 23.0 %collective-permute-start.11 = (bf16[272,256]{1,0:T(8,128)(2,1)}, bf16[272,256]{1,0:T(8,128)(2,1)S(1)}, u32[]{:S(2)}, u32[]{:S(2)}) collective-permute-start(bf16[272,256]{1,0:T(8,128)(2,1)} %get-tuple-element.60), channel_id=1, source_target_pairs={{0,4},{2,6},{4,0},{6,2},{1,5},{3,7},{5,1},{7,3},{8,12},{10,14},{12... | collective-permute-start | bytes 417800 | tf_op jit(solution)/shard_map/ppermute | solution.py:380
  54.0 20.5 %collective-permute-start.12 = (bf16[272,256]{1,0:T(8,128)(2,1)}, bf16[272,256]{1,0:T(8,128)(2,1)S(1)}, u32[]{:S(2)}, u32[]{:S(2)}) collective-permute-start(bf16[272,256]{1,0:T(8,128)(2,1)} %get-tuple-element.61), channel_id=1, source_target_pairs={{0,6},{2,0},{4,2},{6,4},{1,7},{3,1},{5,3},{7,5},{8,14},{10,8},{12,... | collective-permute-start | bytes 417800 | tf_op jit(solution)/shard_map/ppermute | solution.py:380
  74.5 1.0 copy-start.4
  80.0 2.8 %collective-permute-start.17 = (bf16[8,256,256]{2,1,0:T(8,128)(2,1)S(1)}, bf16[8,256,256]{2,1,0:T(8,128)(2,1)S(1)}, u32[]{:S(2)}, u32[]{:S(2)}) collective-permute-start(bf16[8,256,256]{2,1,0:T(8,128)(2,1)S(1)} %get-tuple-element.70), channel_id=1, source_target_pairs={{0,1},{1,0},{2,3},{3,2},{4,5},{5,4},{6,7},{7,6},{8,9},{9,8},{10,11... | collective-permute-start | bytes 3145736 | tf_op jit(solution)/shard_map/ppermute | solution.py:427
  80.5 13.5 %collective-permute-start.13 = (bf16[4,256,256]{2,1,0:T(8,128)(2,1)S(1)}, bf16[4,256,256]{2,1,0:T(8,128)(2,1)S(1)}, u32[]{:S(2)}, u32[]{:S(2)}) collective-permute-start(bf16[4,256,256]{2,1,0:T(8,128)(2,1)S(1)} %get-tuple-element.63), channel_id=1, source_target_pairs={{0,8},{8,16},{16,24},{24,0},{1,9},{9,17},{17,25},{25,1},{2,10},{10... | collective-permute-start | bytes 1572872 | tf_op jit(solution)/shard_map/ppermute | solution.py:380
  80.8 14.4 %collective-permute-start.14 = (bf16[4,256,256]{2,1,0:T(8,128)(2,1)S(1)}, bf16[4,256,256]{2,1,0:T(8,128)(2,1)S(1)}, u32[]{:S(2)}, u32[]{:S(2)}) collective-permute-start(bf16[4,256,256]{2,1,0:T(8,128)(2,1)S(1)} %get-tuple-element.64), channel_id=1, source_target_pairs={{0,24},{8,0},{16,8},{24,16},{1,25},{9,1},{17,9},{25,17},{2,26},{10... | collective-permute-start | bytes 1572872 | tf_op jit(solution)/shard_map/ppermute | solution.py:380
  83.5 13.3 %collective-permute-start.18 = (bf16[2,256,256]{2,1,0:T(8,128)(2,1)S(1)}, bf16[2,256,256]{2,1,0:T(8,128)(2,1)S(1)}, u32[]{:S(2)}, u32[]{:S(2)}) collective-permute-start(bf16[2,256,256]{2,1,0:T(8,128)(2,1)S(1)} %get-tuple-element.72), channel_id=1, source_target_pairs={{0,64},{64,128},{128,192},{192,0},{1,65},{65,129},{129,193},{193,1... | collective-permute-start | bytes 786440 | tf_op jit(solution)/shard_map/ppermute | solution.py:380
  85.0 14.1 %collective-permute-start.19 = (bf16[2,256,256]{2,1,0:T(8,128)(2,1)S(1)}, bf16[2,256,256]{2,1,0:T(8,128)(2,1)S(1)}, u32[]{:S(2)}, u32[]{:S(2)}) collective-permute-start(bf16[2,256,256]{2,1,0:T(8,128)(2,1)S(1)} %get-tuple-element.73), channel_id=1, source_target_pairs={{0,128},{64,192},{128,0},{192,64},{1,129},{65,193},{129,1},{193,65... | collective-permute-start | bytes 786440 | tf_op jit(solution)/shard_map/ppermute | solution.py:380
  87.4 11.7 %collective-permute-start.20 = (bf16[2,256,256]{2,1,0:T(8,128)(2,1)S(1)}, bf16[2,256,256]{2,1,0:T(8,128)(2,1)S(1)}, u32[]{:S(2)}, u32[]{:S(2)}) collective-permute-start(bf16[2,256,256]{2,1,0:T(8,128)(2,1)S(1)} %get-tuple-element.74), channel_id=1, source_target_pairs={{0,192},{64,0},{128,64},{192,128},{1,193},{65,1},{129,65},{193,129... | collective-permute-start | bytes 786440 | tf_op jit(solution)/shard_map/ppermute | solution.py:380
  95.3 9.1 %collective-permute-start.15 = (bf16[2,256,256]{2,1,0:T(8,128)(2,1)S(1)}, bf16[2,256,256]{2,1,0:T(8,128)(2,1)S(1)}, u32[]{:S(2)}, u32[]{:S(2)}) collective-permute-start(bf16[2,256,256]{2,1,0:T(8,128)(2,1)S(1)} %get-tuple-element.67), channel_id=1, source_target_pairs={{0,8},{8,16},{16,24},{24,0},{1,9},{9,17},{17,25},{25,1},{2,10},{10... | collective-permute-start | bytes 786440 | tf_op jit(solution)/shard_map/ppermute | solution.py:380
  95.7 8.7 %collective-permute-start.16 = (bf16[2,256,256]{2,1,0:T(8,128)(2,1)S(1)}, bf16[2,256,256]{2,1,0:T(8,128)(2,1)S(1)}, u32[]{:S(2)}, u32[]{:S(2)}) collective-permute-start(bf16[2,256,256]{2,1,0:T(8,128)(2,1)S(1)} %get-tuple-element.68), channel_id=1, source_target_pairs={{0,24},{8,0},{16,8},{24,16},{1,25},{9,1},{17,9},{25,17},{2,26},{10... | collective-permute-start | bytes 786440 | tf_op jit(solution)/shard_map/ppermute | solution.py:380
  99.2 21.8 %collective-permute-start.24 = (bf16[2,256,256]{2,1,0:T(8,128)(2,1)S(1)}, bf16[2,256,256]{2,1,0:T(8,128)(2,1)S(1)}, u32[]{:S(2)}, u32[]{:S(2)}) collective-permute-start(bf16[2,256,256]{2,1,0:T(8,128)(2,1)S(1)} %total.2.refs_0_), channel_id=1, source_target_pairs={{0,32},{32,0},{1,33},{33,1},{2,34},{34,2},{3,35},{35,3},{4,36},{36... | collective-permute-start | bytes 786440 | tf_op jit(solution)/shard_map/ppermute | solution.py:434
  104.5 16.5 %collective-permute-start.21 = (bf16[256,256]{1,0:T(8,128)(2,1)S(1)}, bf16[256,256]{1,0:T(8,128)(2,1)S(1)}, u32[]{:S(2)}, u32[]{:S(2)}) collective-permute-start(bf16[256,256]{1,0:T(8,128)(2,1)S(1)} %get-tuple-element.78), channel_id=1, source_target_pairs={{0,2},{2,4},{4,6},{6,0},{1,3},{3,5},{5,7},{7,1},{8,10},{10,12},{12... | collective-permute-start | bytes 393224 | tf_op jit(solution)/shard_map/ppermute | solution.py:380
  104.6 20.7 %collective-permute-start.22 = (bf16[256,256]{1,0:T(8,128)(2,1)S(1)}, bf16[256,256]{1,0:T(8,128)(2,1)S(1)}, u32[]{:S(2)}, u32[]{:S(2)}) collective-permute-start(bf16[256,256]{1,0:T(8,128)(2,1)S(1)} %get-tuple-element.79), channel_id=1, source_target_pairs={{0,4},{2,6},{4,0},{6,2},{1,5},{3,7},{5,1},{7,3},{8,12},{10,14},{12... | collective-permute-start | bytes 393224 | tf_op jit(solution)/shard_map/ppermute | solution.py:380
  105.8 22.4 %collective-permute-start.23 = (bf16[256,256]{1,0:T(8,128)(2,1)S(1)}, bf16[256,256]{1,0:T(8,128)(2,1)S(1)}, u32[]{:S(2)}, u32[]{:S(2)}) collective-permute-start(bf16[256,256]{1,0:T(8,128)(2,1)S(1)} %get-tuple-element.80), channel_id=1, source_target_pairs={{0,6},{2,0},{4,2},{6,4},{1,7},{3,1},{5,3},{7,5},{8,14},{10,8},{12,... | collective-permute-start | bytes 393224 | tf_op jit(solution)/shard_map/ppermute | solution.py:380
  129.3 27.9 %all-to-all-start.2 = ((bf16[16,40,256]{2,1,0:T(8,128)(2,1)}), bf16[16,40,256]{2,1,0:T(8,128)(2,1)S(1)}, u32[]{:S(2)}, u32[]{:S(2)}) async-start(bf16[16,40,256]{2,1,0:T(8,128)(2,1)} %bitcast.17), calls=%async_computation.2 | async-start | bytes 655360 | tf_op jit(solution)/shard_map/all_to_all | solution.py:441
  134.1 11.2 %collective-permute-start.25 = (bf16[2,256,256]{2,1,0:T(8,128)(2,1)S(1)}, bf16[2,256,256]{2,1,0:T(8,128)(2,1)S(1)}, u32[]{:S(2)}, u32[]{:S(2)}) collective-permute-start(bf16[2,256,256]{2,1,0:T(8,128)(2,1)S(1)} %total.3.refs_0_), channel_id=1, source_target_pairs={{0,64},{64,128},{128,192},{192,0},{1,65},{65,129},{129,193},{193,1... | collective-permute-start | bytes 786440 | tf_op jit(solution)/shard_map/ppermute | solution.py:380
  135.5 17.2 %collective-permute-start.26 = (bf16[2,256,256]{2,1,0:T(8,128)(2,1)S(1)}, bf16[2,256,256]{2,1,0:T(8,128)(2,1)S(1)}, u32[]{:S(2)}, u32[]{:S(2)}) collective-permute-start(bf16[2,256,256]{2,1,0:T(8,128)(2,1)S(1)} %total.3.refs_0_), channel_id=1, source_target_pairs={{0,128},{64,192},{128,0},{192,64},{1,129},{65,193},{129,1},{193,65... | collective-permute-start | bytes 786440 | tf_op jit(solution)/shard_map/ppermute | solution.py:380
  137.9 15.7 %collective-permute-start.27 = (bf16[2,256,256]{2,1,0:T(8,128)(2,1)S(1)}, bf16[2,256,256]{2,1,0:T(8,128)(2,1)S(1)}, u32[]{:S(2)}, u32[]{:S(2)}) collective-permute-start(bf16[2,256,256]{2,1,0:T(8,128)(2,1)S(1)} %total.3.refs_0_), channel_id=1, source_target_pairs={{0,192},{64,0},{128,64},{192,128},{1,193},{65,1},{129,65},{193,129... | collective-permute-start | bytes 786440 | tf_op jit(solution)/shard_map/ppermute | solution.py:380
  139.1 14.5 %collective-permute-start.28 = (bf16[2,256,256]{2,1,0:T(8,128)(2,1)S(1)}, bf16[2,256,256]{2,1,0:T(8,128)(2,1)S(1)}, u32[]{:S(2)}, u32[]{:S(2)}) collective-permute-start(bf16[2,256,256]{2,1,0:T(8,128)(2,1)S(1)} %total.3.refs_0_), channel_id=1, source_target_pairs={{0,1},{1,0},{2,3},{3,2},{4,5},{5,4},{6,7},{7,6},{8,9},{9,8},{10,11... | collective-permute-start | bytes 786440 | tf_op jit(solution)/shard_map/ppermute | solution.py:443
  145.3 8.3 %collective-permute-start.29 = (bf16[2,256,256]{2,1,0:T(8,128)(2,1)S(1)}, bf16[2,256,256]{2,1,0:T(8,128)(2,1)S(1)}, u32[]{:S(2)}, u32[]{:S(2)}) collective-permute-start(bf16[2,256,256]{2,1,0:T(8,128)(2,1)S(1)} %collective-permute-done.25.refs_1_), channel_id=1, source_target_pairs={{0,1},{1,0},{2,3},{3,2},{4,5},{5,4},{6,7},{7,6},{8,9},{9,8},{10,11... | collective-permute-start | bytes 786440 | tf_op jit(solution)/shard_map/ppermute | solution.py:443
  152.7 2.0 %collective-permute-start.30 = (bf16[2,256,256]{2,1,0:T(8,128)(2,1)S(1)}, bf16[2,256,256]{2,1,0:T(8,128)(2,1)S(1)}, u32[]{:S(2)}, u32[]{:S(2)}) collective-permute-start(bf16[2,256,256]{2,1,0:T(8,128)(2,1)S(1)} %collective-permute-done.26.refs_2_), channel_id=1, source_target_pairs={{0,1},{1,0},{2,3},{3,2},{4,5},{5,4},{6,7},{7,6},{8,9},{9,8},{10,11... | collective-permute-start | bytes 786440 | tf_op jit(solution)/shard_map/ppermute | solution.py:443
  153.6 1.5 collective-permute-start.31
